TPU v7x, 128 devices: a whole 4x4x4 slice. The times are simulated.
128 devices in a mesh: dp: 16 (over x, y), seq: 8 (over z, core).
Axes of the slice: x: 4, y: 4, z: 4, core: 2. Of those that a mesh axis runs over, the one named last changes fastest.
Arguments:
- tokens: bfloat16 [16384, 2048], P(('dp', 'seq')), may hold values from -36 to 36
- segments: int32 [16384], P(('dp', 'seq')), may hold values from 0 to 2, as said below
- mixer_weights: bfloat16 [2048, 7680], P(('dp', 'seq')), may hold values from -0.125 to 0.125
- norm_gains: bfloat16 [2048, 2], P(('dp', 'seq')), may hold values from 0.5 to 1.5
- gate_weights: bfloat16 [5120, 160], P(('dp', 'seq')), may hold values from -0.5 to 0.5
- channel_terms: bfloat16 [2560, 8], P(('dp', 'seq')), may hold values from -1.5 to 10
- feed_weights: bfloat16 [2048, 18432], P(('dp', 'seq')), may hold values from -0.125 to 0.125
- cotangent: bfloat16 [16384, 2048], P(('dp', 'seq')), may hold values from -6 to 6
Outputs:
- activations: bfloat16 [16384, 2048], P(('dp', 'seq'))
- input_gradient: float32 [16384, 2048], P(('dp', 'seq'))
- mixer_gradient: float32 [2048, 7680], P(('dp', 'seq'))
- gain_gradient: float32 [2048, 2], P(('dp', 'seq'))
- gate_gradient: float32 [5120, 160], P(('dp', 'seq'))
- channel_gradient: float32 [2560, 8], P(('dp', 'seq'))
- feed_gradient: float32 [2048, 18432], P(('dp', 'seq'))
Inputs may be any that keep to these rules, and one draw needn't show every extreme that they name: `segments`: in each group of 1024 consecutive tokens the numbers are 0, then 1, then 2, never falling; number 0 covers the first 1 to 127 tokens and number 2 the last 1 to 127.
All inputs are finite; a program needn't handle non-finite values.
Results may differ from a plain program's by a relative error of at most 0.012.
Values may be sent and summed in bfloat16 or wider, within the bound.
A program may use at most 832 MiB of HBM per device.

v0:
```python
import jax
import jax.numpy as jnp
from jax import lax
from jax.sharding import PartitionSpec as P

W = 2560
FF = 6144
H = 16
CONV = 4
BW = 160


epsilon = 1e-06
rate_scale = 8.0
contract_last = (((1,), (1,)), ((), ()))
contract_first = (((0,), (0,)), ((), ()))


def from_behind(block, axis, distance):
    devices = range(lax.axis_size(axis))
    route = [(i - distance, i) for i in devices if i - distance in devices]
    return lax.ppermute(block, axis, route)


def entering(value, axis, join, neutral, backward):
    count, mine = (lax.axis_size(axis), lax.axis_index(axis))
    pieces = jax.tree.map(lambda part: lax.all_gather(part, axis), value)
    if backward:
        pieces = jax.tree.map(lambda part: part[::-1], pieces)
        mine = count - 1 - mine
    subtotal = jax.tree.map(
        lambda part, zero: jnp.full_like(part, 0) + jnp.asarray(zero, part.dtype), value, neutral
    )

    def step(position, subtotal):
        longer = join(subtotal, jax.tree.map(lambda part: part[position], pieces))
        return jax.tree.map(lambda new, old: jnp.where(position < mine, new, old), longer, subtotal)

    return lax.fori_loop(0, count - 1, step, subtotal)


def root_norm(value, gain):
    return value * lax.rsqrt(jnp.mean(value * value, axis=-1, keepdims=True) + epsilon) * gain


def combine(earlier, later):
    return (earlier[0] * later[0], later[0] * earlier[1] + later[1])


def recur_inputs(conv, gate_a, gate_x, channel, start):
    recall = jax.nn.sigmoid(gate_a + channel[:, CONV + 1])
    admit = jax.nn.sigmoid(gate_x + channel[:, CONV + 2])
    lograte = -rate_scale * jax.nn.softplus(-channel[:, CONV + 3]) * recall
    decay = jnp.exp(lograte) * (1.0 - start)
    scale = start + (1.0 - start) * jnp.sqrt(-jnp.expm1(2.0 * lograte))
    return (decay, scale * admit * conv)


def gelu_product(gate, upward):
    return jax.nn.gelu(gate) * upward


def shards(
    tokens,
    segments,
    mixer_weights,
    norm_gains,
    gate_weights,
    channel_terms,
    feed_weights,
    cotangent,
):
    rows = tokens.shape[0]
    rim = CONV - 1
    mixer, gains_low, gates, channel_low = (
        lax.all_gather(mixer_weights, ("dp", "seq"), axis=0, tiled=True),
        lax.all_gather(norm_gains, ("dp", "seq"), axis=0, tiled=True),
        lax.all_gather(gate_weights, ("dp", "seq"), axis=0, tiled=True),
        lax.all_gather(channel_terms, ("dp", "seq"), axis=0, tiled=True),
    )
    gains = gains_low.astype(jnp.float32)
    channel = channel_low.astype(jnp.float32)
    inputs = tokens.astype(jnp.float32)
    labels = (segments + 1).astype(jnp.float32)
    normed = root_norm(inputs, gains[:, 0]).astype(jnp.bfloat16)
    branches = jnp.dot(normed, mixer[:, : 2 * W], preferred_element_type=jnp.float32)
    branch_x = branches[:, :W]
    branch_y = branches[:, W:]
    before_x, before_l = from_behind((branch_x[rows - rim :], labels[rows - rim :]), "seq", 1)
    padded_x = jnp.concatenate([before_x, branch_x], 0)
    padded_l = jnp.concatenate([before_l, labels], 0)
    masks = [
        (padded_l[rim - offset : rim - offset + rows] == labels).astype(jnp.float32)[:, None]
        for offset in range(CONV)
    ]
    taps = [padded_x[rim - offset : rim - offset + rows] * masks[offset] for offset in range(CONV)]
    conv = jnp.zeros((rows, W), jnp.float32) + channel[:, CONV]
    for offset in range(CONV):
        conv = conv + channel[:, offset] * taps[offset]
    start = (padded_l[rim - 1 : rim - 1 + rows] != labels).astype(jnp.float32)[:, None]
    lowered = conv.astype(jnp.bfloat16).reshape(rows, H, BW)
    gate_pair = gates.reshape(2, H, BW, BW)
    raw = jnp.einsum(
        "thi,ghij->gthj", lowered, gate_pair, preferred_element_type=jnp.float32
    ).reshape(2, rows, W)
    decay, drive = recur_inputs(conv, raw[0], raw[1], channel, start)
    products, local_states = lax.associative_scan(combine, (decay, drive), axis=0)
    carry_product, carry_state = entering(
        (products[-1], local_states[-1]),
        "seq",
        combine,
        (jnp.ones((W,), jnp.float32), jnp.zeros((W,), jnp.float32)),
        False,
    )
    states = local_states + products * carry_state
    prior_states = jnp.concatenate([carry_state[None, :], states[:-1]], 0)
    gelu_y = jax.nn.gelu(branch_y)
    mixed = (gelu_y * states).astype(jnp.bfloat16)
    middle = inputs + lax.dot_general(
        mixed, mixer[:, 2 * W :], contract_last, preferred_element_type=jnp.float32
    )
    normed_two = root_norm(middle, gains[:, 1]).astype(jnp.bfloat16)
    feed = lax.all_gather(feed_weights, ("dp", "seq"), axis=0, tiled=True)
    gate_up = jnp.dot(normed_two, feed[:, : 2 * FF], preferred_element_type=jnp.float32)
    hidden = gelu_product(gate_up[:, :FF], gate_up[:, FF:]).astype(jnp.bfloat16)
    feed_out = lax.dot_general(
        hidden, feed[:, 2 * FF :], contract_last, preferred_element_type=jnp.float32
    )
    activations = (middle + feed_out).astype(jnp.bfloat16)
    adjoint_hidden = jnp.dot(cotangent, feed[:, 2 * FF :], preferred_element_type=jnp.float32)
    _, gelu_pull = jax.vjp(gelu_product, gate_up[:, :FF], gate_up[:, FF:])
    adjoint_gate, adjoint_up = gelu_pull(adjoint_hidden)
    adjoint_gate_up = jnp.concatenate([adjoint_gate, adjoint_up], 1).astype(jnp.bfloat16)
    adjoint_normed_two = lax.dot_general(
        adjoint_gate_up, feed[:, : 2 * FF], contract_last, preferred_element_type=jnp.float32
    )
    upper = lax.dot_general(
        normed_two, adjoint_gate_up, contract_first, preferred_element_type=jnp.float32
    )
    lower = lax.dot_general(cotangent, hidden, contract_first, preferred_element_type=jnp.float32)
    feed_gradient = lax.psum_scatter(
        jnp.concatenate([upper, lower], 1), ("dp", "seq"), scatter_dimension=0, tiled=True
    )
    outer = cotangent.astype(jnp.float32)
    _, norm_pull_two = jax.vjp(root_norm, middle, gains[:, 1])
    adjoint_middle_norm, adjoint_gain_two = norm_pull_two(adjoint_normed_two)
    adjoint_middle = outer + adjoint_middle_norm
    adjoint_out = adjoint_middle.astype(jnp.bfloat16)
    adjoint_mixed = jnp.dot(adjoint_out, mixer[:, 2 * W :], preferred_element_type=jnp.float32)
    output_weight_grad = lax.dot_general(
        adjoint_out, mixed, contract_first, preferred_element_type=jnp.float32
    )
    adjoint_states = adjoint_mixed * gelu_y
    _, branch_pull = jax.vjp(jax.nn.gelu, branch_y)
    adjoint_branch_y = branch_pull(adjoint_mixed * states)[0]
    next_decay = jnp.concatenate([decay[1:], jnp.ones((1, W), jnp.float32)], 0)
    suffix_rev, local_rev = lax.associative_scan(
        combine, (next_decay[::-1], adjoint_states[::-1]), axis=0
    )
    suffix_product = suffix_rev[::-1]
    local_adjoint = local_rev[::-1]
    leaving = (decay[0] * suffix_product[0], decay[0] * local_adjoint[0])
    carry_back, carry_in = entering(
        leaving, "seq", combine, (jnp.ones((W,), jnp.float32), jnp.zeros((W,), jnp.float32)), True
    )
    adjoints = local_adjoint + suffix_product * carry_in
    _, recur_pull = jax.vjp(recur_inputs, conv, raw[0], raw[1], channel, start)
    adjoint_conv_direct, adjoint_raw_a, adjoint_raw_x, adjoint_channel, _ = recur_pull(
        (adjoints * prior_states, adjoints)
    )
    adjoint_raw = (
        jnp.stack([adjoint_raw_a, adjoint_raw_x], 0).reshape(2, rows, H, BW).astype(jnp.bfloat16)
    )
    adjoint_conv = adjoint_conv_direct + jnp.einsum(
        "gthj,ghij->thi", adjoint_raw, gate_pair, preferred_element_type=jnp.float32
    ).reshape(rows, W)
    gate_gradient_local = jnp.einsum(
        "thi,gthj->ghij", lowered, adjoint_raw, preferred_element_type=jnp.float32
    ).reshape(2 * W, BW)
    tap_columns = [jnp.sum(adjoint_conv * taps[offset], axis=0) for offset in range(CONV)]
    tap_columns.append(jnp.sum(adjoint_conv, axis=0))
    channel_gradient_local = adjoint_channel + jnp.pad(jnp.stack(tap_columns, 1), ((0, 0), (0, 3)))
    adjoint_padded = jnp.zeros((rows + rim, W), jnp.float32)
    for offset in range(CONV):
        adjoint_padded = adjoint_padded + jnp.pad(
            channel[:, offset] * masks[offset] * adjoint_conv, ((rim - offset, offset), (0, 0))
        )
    rim_back = from_behind(adjoint_padded[:rim], "seq", -1)
    adjoint_branch_x = adjoint_padded[rim:] + jnp.concatenate(
        [jnp.zeros((rows - rim, W), jnp.float32), rim_back], 0
    )
    adjoint_both = jnp.concatenate([adjoint_branch_x, adjoint_branch_y], 1).astype(jnp.bfloat16)
    adjoint_normed = lax.dot_general(
        adjoint_both, mixer[:, : 2 * W], contract_last, preferred_element_type=jnp.float32
    )
    branch_weight_grad = lax.dot_general(
        normed, adjoint_both, contract_first, preferred_element_type=jnp.float32
    )
    _, norm_pull_one = jax.vjp(root_norm, inputs, gains[:, 0])
    adjoint_inputs, adjoint_gain_one = norm_pull_one(adjoint_normed)
    input_gradient = adjoint_middle + adjoint_inputs
    mixer_gradient, gain_gradient, gate_gradient, channel_gradient = (
        lax.psum_scatter(
            jnp.concatenate([branch_weight_grad, output_weight_grad], 1),
            ("dp", "seq"),
            scatter_dimension=0,
            tiled=True,
        ),
        lax.psum_scatter(
            jnp.stack([adjoint_gain_one, adjoint_gain_two], 1),
            ("dp", "seq"),
            scatter_dimension=0,
            tiled=True,
        ),
        lax.psum_scatter(gate_gradient_local, ("dp", "seq"), scatter_dimension=0, tiled=True),
        lax.psum_scatter(channel_gradient_local, ("dp", "seq"), scatter_dimension=0, tiled=True),
    )
    return (
        activations,
        input_gradient,
        mixer_gradient,
        gain_gradient,
        gate_gradient,
        channel_gradient,
        feed_gradient,
    )


def solution(mesh):
    placed = (
        P(("dp", "seq"), None),
        P(("dp", "seq")),
        P(("dp", "seq"), None),
        P(("dp", "seq"), None),
        P(("dp", "seq"), None),
        P(("dp", "seq"), None),
        P(("dp", "seq"), None),
        P(("dp", "seq"), None),
    )
    return jax.shard_map(
        shards,
        mesh=mesh,
        in_specs=placed,
        out_specs=(
            P(("dp", "seq"), None),
            P(("dp", "seq"), None),
            P(("dp", "seq"), None),
            P(("dp", "seq"), None),
            P(("dp", "seq"), None),
            P(("dp", "seq"), None),
            P(("dp", "seq"), None),
        ),
        check_vma=False,
    )
```

profile of v0, /device:TPU:1, one launch (start us, length us, event | category | flops | bytes accessed | tf_op | source)
XLA Modules:
  0.0 3000.4 jit_solution(191998120683761593)
XLA Ops:
  15.2 31.4 %all-gather = bf16[128,16,2]{1,2,0:T(2,128)(2,1)S(1)} all-gather(bf16[1,16,2]{1,2,0:T(2,128)(2,1)} %bitcast.98), channel_id=1, replica_groups=mesh['dp'=16,'seq'=8] {'dp','seq'}, dimensions={0}, use_global_device_ids=true | all-gather | bytes 8256 | tf_op jit(solution)/shard_map/all_gather | solution.py:77
  46.9 33.6 %all-gather.1 = bf16[128,20,8]{1,2,0:T(8,128)(2,1)S(1)} all-gather(bf16[1,20,8]{1,2,0:T(8,128)(2,1)} %bitcast.97), channel_id=1, replica_groups=mesh['dp'=16,'seq'=8] {'dp','seq'}, dimensions={0}, use_global_device_ids=true | all-gather | bytes 41280 | tf_op jit(solution)/shard_map/all_gather | solution.py:79
  82.0 36.2 %all-gather.10.cloned.1.call-done = bf16[2048,7680]{1,0:T(8,128)(2,1)} async-done(((bf16[16,7680]{1,0:T(8,128)(2,1)}), bf16[2048,7680]{1,0:T(8,128)(2,1)}) %all-gather.10.cloned.1.call-update) | async-done | bytes 31457296 | tf_op jit(solution)/shard_map/all_gather | solution.py:76
  118.1 8.6 fusion.10
  132.6 53.5 %all-gather.12.cloned.1.call-done = bf16[5120,160]{1,0:T(8,128)(2,1)} async-done(((bf16[40,160]{1,0:T(8,128)(2,1)}), bf16[5120,160]{1,0:T(8,128)(2,1)}) %all-gather.12.cloned.1.call-update) | async-done | bytes 1638416 | tf_op jit(solution)/shard_map/all_gather | solution.py:78
  312.9 13.3 all-gather.2
  333.8 12.9 all-gather.3
  348.2 9.9 slice.657
  358.1 9.9 slice.648
  379.0 8.7 multiply_reduce_fusion.7
  387.7 21.2 fusion.2
  409.0 14.9 fusion.22
  423.9 24.9 multiply_reduce_fusion.5
  451.2 7.5 fusion.70
  469.2 9.8 slice.652
  520.2 6.3 slice.702
  585.8 10.7 rev.14
  596.5 10.7 rev.15
  607.2 12.9 all-gather.5
  620.5 12.7 all-gather.4
  669.8 13.0 fusion.61
  689.2 8.7 fusion.75
  697.9 16.4 fusion.66
  714.3 41.8 %pad_maximum_fusion.1 = f32[2048,7680]{1,0:T(8,128)} fusion(f32[2048,2560]{1,0:T(8,128)} %fusion.75, f32[2048,5120]{1,0:T(8,128)} %fusion.66), kind=kLoop, calls=%fused_computation.7 | loop fusion | flops 15728640 | bytes 125829120 | tf_op jit(solution)/shard_map/concatenate | solution.py:204
  757.6 19.5 convolution_bitcast_fusion
  777.2 36.5 %fusion.36 = f32[2048,12288]{1,0:T(8,128)} fusion(bf16[128,6144]{1,0:T(8,128)(2,1)} %get-tuple-element.309, bf16[128,6144]{1,0:T(8,128)(2,1)} %get-tuple-element.308, f32[128,2048]{1,0:T(8,128)S(1)} %copy-done.18, f32[2048]{0:T(1024)S(1)} %bitcast.86, f32[128]{0:T(128)S(1)} %copy-done.67), kind=kOutput, calls=%fused_computation.50 | convolution fusion | flops 6449528832 | bytes 104866304 | tf_op jit(solution)/shard_map/dot_general | solution.py:137
  813.7 98.3 %pad_maximum_fusion = f32[2048,18432]{1,0:T(8,128)} fusion(f32[2048,6144]{1,0:T(8,128)} %convolution_bitcast_fusion, f32[2048,12288]{1,0:T(8,128)} %fusion.36), kind=kLoop, calls=%fused_computation.6 | loop fusion | flops 37748736 | bytes 301989888 | tf_op jit(solution)/shard_map/concatenate | solution.py:142
  912.1 14.3 fusion.29
  930.4 502.1 %reduce-scatter.14.cloned.1.call-done = f32[16,2]{1,0:T(8,128)} async-done(((f32[2048,2]{1,0:T(8,128)}), f32[16,2]{1,0:T(8,128)}) %reduce-scatter.14.cloned.1.call-update) | async-done | bytes 144
  1433.9 640.6 %reduce-scatter.16.cloned.1.call-done = f32[40,160]{1,0:T(8,128)} async-done(((f32[5120,160]{1,0:T(8,128)}), f32[40,160]{1,0:T(8,128)}) %reduce-scatter.16.cloned.1.call-update) | async-done | bytes 25616
  2074.5 341.7 %reduce-scatter.10.cloned.1.call-done = f32[16,7680]{1,0:T(8,128)} async-done(((f32[2048,7680]{1,0:T(8,128)}), f32[16,7680]{1,0:T(8,128)}) %reduce-scatter.10.cloned.1.call-update) | async-done | bytes 491536 | tf_op jit(solution)/shard_map/reduce_scatter | solution.py:203
  2416.1 577.2 %reduce-scatter.12.cloned.1.call-done = f32[16,18432]{1,0:T(8,128)} async-done(((f32[2048,18432]{1,0:T(8,128)}), f32[16,18432]{1,0:T(8,128)}) %reduce-scatter.12.cloned.1.call-update) | async-done | bytes 1179664 | tf_op jit(solution)/shard_map/reduce_scatter | solution.py:141
  (539 shorter events, 325.5 us)
Async XLA Ops:
  7.2 111.0 %all-gather.10.cloned.1.call-start = ((), (), s32[]{:S(2)}) async-start(), calls=%async_computation.4 | async-start | bytes 31703040 | tf_op jit(solution)/shard_map/all_gather | solution.py:76
  7.9 178.2 %all-gather.12.cloned.1.call-start = ((), (), s32[]{:S(2)}) async-start(), calls=%async_computation.5 | async-start | bytes 2641920 | tf_op jit(solution)/shard_map/all_gather | solution.py:78
  8.6 379.1 %all-gather.14.cloned.1.call-start = ((), (), s32[]{:S(2)}) async-start(), calls=%async_computation.6 | async-start | bytes 76087296 | tf_op jit(solution)/shard_map/all_gather | solution.py:123
  9.4 72.1 %copy-start.14 = (bf16[128,2048]{1,0:T(8,128)(2,1)S(1)}, bf16[128,2048]{1,0:T(8,128)(2,1)}, u32[]{:S(2)}) copy-start(bf16[128,2048]{1,0:T(8,128)(2,1)} %param.12) | copy-start | bytes 1572868
  9.4 919.6 %all-reduce.70.cloned.1.call-start = ((), (), s32[]{:S(2)}) async-start(), calls=%async_computation.11 | async-start | bytes 163840
  10.2 71.6 %collective-permute-start = (f32[3]{0:T(128)S(1)}, f32[3]{0:T(128)S(1)}, u32[]{:S(2)}, u32[]{:S(2)}) collective-permute-start(f32[3]{0:T(128)S(1)} %slice.554), channel_id=1, source_target_pairs={{0,1},{1,2},{2,3},{3,4},{4,5},{5,6},{6,7},{8,9},{9,10},{10,11},{11... | collective-permute-start | bytes 44 | tf_op jit(solution)/shard_map/ppermute | solution.py:22
  46.8 35.1 %copy-start.96 = (s32[128]{0:T(128)S(1)}, s32[128]{0:T(128)}, u32[]{:S(2)}) copy-start(s32[128]{0:T(128)} %param.13) | copy-start | bytes 1540
  81.2 45.5 %copy-start.50 = (f32[2560,8]{0,1:T(8,128)}, f32[2560,8]{0,1:T(8,128)S(1)}, u32[]{:S(2)}) copy-start(f32[2560,8]{0,1:T(8,128)S(1)} %reshape.148) | copy-start | bytes 245764
  81.5 48.6 %copy-start.57 = (f32[2560]{0:T(1024)}, f32[2560]{0:T(1024)S(1)}, u32[]{:S(2)}) copy-start(f32[2560]{0:T(1024)S(1)} %get-tuple-element.267) | copy-start | bytes 30724
  81.5 48.6 %copy-start.59 = (f32[2560]{0:T(1024)}, f32[2560]{0:T(1024)S(1)}, u32[]{:S(2)}) copy-start(f32[2560]{0:T(1024)S(1)} %get-tuple-element.268) | copy-start | bytes 30724
  81.5 48.6 %copy-start.61 = (f32[2560]{0:T(1024)}, f32[2560]{0:T(1024)S(1)}, u32[]{:S(2)}) copy-start(f32[2560]{0:T(1024)S(1)} %get-tuple-element.269) | copy-start | bytes 30724
  81.5 48.6 %copy-start.63 = (f32[2560]{0:T(1024)}, f32[2560]{0:T(1024)S(1)}, u32[]{:S(2)}) copy-start(f32[2560]{0:T(1024)S(1)} %get-tuple-element.270) | copy-start | bytes 30724
  81.7 36.4 %copy-start.97 = (f32[128]{0:T(128)}, f32[128]{0:T(128)S(1)}, u32[]{:S(2)}) copy-start(f32[128]{0:T(128)S(1)} %fusion.64) | copy-start | bytes 1540
  81.7 36.4 %copy-start.82 = (f32[128]{0:T(128)}, f32[128]{0:T(128)S(1)}, u32[]{:S(2)}) copy-start(f32[128]{0:T(128)S(1)} %fusion.99) | copy-start | bytes 1540
  81.8 45.0 %copy-start.53 = (f32[2048,1]{0,1:T(1,128)}, f32[2048,1]{0,1:T(1,128)S(1)}, u32[]{:S(2)}) copy-start(f32[2048,1]{0,1:T(1,128)S(1)} %get-tuple-element.384) | copy-start | bytes 24580
  81.8 367.0 %copy-start.46 = (f32[2048,1]{0,1:T(1,128)}, f32[2048,1]{0,1:T(1,128)S(1)}, u32[]{:S(2)}) copy-start(f32[2048,1]{0,1:T(1,128)S(1)} %get-tuple-element.383) | copy-start | bytes 24580
  82.0 48.2 %copy-start.87 = (f32[128]{0:T(128)}, f32[128]{0:T(128)S(1)}, u32[]{:S(2)}) copy-start(f32[128]{0:T(128)S(1)} %get-tuple-element.385) | copy-start | bytes 1540
  82.0 48.2 %copy-start.89 = (f32[128]{0:T(128)}, f32[128]{0:T(128)S(1)}, u32[]{:S(2)}) copy-start(f32[128]{0:T(128)S(1)} %get-tuple-element.386) | copy-start | bytes 1540
  82.0 48.2 %copy-start.91 = (f32[128]{0:T(128)}, f32[128]{0:T(128)S(1)}, u32[]{:S(2)}) copy-start(f32[128]{0:T(128)S(1)} %get-tuple-element.387) | copy-start | bytes 1540
  82.0 48.2 %copy-start.93 = (f32[128]{0:T(128)}, f32[128]{0:T(128)S(1)}, u32[]{:S(2)}) copy-start(f32[128]{0:T(128)S(1)} %get-tuple-element.388) | copy-start | bytes 1540
  126.8 3.3 collective-permute-start.1
  129.6 62.8 %copy-start.85 = (f32[128]{0:T(128)}, f32[128]{0:T(128)S(1)}, u32[]{:S(2)}) copy-start(f32[128]{0:T(128)S(1)} %get-tuple-element.303) | copy-start | bytes 1540
  132.6 56.4 %copy-start.10 = (bf16[128,2560]{0,1:T(8,128)(2,1)}, bf16[128,2560]{0,1:T(8,128)(2,1)S(1)}, u32[]{:S(2)}) copy-start(bf16[128,2560]{0,1:T(8,128)(2,1)S(1)} %copy.61) | copy-start | bytes 1966084
  348.2 19.8 copy-start.33
  387.7 61.1 %copy-start.66 = (f32[128]{0:T(128)}, f32[128]{0:T(128)S(1)}, u32[]{:S(2)}) copy-start(f32[128]{0:T(128)S(1)} %fusion.100) | copy-start | bytes 1540
  387.7 21.2 copy-start.39
  607.2 27.5 copy-start.86
  663.5 5.3 collective-permute-start.2
  666.3 766.2 %reduce-scatter.14.cloned.1.call-start = ((), (), s32[]{:S(2)}) async-start(), calls=%async_computation.9 | async-start | bytes 1056768
  684.2 1390.3 %reduce-scatter.16.cloned.1.call-start = ((), (), s32[]{:S(2)}) async-start(), calls=%async_computation.10 | async-start | bytes 5283840
  687.8 1728.3 %reduce-scatter.10.cloned.1.call-start = ((), (), s32[]{:S(2)}) async-start(), calls=%async_computation.7 | async-start | bytes 63406080 | tf_op jit(solution)/shard_map/reduce_scatter | solution.py:203
  756.1 2237.2 %reduce-scatter.12.cloned.1.call-start = ((), (), s32[]{:S(2)}) async-start(), calls=%async_computation.8 | async-start | bytes 152174592 | tf_op jit(solution)/shard_map/reduce_scatter | solution.py:141
  (79 other events, 439.1 us)
Sparse Core Ops, SparseCore 0:
  11.0 107.0 all-gather.9
  121.3 64.8 all-gather.11
  189.2 177.4 all-gather.13
  666.5 134.5 all-reduce.69
  803.3 629.1 reduce-scatter.13
  1435.3 639.1 reduce-scatter.15
  2081.5 334.6 reduce-scatter.9
  2423.5 569.8 reduce-scatter.11
where the time goes:
time: 3010 us; the launch traced here: 3000 us
  waiting for transfers between devices  2160 us (72%)
  local copies, waits for them, and re-layouts  257 us (9%)
  other arithmetic  242 us (8%)
  matrix products  202 us (7%)
  blocking collectives  117 us (4%)
    unnamed x11, waiting for transfers between devices  1140 us
    reduce_scatter x1, waiting for transfers between devices, shards(): lax.psum_scatter(jnp.concatenate([upper, lower], 1), ('dp', 'seq'), scatt...  577 us
    reduce_scatter x1, waiting for transfers between devices, shards(): lax.psum_scatter(jnp.concatenate([branch_weight_grad, output_weight_grad]...  342 us
    concatenate x1, other arithmetic, shards(): jnp.concatenate([upper, lower], 1)  98.3 us
    slice x49, local copies, waits for them, and re-layouts, shards(): lax.associative_scan(combine, (next_decay[::-1], adjoint_states[::-1]), a...  93.8 us
  transfers between devices with their start and end apart: 11, of which 8 were waited for; matrix products, arithmetic and copies ran while one was open for 15% of the time, Pallas kernels for 0%

commit v1 on v0

v1 whole, which is shorter than its diff:
```python
import functools

import jax
import jax.numpy as jnp
from jax import lax
from jax.experimental import pallas as pl
from jax.experimental.pallas import tpu as pltpu
from jax.sharding import PartitionSpec as P

D = 2048
W = 2560
FF = 6144
CONV = 4
BW = 160
SEQ = 8
DP = 16
T = 128
G = 1024
WL = W // SEQ
WP = 384
MW = 3 * WP
FL = FF // SEQ
FW = 3 * FL
HALF = T // 2

epsilon = 1e-06
rate_scale = 8.0
f32 = jnp.float32
bf16 = jnp.bfloat16
MESH = pl.DeviceIdType.MESH
ANY = pl.ANY
VMEM = pltpu.VMEM
DMA = pltpu.SemaphoreType.DMA


class Place:
    def __init__(self):
        self.dp = lax.axis_index("dp")
        self.sq = lax.axis_index("seq")
        self.x, self.y = self.dp // 4, self.dp % 4
        self.z, self.c = self.sq // 2, self.sq % 2

    def chip(self, k):
        return (self.z + k) % 4

    def slot(self, k, c):
        return 2 * self.chip(k) + c

    def z_peer(self, k):
        return (self.dp, 2 * self.chip(k) + self.c)

    def sibling(self):
        return (self.dp, 2 * self.z + 1 - self.c)

    def x_dp(self, k):
        return (self.x + k) % 4 * 4 + self.y

    def y_dp(self, k):
        return self.x * 4 + (self.y + k) % 4

    def dp_peer(self, dp):
        return (dp, self.sq)

    def seq_peer(self, k):
        return (self.dp, (self.sq + k) % SEQ)


def remote(src, dst, send, recv, device):
    return pltpu.make_async_remote_copy(
        src_ref=src, dst_ref=dst, send_sem=send, recv_sem=recv, device_id=device, device_id_type=MESH
    )


def greet(peers):
    barrier = pltpu.get_barrier_semaphore()
    for device in peers:
        pl.semaphore_signal(barrier, inc=1, device_id=device, device_id_type=MESH)
    return barrier, len(peers)


def z_peers(me):
    return [me.z_peer(1), me.z_peer(3), me.sibling()]


def dp_peers(me):
    return [me.dp_peer((me.dp + k) % DP) for k in range(1, DP)]


def seq_peers(me):
    return [me.seq_peer(k) for k in range(1, SEQ)]


class Gather:
    sems = 10

    def __init__(self, me, own, full, send, recv):
        self.me, self.own, self.full, self.send, self.recv = me, own, full, send, recv
        self.sent = []
        self.a, self.b = pl.ds(0, HALF), pl.ds(HALF, HALF)

    def push(self, n, src, dst, device):
        copy = remote(src, dst, self.send.at[n], self.recv.at[n], device)
        copy.start()
        self.sent.append(copy)

    def arrived(self, n, dst):
        remote(dst, dst, self.send.at[n], self.recv.at[n], self.me.sibling()).wait_recv()

    def start(self):
        me, full = self.me, self.full
        mine = me.sq
        right, left = me.z_peer(1), me.z_peer(3)
        self.push(0, self.own.at[self.a], full.at[mine, self.a], right)
        self.push(1, self.own.at[self.b], full.at[mine, self.b], left)
        self.push(2, self.own.at[self.b], full.at[mine, self.b], right)
        self.push(3, self.own.at[self.a], full.at[mine, self.a], left)
        self.push(4, self.own, full.at[mine], me.sibling())

    def forward(self):
        me, full = self.me, self.full
        right, left = me.z_peer(1), me.z_peer(3)
        from_left, from_right = me.slot(3, me.c), me.slot(1, me.c)
        self.arrived(0, full.at[from_left, self.a])
        self.push(5, full.at[from_left, self.a], full.at[from_left, self.a], right)
        self.arrived(1, full.at[from_right, self.b])
        self.push(6, full.at[from_right, self.b], full.at[from_right, self.b], left)

    def across(self):
        me, full = self.me, self.full
        from_left, from_right, far = me.slot(3, me.c), me.slot(1, me.c), me.slot(2, me.c)
        self.arrived(2, full.at[from_left, self.b])
        self.push(7, full.at[from_left], full.at[from_left], me.sibling())
        self.arrived(3, full.at[from_right, self.a])
        self.push(8, full.at[from_right], full.at[from_right], me.sibling())
        self.arrived(5, full.at[far, self.a])
        self.arrived(6, full.at[far, self.b])
        self.push(9, full.at[far], full.at[far], me.sibling())

    def finish(self):
        me, full = self.me, self.full
        other = 1 - me.c
        self.arrived(4, full.at[me.slot(0, other)])
        self.arrived(7, full.at[me.slot(3, other)])
        self.arrived(8, full.at[me.slot(1, other)])
        self.arrived(9, full.at[me.slot(2, other)])
        for copy in self.sent:
            copy.wait_send()


def add_rows(out, at, terms, rows, step=32):
    def body(i, carry):
        here = pl.ds(pl.multiple_of(i * step, step), step)
        total = terms[0](here)
        for term in terms[1:]:
            total = total + term(here)
        there = pl.ds(pl.multiple_of(at + i * step, step), step)
        out[there] = total.astype(out.dtype)
        return carry

    lax.fori_loop(0, rows // step, body, 0)


def reads(ref, start=0):
    def term(here):
        return ref[pl.ds(pl.multiple_of(here.start + start, 16), here.size)].astype(f32)

    return term


class Scatter:
    sems = 10

    @staticmethod
    def scratch(n):
        return [
            VMEM((4, T, n), bf16),
            VMEM((4, T, n), bf16),
            VMEM((2, HALF, n), bf16),
            VMEM((2, HALF, n), bf16),
            VMEM((4, HALF, n), bf16),
            DMA((10,)),
            DMA((10,)),
        ]

    def __init__(self, me, part, other, pair, through, passed, final, send, recv):
        self.me, self.part = me, part
        self.other, self.pair, self.through, self.passed, self.final = other, pair, through, passed, final
        self.send, self.recv = send, recv
        self.sent = []

    def push(self, n, src, dst, device):
        copy = remote(src, dst, self.send.at[n], self.recv.at[n], device)
        copy.start()
        self.sent.append(copy)

    def arrived(self, n, dst):
        remote(dst, dst, self.send.at[n], self.recv.at[n], self.me.sibling()).wait_recv()

    def start(self):
        me = self.me
        for k in (2, 1, 3, 0):
            self.push(k, self.part.at[me.slot(k, 1 - me.c)], self.other.at[k], me.sibling())

    def join(self):
        me = self.me
        a, b = pl.ds(0, HALF), pl.ds(HALF, HALF)
        right, left = me.z_peer(1), me.z_peer(3)
        for k in (2, 1, 3, 0):
            self.arrived(k, self.other.at[k])
            add_rows(
                self.pair.at[k], 0, [reads(self.part.at[me.slot(k, me.c)]), reads(self.other.at[k])], T
            )
            if k == 2:
                self.push(4, self.pair.at[2, a], self.through.at[0], right)
                self.push(5, self.pair.at[2, b], self.through.at[1], left)
            if k == 1:
                self.push(6, self.pair.at[1, b], self.final.at[0], right)
            if k == 3:
                self.push(7, self.pair.at[3, a], self.final.at[1], left)

    def relay(self):
        me = self.me
        right, left = me.z_peer(1), me.z_peer(3)
        self.arrived(4, self.through.at[0])
        add_rows(self.passed.at[0], 0, [reads(self.through.at[0]), reads(self.pair.at[1])], HALF)
        self.push(8, self.passed.at[0], self.final.at[2], right)
        self.arrived(5, self.through.at[1])
        add_rows(self.passed.at[1], 0, [reads(self.through.at[1]), reads(self.pair.at[3], HALF)], HALF)
        self.push(9, self.passed.at[1], self.final.at[3], left)

    def finish(self, out, extra=None):
        for n, k in ((6, 0), (7, 1), (8, 2), (9, 3)):
            self.arrived(n, self.final.at[k])
        more = [] if extra is None else [reads(extra)]
        add_rows(
            out, 0, [reads(self.pair.at[0]), reads(self.final.at[1]), reads(self.final.at[2])] + more, HALF
        )
        more = [] if extra is None else [reads(extra, HALF)]
        add_rows(
            out,
            HALF,
            [reads(self.pair.at[0], HALF), reads(self.final.at[0]), reads(self.final.at[3])] + more,
            HALF,
        )
        for copy in self.sent:
            copy.wait_send()


def prologue_kernel(
    tok, cot, mix, feed, small, gates, chan,
    tok_all, cot_all, mix_all, feed_own, small_all, gain_all, gate_all, chan_all,
    gain_own, gate_own, chan_own, small_in,
    ts, tr, cs, cr, ms, mr, fs, fr, ss, sr, p1s, p1r, p2s, p2r, gs, gr, es, er, hs, hr, ls,
):
    me = Place()
    quarter, at = me.dp // 8, me.dp % 8
    gate_to = (8 * quarter + me.sq, at)
    gate_self = me.sq == at
    chan_to = (8 * (me.dp % 2) + me.sq, me.dp // 2)
    chan_from = (2 * me.sq + me.dp // 8, me.dp % 8)
    chan_self = jnp.logical_and(chan_to[0] == me.dp, chan_to[1] == me.sq)
    barrier, count = greet(seq_peers(me) + dp_peers(me))

    @pl.when(jnp.logical_not(gate_self))
    def _():
        pl.semaphore_signal(barrier, inc=1, device_id=gate_to, device_id_type=MESH)

    @pl.when(jnp.logical_not(chan_self))
    def _():
        pl.semaphore_signal(barrier, inc=1, device_id=chan_from, device_id_type=MESH)

    local = [
        pltpu.make_async_copy(tok, tok_all.at[me.sq], ls.at[0]),
        pltpu.make_async_copy(cot, cot_all.at[me.sq], ls.at[1]),
        pltpu.make_async_copy(mix.at[me.sq], mix_all.at[me.dp, me.sq], ls.at[2]),
        pltpu.make_async_copy(feed.at[me.sq], feed_own.at[me.sq], ls.at[3]),
        pltpu.make_async_copy(small, small_in.at[me.sq], ls.at[4]),
    ]
    for copy in local:
        copy.start()

    pl.semaphore_wait(barrier, count + jnp.where(gate_self, 0, 1) + jnp.where(chan_self, 0, 1))

    sent = []
    order = (4, 3, 5, 2, 6, 1, 7)
    for k in order:
        device = me.seq_peer(k)
        to = (me.sq + k) % SEQ
        sent.append(remote(mix.at[to], mix_all.at[me.dp, me.sq], ms.at[k], mr.at[k], device))
        sent[-1].start()
        sent.append(remote(small, small_in.at[me.sq], ss.at[k], sr.at[k], device))
        sent[-1].start()
    gate_copy = remote(gates, gate_own, hs.at[0], hr.at[0], gate_to)
    chan_copy = remote(chan, chan_own, hs.at[1], hr.at[1], chan_to)
    gate_local = pltpu.make_async_copy(gates, gate_own, ls.at[5])
    chan_local = pltpu.make_async_copy(chan, chan_own, ls.at[6])

    @pl.when(jnp.logical_not(gate_self))
    def _():
        gate_copy.start()

    @pl.when(gate_self)
    def _():
        gate_local.start()

    @pl.when(jnp.logical_not(chan_self))
    def _():
        chan_copy.start()

    @pl.when(chan_self)
    def _():
        chan_local.start()

    first = Gather(me, tok, tok_all, ts, tr)
    first.start()
    for k in order:
        to = (me.sq + k) % SEQ
        sent.append(remote(feed.at[to], feed_own.at[me.sq], fs.at[k], fr.at[k], me.seq_peer(k)))
        sent[-1].start()

    for copy in local:
        copy.wait()
    for k in range(1, SEQ):
        source = (me.sq - k + SEQ) % SEQ
        remote(mix.at[0], mix_all.at[me.dp, source], ms.at[k], mr.at[k], me.sibling()).wait_recv()

    lo, hi = pl.ds(0, 4), pl.ds(4, 4)
    for k in (2, 1, 3):
        block = mix_all.at[me.dp, lo]
        sent.append(remote(block, block, p1s.at[k], p1r.at[k], me.dp_peer(me.x_dp(k))))
        sent[-1].start()
        block = mix_all.at[me.dp, hi]
        sent.append(remote(block, block, p1s.at[4 + k], p1r.at[4 + k], me.dp_peer(me.y_dp(k))))
        sent[-1].start()

    for k in range(1, SEQ):
        source = (me.sq - k + SEQ) % SEQ
        remote(small, small_in.at[source], ss.at[k], sr.at[k], me.sibling()).wait_recv()
    gain = small_in[0, 0:16].astype(f32)
    for k in range(1, SEQ):
        gain = gain + small_in[k, 0:16].astype(f32)
    gain_own[...] = gain.astype(bf16)
    for k in range(SEQ):
        small_all[k] = small_in[k]

    @pl.when(jnp.logical_not(gate_self))
    def _():
        gate_copy.wait()

    @pl.when(gate_self)
    def _():
        gate_local.wait()

    @pl.when(jnp.logical_not(chan_self))
    def _():
        chan_copy.wait()

    @pl.when(chan_self)
    def _():
        chan_local.wait()

    own = [
        pltpu.make_async_copy(gain_own, gain_all.at[me.dp], ls.at[0]),
        pltpu.make_async_copy(gate_own, gate_all.at[me.dp], ls.at[1]),
        pltpu.make_async_copy(chan_own, chan_all.at[me.dp], ls.at[2]),
    ]
    for copy in own:
        copy.start()
    for k in range(1, DP):
        device = me.dp_peer((me.dp + k) % DP)
        for n, (src, dst) in enumerate(((gain_own, gain_all), (gate_own, gate_all), (chan_own, chan_all))):
            sent.append(remote(src, dst.at[me.dp], es.at[n, k], er.at[n, k], device))
            sent[-1].start()

    first.forward()

    for j in (0, 2, 1, 3):
        if j:
            source = me.x_dp(4 - j)
            remote(mix_all.at[source, lo], mix_all.at[source, lo], p1s.at[j], p1r.at[j], me.sibling()).wait_recv()
            source = me.y_dp(4 - j)
            remote(
                mix_all.at[source, hi], mix_all.at[source, hi], p1s.at[4 + j], p1r.at[4 + j], me.sibling()
            ).wait_recv()
        for k in (2, 1, 3):
            block = mix_all.at[me.x_dp((4 - j) % 4), lo]
            sent.append(remote(block, block, p2s.at[j, k], p2r.at[j, k], me.dp_peer(me.y_dp(k))))
            sent[-1].start()
            block = mix_all.at[me.y_dp((4 - j) % 4), hi]
            sent.append(remote(block, block, p2s.at[4 + j, k], p2r.at[4 + j, k], me.dp_peer(me.x_dp(k))))
            sent[-1].start()

    second = Gather(me, cot, cot_all, cs, cr)
    second.start()
    first.across()
    second.forward()
    first.finish()
    second.across()
    second.finish()
    for k in range(1, SEQ):
        source = (me.sq - k + SEQ) % SEQ
        remote(feed.at[0], feed_own.at[source], fs.at[k], fr.at[k], me.sibling()).wait_recv()
    for copy in own:
        copy.wait()
    for k in range(1, DP):
        source = (me.dp - k + DP) % DP
        for n, (src, dst) in enumerate(((gain_own, gain_all), (gate_own, gate_all), (chan_own, chan_all))):
            remote(src, dst.at[source], es.at[n, k], er.at[n, k], me.sibling()).wait_recv()
    for j in range(4):
        for k in (1, 2, 3):
            row = (me.x - j + 4) % 4 * 4 + (me.y - k + 4) % 4
            block = mix_all.at[row, lo]
            remote(block, block, p2s.at[j, k], p2r.at[j, k], me.sibling()).wait_recv()
            row = (me.x - k + 4) % 4 * 4 + (me.y - j + 4) % 4
            block = mix_all.at[row, hi]
            remote(block, block, p2s.at[4 + j, k], p2r.at[4 + j, k], me.sibling()).wait_recv()
    for copy in sent:
        copy.wait_send()


def prologue(tokens, cot, mix, feed, small, gates, chan):
    sds = jax.ShapeDtypeStruct
    hbm, vmem = pl.BlockSpec(memory_space=ANY), pl.BlockSpec(memory_space=VMEM)
    return pl.pallas_call(
        prologue_kernel,
        out_shape=(
            sds((SEQ, T, D), bf16), sds((SEQ, T, D), bf16), sds((DP, SEQ, 16, MW), bf16),
            sds((SEQ, 16, FW), bf16), sds((SEQ, 32, 128), bf16), sds((DP, 16, 128), bf16),
            sds((DP, 16, 512), bf16), sds((DP, 16, 256), bf16),
        ),
        in_specs=[hbm, hbm, hbm, hbm, vmem, vmem, vmem],
        out_specs=[hbm, hbm, hbm, hbm, vmem, vmem, vmem, vmem],
        scratch_shapes=[
            VMEM((16, 128), bf16), VMEM((16, 512), bf16), VMEM((16, 256), bf16), VMEM((SEQ, 32, 128), bf16),
            DMA((10,)), DMA((10,)), DMA((10,)), DMA((10,)),
            DMA((SEQ,)), DMA((SEQ,)), DMA((SEQ,)), DMA((SEQ,)), DMA((SEQ,)), DMA((SEQ,)),
            DMA((8,)), DMA((8,)), DMA((8, 4)), DMA((8, 4)),
            DMA((1,)), DMA((1,)), DMA((3, DP)), DMA((3, DP)), DMA((2,)), DMA((2,)), DMA((8,)),
        ],
        compiler_params=pltpu.CompilerParams(collective_id=1, has_side_effects=True, vmem_limit_bytes=32 << 20),
        cost_estimate=pl.CostEstimate(flops=1000, bytes_accessed=100 << 20, transcendentals=0),
        name="prologue",
    )(tokens, cot, mix, feed, small, gates, chan)


def norm_rows(value, gain):
    return value * lax.rsqrt(jnp.mean(value * value, axis=-1, keepdims=True) + epsilon) * gain


def middle_kernel(part, tok, gain, middle, norm_all, own, *rest):
    scatter, (gs, gr, ls) = rest[:7], rest[7:]
    me = Place()
    barrier, count = greet(z_peers(me))
    pl.semaphore_wait(barrier, count)
    total = Scatter(me, part, *scatter)
    total.start()
    total.join()
    total.relay()
    total.finish(middle, tok)

    def body(i, carry):
        here = pl.ds(pl.multiple_of(i * 16, 16), 16)
        own[here] = norm_rows(middle[here], gain[...]).astype(bf16)
        return carry

    lax.fori_loop(0, T // 16, body, 0)
    keep = pltpu.make_async_copy(own, norm_all.at[me.sq], ls.at[0])
    keep.start()
    gather = Gather(me, own, norm_all, gs, gr)
    gather.start()
    gather.forward()
    gather.across()
    gather.finish()
    keep.wait()


def middle_call(part, tok, gain):
    sds = jax.ShapeDtypeStruct
    hbm, vmem = pl.BlockSpec(memory_space=ANY), pl.BlockSpec(memory_space=VMEM)
    return pl.pallas_call(
        middle_kernel,
        out_shape=(sds((T, D), f32), sds((SEQ, T, D), bf16)),
        in_specs=[vmem, vmem, vmem],
        out_specs=[vmem, hbm],
        scratch_shapes=[VMEM((T, D), bf16)] + Scatter.scratch(D) + [DMA((10,)), DMA((10,)), DMA((1,))],
        compiler_params=pltpu.CompilerParams(collective_id=2, has_side_effects=True, vmem_limit_bytes=40 << 20),
        cost_estimate=pl.CostEstimate(flops=1000, bytes_accessed=100 << 20, transcendentals=0),
        name="middle",
    )(part, tok, gain)


def norm_pull(value, gain, incoming):
    r = lax.rsqrt(jnp.mean(value * value, axis=-1, keepdims=True) + epsilon)
    scaled = incoming * gain
    inner = jnp.mean(value * scaled, axis=-1, keepdims=True)
    normed = value * r
    return r * (scaled - normed * (inner * r)), incoming * normed


def turn_kernel(part, middle, cot, gain, adj_middle, gain_grad, adj_all, adj, own, *rest):
    scatter, (gs, gr, ls) = rest[:7], rest[7:]
    me = Place()
    barrier, count = greet(z_peers(me))
    pl.semaphore_wait(barrier, count)
    total = Scatter(me, part, *scatter)
    total.start()
    total.join()
    total.relay()
    total.finish(adj)

    def body(i, carry):
        here = pl.ds(pl.multiple_of(i * 16, 16), 16)
        pulled, terms = norm_pull(middle[here], gain[...], adj[here])
        value = cot[here].astype(f32) + pulled
        adj_middle[here] = value
        own[here] = value.astype(bf16)
        return carry + jnp.sum(terms, axis=0, keepdims=True)

    gain_grad[...] = lax.fori_loop(0, T // 16, body, jnp.zeros((1, D), f32))
    keep = pltpu.make_async_copy(own, adj_all.at[me.sq], ls.at[0])
    keep.start()
    gather = Gather(me, own, adj_all, gs, gr)
    gather.start()
    gather.forward()
    gather.across()
    gather.finish()
    keep.wait()


def turn_call(part, middle, cot, gain):
    sds = jax.ShapeDtypeStruct
    hbm, vmem = pl.BlockSpec(memory_space=ANY), pl.BlockSpec(memory_space=VMEM)
    return pl.pallas_call(
        turn_kernel,
        out_shape=(sds((T, D), f32), sds((1, D), f32), sds((SEQ, T, D), bf16)),
        in_specs=[vmem] * 4,
        out_specs=[vmem, vmem, hbm],
        scratch_shapes=[VMEM((T, D), f32), VMEM((T, D), bf16)]
        + Scatter.scratch(D)
        + [DMA((10,)), DMA((10,)), DMA((1,))],
        compiler_params=pltpu.CompilerParams(collective_id=3, has_side_effects=True, vmem_limit_bytes=40 << 20),
        cost_estimate=pl.CostEstimate(flops=1000, bytes_accessed=100 << 20, transcendentals=0),
        name="turn",
    )(part, middle, cot, gain)


def close_kernel(
    part, feed_part, mg, eg, tok, adj_middle, middle, gain, gain_two,
    in_grad, act, mix_out, gate_out, chan_out, gain_out,
    adj, r1, s1, r2, last, e_in, gate_sum, chan_sum, gp, gp_in, gain_sum, gain_in, *rest,
):
    one, two = rest[:7], rest[7:14]
    m1s, m1r, m2s, m2r, m3s, m3r, es, er, gs, gr, hs, hr, qs, qr, ls = rest[14:]
    me = Place()
    quarter, at = me.dp // 8, me.dp % 8
    gate_to = (8 * quarter + me.sq, at)
    gate_self = me.sq == at
    chan_from = (8 * (me.dp % 2) + me.sq, me.dp // 2)
    chan_to = (2 * me.sq + me.dp // 8, me.dp % 8)
    chan_self = jnp.logical_and(chan_from[0] == me.dp, chan_from[1] == me.sq)
    barrier, count = greet(seq_peers(me) + dp_peers(me))

    @pl.when(jnp.logical_not(gate_self))
    def _():
        pl.semaphore_signal(barrier, inc=1, device_id=gate_to, device_id_type=MESH)

    @pl.when(jnp.logical_not(chan_self))
    def _():
        pl.semaphore_signal(barrier, inc=1, device_id=chan_from, device_id_type=MESH)

    pl.semaphore_wait(barrier, count + jnp.where(gate_self, 0, 1) + jnp.where(chan_self, 0, 1))

    sent = []

    def push(src, dst, send, recv, device):
        sent.append(remote(src, dst, send, recv, device))
        sent[-1].start()

    def arrived(dst, send, recv):
        remote(dst, dst, send, recv, me.sibling()).wait_recv()

    lo, hi = pl.ds(0, 4), pl.ds(4, 4)
    inner = Scatter(me, part, *one)
    outer = Scatter(me, feed_part, *two)
    inner.start()
    for k in (2, 1, 3):
        push(mg.at[:, (me.y + k) % 4, lo], r1.at[0, k - 1], m1s.at[k], m1r.at[k], me.dp_peer(me.y_dp(k)))
        push(mg.at[(me.x + k) % 4, :, hi], r1.at[1, k - 1], m1s.at[4 + k], m1r.at[4 + k], me.dp_peer(me.x_dp(k)))
    for k in range(1, DP):
        to = (me.dp + k) % DP
        push(eg.at[to], e_in.at[k], es.at[k], er.at[k], me.dp_peer(to))
    inner.join()
    outer.start()
    inner.relay()
    outer.join()
    inner.finish(adj)

    def pull(i, carry):
        here = pl.ds(pl.multiple_of(i * 16, 16), 16)
        pulled, terms = norm_pull(tok[here].astype(f32), gain[...], adj[here])
        in_grad[here] = adj_middle[here] + pulled
        return carry + jnp.sum(terms, axis=0, keepdims=True)

    gain_one = lax.fori_loop(0, T // 16, pull, jnp.zeros((1, D), f32))
    gp[...] = jnp.zeros(gp.shape, f32)
    for k in range(DP):
        gp[k, 0:1] = gain_one[:, k * 128 : (k + 1) * 128]
        gp[k, 1:2] = gain_two[:, k * 128 : (k + 1) * 128]
    for k in range(1, DP):
        to = (me.dp + k) % DP
        push(gp.at[to], gp_in.at[k], gs.at[k], gr.at[k], me.dp_peer(to))
    outer.relay()

    for k in range(1, DP):
        arrived(e_in.at[k], es.at[k], er.at[k])

    def small(n, carry):
        def step(k, total):
            return total + e_in[k, n].astype(f32)

        total = lax.fori_loop(1, DP, step, eg[me.dp, n].astype(f32))

        @pl.when(n < 4)
        def _():
            gate_sum[n] = total

        @pl.when(n == 4)
        def _():
            chan_sum[...] = total

        return carry

    lax.fori_loop(0, 5, small, 0)
    gate_copy = remote(gate_sum, gate_out, hs.at[0], hr.at[0], gate_to)
    chan_copy = remote(chan_sum, chan_out, hs.at[1], hr.at[1], chan_to)
    gate_local = pltpu.make_async_copy(gate_sum, gate_out, ls.at[0])
    chan_local = pltpu.make_async_copy(chan_sum, chan_out, ls.at[1])

    @pl.when(jnp.logical_not(gate_self))
    def _():
        gate_copy.start()

    @pl.when(gate_self)
    def _():
        gate_local.start()

    @pl.when(jnp.logical_not(chan_self))
    def _():
        chan_copy.start()

    @pl.when(chan_self)
    def _():
        chan_local.start()

    for k in (1, 3, 2):
        arrived(r1.at[0, k - 1], m1s.at[k], m1r.at[k])
        arrived(r1.at[1, k - 1], m1s.at[4 + k], m1r.at[4 + k])
    for j in (2, 1, 3, 0):

        def first(i, carry, j=j):
            xx, yy = (me.x + j) % 4, (me.y + j) % 4
            total = mg[xx, me.y, i].astype(f32)
            for k in range(3):
                total = total + r1[0, k, xx, i].astype(f32)
            s1[0, j, i] = total.astype(bf16)
            total = mg[me.x, yy, 4 + i].astype(f32)
            for k in range(3):
                total = total + r1[1, k, yy, i].astype(f32)
            s1[1, j, i] = total.astype(bf16)
            return carry

        lax.fori_loop(0, 4, first, 0)
        if j:
            push(s1.at[0, j], r2.at[0, j - 1], m2s.at[j], m2r.at[j], me.dp_peer(me.x_dp(j)))
            push(s1.at[1, j], r2.at[1, j - 1], m2s.at[4 + j], m2r.at[4 + j], me.dp_peer(me.y_dp(j)))

    for k in range(1, DP):
        arrived(gp_in.at[k], gs.at[k], gr.at[k])

    def gains(k, total):
        return total + gp_in[k]

    gain_sum[...] = lax.fori_loop(1, DP, gains, gp[me.dp])
    for k in range(1, SEQ):
        push(gain_sum, gain_in.at[k], qs.at[k], qr.at[k], me.seq_peer(k))

    outer.finish(adj, middle)

    def lower(i, carry):
        here = pl.ds(pl.multiple_of(i * 16, 16), 16)
        act[here] = adj[here].astype(bf16)
        return carry

    lax.fori_loop(0, T // 16, lower, 0)

    for j in (1, 3, 2):
        arrived(r2.at[0, j - 1], m2s.at[j], m2r.at[j])
        arrived(r2.at[1, j - 1], m2s.at[4 + j], m2r.at[4 + j])

    def second(i, carry):
        for h in range(2):
            total = s1[h, 0, i].astype(f32)
            for k in range(3):
                total = total + r2[h, k, i].astype(f32)
            last[4 * h + i] = total.astype(bf16)
        return carry

    lax.fori_loop(0, 4, second, 0)
    keep = pltpu.make_async_copy(last.at[me.sq], mix_out.at[me.sq], ls.at[2])
    keep.start()
    for k in (4, 3, 5, 2, 6, 1, 7):
        to = (me.sq + k) % SEQ
        push(last.at[to], mix_out.at[me.sq], m3s.at[k], m3r.at[k], me.seq_peer(k))
    for k in range(1, SEQ):
        arrived(gain_in.at[k], qs.at[k], qr.at[k])
    total = gain_sum[...]
    for k in range(1, SEQ):
        total = total + gain_in[k]
    gain_out[...] = total

    @pl.when(jnp.logical_not(gate_self))
    def _():
        gate_copy.wait()

    @pl.when(gate_self)
    def _():
        gate_local.wait()

    @pl.when(jnp.logical_not(chan_self))
    def _():
        chan_copy.wait()

    @pl.when(chan_self)
    def _():
        chan_local.wait()

    for k in range(1, SEQ):
        arrived(mix_out.at[(me.sq - k + SEQ) % SEQ], m3s.at[k], m3r.at[k])
    keep.wait()
    for copy in sent:
        copy.wait_send()


def close_call(part, feed_part, mg, eg, tok, adj_middle, middle, gain, gain_two):
    sds = jax.ShapeDtypeStruct
    vmem = pl.BlockSpec(memory_space=VMEM)
    return pl.pallas_call(
        close_kernel,
        out_shape=(
            sds((T, D), f32), sds((T, D), bf16), sds((SEQ, 16, MW), bf16),
            sds((4, 16, 128), f32), sds((16, 128), f32), sds((8, 128), f32),
        ),
        in_specs=[vmem] * 9,
        out_specs=[vmem] * 6,
        scratch_shapes=[
            VMEM((T, D), f32),
            VMEM((2, 3, 4, 4, 16, MW), bf16), VMEM((2, 4, 4, 16, MW), bf16), VMEM((2, 3, 4, 16, MW), bf16),
            VMEM((SEQ, 16, MW), bf16), VMEM((DP, 5, 16, 128), bf16), VMEM((4, 16, 128), f32),
            VMEM((16, 128), f32), VMEM((DP, 8, 128), f32), VMEM((DP, 8, 128), f32),
            VMEM((8, 128), f32), VMEM((SEQ, 8, 128), f32),
        ]
        + Scatter.scratch(D)
        + Scatter.scratch(D)
        + [
            DMA((8,)), DMA((8,)), DMA((8,)), DMA((8,)), DMA((8,)), DMA((8,)),
            DMA((DP,)), DMA((DP,)), DMA((DP,)), DMA((DP,)), DMA((2,)), DMA((2,)),
            DMA((SEQ,)), DMA((SEQ,)), DMA((3,)),
        ],
        compiler_params=pltpu.CompilerParams(collective_id=4, has_side_effects=True, vmem_limit_bytes=60 << 20),
        cost_estimate=pl.CostEstimate(flops=1000, bytes_accessed=100 << 20, transcendentals=0),
        name="close",
    )(part, feed_part, mg, eg, tok, adj_middle, middle, gain, gain_two)


def swap_kernel(src, dst, ss, sr, ls):
    me = Place()
    barrier, count = greet(seq_peers(me))
    keep = pltpu.make_async_copy(src.at[me.sq], dst.at[me.sq], ls.at[0])
    keep.start()
    pl.semaphore_wait(barrier, count)
    sent = []
    for k in (4, 3, 5, 2, 6, 1, 7):
        to = (me.sq + k) % SEQ
        sent.append(remote(src.at[to], dst.at[me.sq], ss.at[k], sr.at[k], me.seq_peer(k)))
        sent[-1].start()
    for k in range(1, SEQ):
        source = (me.sq - k + SEQ) % SEQ
        remote(dst.at[source], dst.at[source], ss.at[k], sr.at[k], me.sibling()).wait_recv()
    keep.wait()
    for copy in sent:
        copy.wait_send()


def swap_call(src):
    hbm = pl.BlockSpec(memory_space=ANY)
    return pl.pallas_call(
        swap_kernel,
        out_shape=jax.ShapeDtypeStruct(src.shape, src.dtype),
        in_specs=[hbm],
        out_specs=hbm,
        scratch_shapes=[DMA((SEQ,)), DMA((SEQ,)), DMA((1,))],
        compiler_params=pltpu.CompilerParams(collective_id=5, has_side_effects=True),
        cost_estimate=pl.CostEstimate(flops=1000, bytes_accessed=1 << 20, transcendentals=0),
        name="swap",
    )(src)


CHUNK = 256
STEPS = G // CHUNK
contract_last = (((1,), (1,)), ((), ()))
contract_first = (((0,), (0,)), ((), ()))
gelu_c = 0.7978845608028654
gelu_k = 0.044715


def gelu_parts(v):
    square = v * v
    t = jnp.tanh(gelu_c * (v + gelu_k * square * v))
    half = 0.5 * (1.0 + t)
    slope = half + 0.5 * v * (1.0 - t * t) * (gelu_c * (1.0 + 3.0 * gelu_k * square))
    return v * half, slope


def minus_expm1(z):
    series = -z * (1.0 + z * (1 / 2 + z * (1 / 6 + z * (1 / 24 + z * (1 / 120 + z * (1 / 720))))))
    return jnp.where(z > -0.25, series, 1.0 - jnp.exp(z))


def recur(conv, raw_a, raw_x, terms, start):
    recall = jax.nn.sigmoid(raw_a + terms[5:6])
    admit = jax.nn.sigmoid(raw_x + terms[6:7])
    lograte = terms[7:8] * recall
    decay = jnp.exp(lograte) * (1.0 - start)
    root = jnp.sqrt(minus_expm1(2.0 * lograte))
    scale = start + (1.0 - start) * root
    return recall, admit, lograte, decay, root, scale


def nt(left, right):
    return lax.dot_general(left, right, contract_last, preferred_element_type=f32)


def tn(left, right):
    return lax.dot_general(left, right, contract_first, preferred_element_type=f32)


def nn(left, right):
    return jnp.dot(left, right, preferred_element_type=f32)


def mix_kernel(
    tok, w, gates, terms_ref, gain, meta,
    normed, x_out, y_out, conv_out, ra_out, rx_out, prior_out, mixed, part,
    xpad, dec, drv, sts, carry,
):
    step = pl.program_id(0)

    @pl.when(step == 0)
    def _():
        xpad[0:8] = jnp.zeros((8, WP), f32)
        carry[...] = jnp.zeros((8, WP), f32)

    @pl.when(step > 0)
    def _():
        xpad[0:8] = xpad[CHUNK : CHUNK + 8]

    def body(i, c):
        here = pl.ds(pl.multiple_of(i * 16, 16), 16)
        normed[here] = norm_rows(tok[here].astype(f32), gain[...]).astype(bf16)
        return c

    lax.fori_loop(0, CHUNK // 16, body, 0)
    both = nn(normed[...], w[:, : 2 * WP])
    x_out[...] = both[:, :WP]
    xpad[8:] = both[:, :WP]
    y_out[...] = both[:, WP:]
    terms = terms_ref[...]
    start = meta[:, 0:1]
    conv = terms[4:5] + terms[0:1] * both[:, :WP]
    for k in range(1, CONV):
        conv = conv + terms[k : k + 1] * (meta[:, k : k + 1] * xpad[8 - k : 8 - k + CHUNK])
    conv_out[...] = conv
    lowered = conv.astype(bf16)
    raw_a = nn(lowered, gates[0])
    raw_x = nn(lowered, gates[1])
    ra_out[...] = raw_a
    rx_out[...] = raw_x
    recall, admit, lograte, decay, root, scale = recur(conv, raw_a, raw_x, terms, start)
    dec[...] = decay
    drv[...] = scale * admit * conv
    row = lax.broadcasted_iota(jnp.int32, (8, WP), 0)

    def scan(i, before):
        here = pl.ds(pl.multiple_of(i * 8, 8), 8)
        a, b = dec[here], drv[here]
        for s in (1, 2, 4):
            b = b + a * jnp.where(row >= s, pltpu.roll(b, s, 0), 0.0)
            a = a * jnp.where(row >= s, pltpu.roll(a, s, 0), 1.0)
        state = b + a * before
        sts[here] = state
        prior_out[here] = jnp.where(row >= 1, pltpu.roll(state, 1, 0), before)
        return jnp.broadcast_to(state[7:8], (8, WP))

    carry[...] = lax.fori_loop(0, CHUNK // 8, scan, carry[...], unroll=4)
    value, _ = gelu_parts(y_out[...])
    mixed[...] = (value * sts[...]).astype(bf16)
    part[...] = nt(mixed[...], w[:, 2 * WP :]).astype(bf16)


def rows_spec(width, back=False):
    if back:
        return pl.BlockSpec((CHUNK, width), lambda i: (STEPS - 1 - i, 0))
    return pl.BlockSpec((CHUNK, width), lambda i: (i, 0))


def whole(shape):
    return pl.BlockSpec(shape, lambda i: (0,) * len(shape))


def mix_call(tok, w, gates, terms, gain, meta):
    sds = jax.ShapeDtypeStruct
    wide = [sds((G, WP), f32)] * 6
    return pl.pallas_call(
        mix_kernel,
        grid=(STEPS,),
        out_shape=(sds((G, D), bf16), *wide, sds((G, WP), bf16), sds((G, D), bf16)),
        in_specs=[
            rows_spec(D), whole((D, MW)), whole((2, WP, WP)), whole((16, WP)), whole((1, D)), rows_spec(8),
        ],
        out_specs=[rows_spec(D)] + [rows_spec(WP)] * 6 + [rows_spec(WP), rows_spec(D)],
        scratch_shapes=[
            VMEM((CHUNK + 8, WP), f32), VMEM((CHUNK, WP), f32), VMEM((CHUNK, WP), f32),
            VMEM((CHUNK, WP), f32), VMEM((8, WP), f32),
        ],
        compiler_params=pltpu.CompilerParams(vmem_limit_bytes=50 << 20),
        cost_estimate=pl.CostEstimate(flops=2 * G * D * MW, bytes_accessed=30 << 20, transcendentals=0),
        name="mix",
    )(tok, w, gates, terms, gain, meta)


def unmix_kernel(
    adj_out, w, gates, terms_ref, meta, x_in, y_in, conv_in, ra_in, rx_in, prior_in,
    both, part, gate_grad, sums,
    dec, adj, acp, carry,
):
    step = pl.program_id(0)

    @pl.when(step == 0)
    def _():
        dec[CHUNK:] = jnp.zeros((8, WP), f32)
        acp[CHUNK:] = jnp.zeros((8, WP), f32)
        carry[...] = jnp.zeros((8, WP), f32)
        gate_grad[...] = jnp.zeros(gate_grad.shape, f32)
        sums[...] = jnp.zeros(sums.shape, f32)

    @pl.when(step > 0)
    def _():
        dec[CHUNK:] = dec[0:8]
        acp[CHUNK:] = acp[0:8]

    terms = terms_ref[...]
    start = meta[:, 0:1]
    conv, prior = conv_in[...], prior_in[...]
    recall, admit, lograte, decay, root, scale = recur(conv, ra_in[...], rx_in[...], terms, start)
    dec[0:CHUNK] = decay
    states = decay * prior + scale * admit * conv
    adj_mixed = nn(adj_out[...], w[:, 2 * WP :])
    value, slope = gelu_parts(y_in[...])
    adj[...] = adj_mixed * value
    both[:, WP:] = (adj_mixed * states * slope).astype(bf16)
    row = lax.broadcasted_iota(jnp.int32, (8, WP), 0)

    def scan(i, after):
        at = pl.multiple_of((CHUNK // 8 - 1 - i) * 8, 8)
        here = pl.ds(at, 8)
        later = dec[pl.ds(pl.multiple_of(at + 8, 8), 8)]
        a = jnp.where(row < 7, pltpu.roll(dec[here], 7, 0), later[0:1])
        b = adj[here]
        for s in (1, 2, 4):
            b = b + a * jnp.where(row < 8 - s, pltpu.roll(b, 8 - s, 0), 0.0)
            a = a * jnp.where(row < 8 - s, pltpu.roll(a, 8 - s, 0), 1.0)
        value = b + a * after
        adj[here] = value
        return jnp.broadcast_to(value[0:1], (8, WP))

    carry[...] = lax.fori_loop(0, CHUNK // 8, scan, carry[...], unroll=4)
    adjoint = adj[...]
    flow = adjoint * admit * conv
    adj_lograte = adjoint * prior * decay - (1.0 - start) * flow * (jnp.exp(2.0 * lograte) / root)
    adj_ra = adj_lograte * terms[7:8] * (recall * (1.0 - recall))
    adj_rx = flow * scale * (1.0 - admit)

    def total(v):
        return jnp.sum(v, axis=0, keepdims=True)

    sums[5:6] += total(adj_ra)
    sums[6:7] += total(adj_rx)
    sums[7:8] += total(adj_lograte * recall) * terms[8:9]
    low_a, low_x = adj_ra.astype(bf16), adj_rx.astype(bf16)
    lowered = conv.astype(bf16)
    adj_conv = adjoint * scale * admit + nt(low_a, gates[0]) + nt(low_x, gates[1])
    gate_grad[0] += tn(lowered, low_a)
    gate_grad[1] += tn(lowered, low_x)
    acp[0:CHUNK] = adj_conv
    x = x_in[...]
    adj_x = terms[0:1] * adj_conv
    sums[4:5] += total(adj_conv)
    sums[0:1] += total(adj_conv * x)
    for k in range(1, CONV):
        moved = meta[:, 3 + k : 4 + k] * acp[k : k + CHUNK]
        adj_x = adj_x + terms[k : k + 1] * moved
        sums[k : k + 1] += total(moved * x)
    both[:, :WP] = adj_x.astype(bf16)
    part[...] = nt(both[...], w[:, : 2 * WP]).astype(bf16)


def unmix_call(adj_out, w, gates, terms, meta, saved):
    sds = jax.ShapeDtypeStruct
    return pl.pallas_call(
        unmix_kernel,
        grid=(STEPS,),
        out_shape=(sds((G, 2 * WP), bf16), sds((G, D), bf16), sds((2, WP, WP), f32), sds((8, WP), f32)),
        in_specs=[
            rows_spec(D, True), whole((D, MW)), whole((2, WP, WP)), whole((16, WP)), rows_spec(8, True),
        ]
        + [rows_spec(WP, True)] * 6,
        out_specs=[rows_spec(2 * WP, True), rows_spec(D, True), whole((2, WP, WP)), whole((8, WP))],
        scratch_shapes=[
            VMEM((CHUNK + 8, WP), f32), VMEM((CHUNK, WP), f32), VMEM((CHUNK + 8, WP), f32), VMEM((8, WP), f32),
        ],
        compiler_params=pltpu.CompilerParams(vmem_limit_bytes=50 << 20),
        cost_estimate=pl.CostEstimate(flops=2 * G * D * MW, bytes_accessed=30 << 20, transcendentals=0),
        name="unmix",
    )(adj_out, w, gates, terms, meta, *saved)


def feed_kernel(n2, cot, w, part, back, hidden, adj_gu):
    gu = nn(n2[...], w[:, : 2 * FL])
    gate, up = gu[:, :FL], gu[:, FL:]
    adj_hidden = nn(cot[...], w[:, 2 * FL :])
    value, slope = gelu_parts(gate)
    hidden[...] = (value * up).astype(bf16)
    adj_gu[:, :FL] = (adj_hidden * up * slope).astype(bf16)
    adj_gu[:, FL:] = (adj_hidden * value).astype(bf16)
    part[...] = nt(hidden[...], w[:, 2 * FL :]).astype(bf16)
    back[...] = nt(adj_gu[...], w[:, : 2 * FL]).astype(bf16)


def feed_call(n2, cot, w):
    sds = jax.ShapeDtypeStruct
    return pl.pallas_call(
        feed_kernel,
        grid=(STEPS,),
        out_shape=(sds((G, D), bf16), sds((G, D), bf16), sds((G, FL), bf16), sds((G, 2 * FL), bf16)),
        in_specs=[rows_spec(D), rows_spec(D), whole((D, FW))],
        out_specs=[rows_spec(D), rows_spec(D), rows_spec(FL), rows_spec(2 * FL)],
        compiler_params=pltpu.CompilerParams(vmem_limit_bytes=60 << 20),
        cost_estimate=pl.CostEstimate(flops=4 * G * D * FW, bytes_accessed=30 << 20, transcendentals=0),
        name="feed",
    )(n2, cot, w)


def grad_kernel(left, right, left_two, right_two, out):
    width = right.shape[1]
    out[:, :width] = tn(left[...], right[...]).astype(bf16)
    out[:, width:] = tn(left_two[...], right_two[...]).astype(bf16)


def grad_call(left, right, left_two, right_two, name):
    width = right.shape[1] + right_two.shape[1]
    block = 256
    return pl.pallas_call(
        grad_kernel,
        grid=(D // block,),
        out_shape=jax.ShapeDtypeStruct((D, width), bf16),
        in_specs=[
            pl.BlockSpec((G, block), lambda i: (0, i)), whole(right.shape),
            pl.BlockSpec((G, block), lambda i: (0, i)), whole(right_two.shape),
        ],
        out_specs=pl.BlockSpec((block, width), lambda i: (i, 0)),
        compiler_params=pltpu.CompilerParams(vmem_limit_bytes=50 << 20),
        cost_estimate=pl.CostEstimate(flops=2 * G * D * width, bytes_accessed=20 << 20, transcendentals=0),
        name=name,
    )(left, right, left_two, right_two)


def shards(tokens, segments, mixer_weights, norm_gains, gate_weights, channel_terms, feed_weights, cotangent):
    sq = lax.axis_index("seq")
    mix = jnp.pad(mixer_weights.reshape(16, 3, SEQ, WL), ((0, 0), (0, 0), (0, 0), (0, WP - WL)))
    mix = mix.transpose(2, 0, 1, 3).reshape(SEQ, 16, MW)
    feed = feed_weights.reshape(16, 3, SEQ, FL).transpose(2, 0, 1, 3).reshape(SEQ, 16, FW)
    gain_rows = jnp.pad(norm_gains.T, ((0, 0), (0, 112)))
    placed = jnp.where(
        lax.broadcasted_iota(jnp.int32, (SEQ, 1, 1), 0) == sq, gain_rows[None], jnp.zeros((), bf16)
    ).reshape(16, 128)
    small = jnp.concatenate([placed, jnp.pad(segments.astype(bf16)[None], ((0, 15), (0, 0)))], 0)
    gate_block = jnp.pad(gate_weights.reshape(-1), (0, 16 * 512 - 40 * BW)).reshape(16, 512)
    chan_block = jnp.pad(channel_terms.reshape(-1), (0, 16 * 256 - 160)).reshape(16, 256)
    tok_all, cot_all, mix_all, feed_own, small_all, gain_all, gate_all, chan_all = prologue(
        tokens, cotangent, mix, feed, small, gate_block, chan_block
    )
    feed_w = lax.all_gather(feed_own.reshape(T, FW), "dp", axis=0, tiled=True)
    gains = gain_all[:, :, :16].reshape(DP, SEQ, 2, 16).transpose(2, 0, 1, 3).reshape(2, 1, D).astype(f32)
    gate_pair = gate_all.reshape(DP, -1)[:, : 40 * BW].reshape(2, 2, BW, BW)
    gates = jnp.pad(gate_pair[:, 0], ((0, 0), (0, WP - BW), (0, WP - BW))) + jnp.pad(
        gate_pair[:, 1], ((0, 0), (BW, WP - 2 * BW), (BW, WP - 2 * BW))
    )
    channel = chan_all.reshape(DP, -1)[:, :160].reshape(WL, 8).T.astype(f32)
    channel = jnp.pad(channel, ((0, 0), (0, WP - WL)))
    lam = channel[7:8]
    terms = jnp.concatenate(
        [channel[:7], -rate_scale * jax.nn.softplus(-lam), rate_scale * jax.nn.sigmoid(-lam), jnp.zeros((7, WP), f32)], 0
    )
    labels = small_all[:, 16].reshape(G).astype(f32)
    behind = [jnp.concatenate([jnp.full((k,), -1.0, f32), labels[: G - k]]) == labels for k in range(1, CONV)]
    ahead = [jnp.concatenate([behind[k - 1][k:], jnp.zeros((k,), bool)]) for k in range(1, CONV)]
    meta = jnp.stack([jnp.logical_not(behind[0])] + behind + ahead + [behind[0]], 1).astype(f32)
    w = mix_all.reshape(D, MW)
    tok_group, cot_group = tok_all.reshape(G, D), cot_all.reshape(G, D)

    normed, *saved, mixed, part = mix_call(tok_group, w, gates, terms, gains[0], meta)
    middle, norm_two = middle_call(part.reshape(SEQ, T, D), tokens, gains[1])
    norm_two = norm_two.reshape(G, D)
    feed_part, back_part, hidden, adj_gu = feed_call(norm_two, cot_group, feed_w)
    feed_grad = grad_call(norm_two, adj_gu, cot_group, hidden, "feedgrad")
    feed_sum = lax.psum_scatter(feed_grad, "dp", scatter_dimension=0, tiled=True)
    adj_middle, gain_two, adj_all = turn_call(back_part.reshape(SEQ, T, D), middle, cotangent, gains[1])
    adj_all = adj_all.reshape(G, D)
    both, in_part, gate_grad, sums = unmix_call(adj_all, w, gates, terms, meta, saved)
    mix_grad = grad_call(normed, both, adj_all, mixed, "mixgrad")

    gate_piece = jnp.stack([gate_grad[:, :BW, :BW], gate_grad[:, BW : 2 * BW, BW : 2 * BW]], 1)
    gate_piece = jnp.pad(gate_piece.reshape(DP, 40 * BW), ((0, 0), (0, 16 * 512 - 40 * BW))).reshape(DP, 4, 16, 128)
    chan_piece = jnp.pad(sums[:, :WL].T.reshape(DP, 160), ((0, 0), (0, 16 * 128 - 160))).reshape(DP, 1, 16, 128)
    extra = jnp.concatenate([gate_piece, chan_piece], 1).astype(bf16)
    input_gradient, activations, mix_out, gate_out, chan_out, gain_out = close_call(
        in_part.reshape(SEQ, T, D), feed_part.reshape(SEQ, T, D), mix_grad.reshape(4, 4, SEQ, 16, MW), extra,
        tokens, adj_middle, middle, gains[0], gain_two,
    )
    feed_out = swap_call(feed_sum.reshape(SEQ, 16, FW))
    mixer_gradient = (
        mix_out.reshape(SEQ, 16, 3, WP)[..., :WL].transpose(1, 2, 0, 3).reshape(16, 3 * W).astype(f32)
    )
    feed_gradient = feed_out.reshape(SEQ, 16, 3, FL).transpose(1, 2, 0, 3).reshape(16, 3 * FF).astype(f32)
    gate_gradient = gate_out.reshape(-1)[: 40 * BW].reshape(40, BW)
    channel_gradient = chan_out.reshape(-1)[:160].reshape(20, 8)
    gain_gradient = lax.dynamic_slice(gain_out, (0, sq * 16), (2, 16)).T
    return (activations, input_gradient, mixer_gradient, gain_gradient, gate_gradient, channel_gradient, feed_gradient)


def solution(mesh):
    one = P(("dp", "seq"))
    two = P(("dp", "seq"), None)
    placed = (two, one, two, two, two, two, two, two)
    return jax.shard_map(shards, mesh=mesh, in_specs=placed, out_specs=(two,) * 7, check_vma=False)
```

time: 3010 us -> 377 us (0.13)
  waiting for transfers between devices: 2160 us -> 0.04 us
  Pallas kernels: 0 us -> 317 us
  other arithmetic: 242 us -> 2.32 us
  local copies, waits for them, and re-layouts: 257 us -> 41.6 us
  matrix products: 202 us -> 0 us
  blocking collectives: 117 us -> 0 us
    unnamed x11 -> x2, waiting for transfers between devices: 1140 us -> 0.03 us
    reduce_scatter x2 -> x1, waiting for transfers between devices: 919 us -> 0.01 us  [shards(): lax.psum_scatter(feed_grad, 'dp', scatter_dimension=0, tiled=True)]
    pallas_call x0 -> x10, Pallas kernels: none -> 317 us  [the longest x1 59.7 us: prologue(): pl.pallas_call(prologue_kernel, out_shape=(sds((SEQ, T, D), bf16), sds((S...]
    dot_general x15 -> x0, matrix products: 202 us -> none  [the longest x1 36.5 us: shards(): lax.dot_general(normed_two, adjoint_gate_up, contract_first, preferred_el...]
    concatenate x25 -> x4, other arithmetic: 155 us -> 0.92 us  [the longest x1 0.76 us: shards(): extra = jnp.concatenate([gate_piece, chan_piece], 1).astype(bf16)]
    slice x99 -> x9, local copies, waits for them, and re-layouts: 136 us -> 1.8 us  [the longest x2 0.79 us: shards(): channel_gradient = chan_out.reshape(-1)[:160].reshape(20, 8)]
    all_gather x6 -> x0, blocking collectives: 117 us -> none  [the longest x4 51.9 us: entering(): pieces = jax.tree.map(lambda part: lax.all_gather(part, axis), value)]
    all_gather x3 -> x1, waiting for transfers between devices: 89.7 us -> 0.01 us  [shards(): feed_w = lax.all_gather(feed_own.reshape(T, FW), 'dp', axis=0, tiled=True)]
  transfers between devices with their start and end apart: 11 -> 2, of which waited for: 8 -> 0; matrix products, arithmetic and copies ran while one was open for 15% -> 3% of each run, Pallas kernels for 0% -> 54%
where the time goes in v1:
time: 377 us; the launch traced here: 376 us
  Pallas kernels  317 us (84%)
  local copies, waits for them, and re-layouts  41.6 us (11%)
  between operations  14.6 us (4%)
    pallas_call x1, Pallas kernels, prologue(): pl.pallas_call(prologue_kernel, out_shape=(sds((SEQ, T, D), bf16), sds((S...  59.7 us
    pallas_call x1, Pallas kernels, close_call(): pl.pallas_call(close_kernel, out_shape=(sds((T, D), f32), sds((T, D), bf1...  58.4 us
    pallas_call x1, Pallas kernels, turn_call(): pl.pallas_call(turn_kernel, out_shape=(sds((T, D), f32), sds((1, D), f32)...  46.7 us
    pallas_call x1, Pallas kernels, middle_call(): pl.pallas_call(middle_kernel, out_shape=(sds((T, D), f32), sds((SEQ, T, D...  44.4 us
    unnamed x56, local copies, waits for them, and re-layouts  26.5 us
    pallas_call x2, Pallas kernels, grad_call(): pl.pallas_call(grad_kernel, grid=(D // block,), out_shape=jax.ShapeDtypeS...  26.5 us
    pallas_call x1, Pallas kernels, feed_call(): pl.pallas_call(feed_kernel, grid=(STEPS,), out_shape=(sds((G, D), bf16),...  26.5 us
    pallas_call x1, Pallas kernels, mix_call(): pl.pallas_call(mix_kernel, grid=(STEPS,), out_shape=(sds((G, D), bf16), *...  23.2 us
  transfers between devices with their start and end apart: 2, of which 0 were waited for; matrix products, arithmetic and copies ran while one was open for 3% of the time, Pallas kernels for 54%

profile of v1, /device:TPU:1, one launch (start us, length us, event | category | flops | bytes accessed | tf_op | source)
XLA Modules:
  0.0 376.3 jit_solution(8011499121820532963)
XLA Ops:
  9.7 0.8 reshape.216
  10.5 1.2 reshape.212
  13.7 59.7 %prologue.1 = (bf16[8,128,2048]{2,1,0:T(8,128)(2,1)S(1)}, bf16[8,128,2048]{2,1,0:T(8,128)(2,1)S(1)}, bf16[16,8,16,1152]{3,2,1,0:T(8,128)(2,1)S(1)}, bf16[8,16,23...) custom-call(bf16[128,2048]{1,0:T(8,128)(2,1)S(1)} %copy-done.1, ...), custom_call_target="tpu_custom_call" | custom-call | flops 1000 | bytes 104857600 | tf_op jit(solution)/shard_map/prologue/pallas_call | solution.py:424
  73.4 2.2 copy-done
  75.6 2.0 copy-done.11
  77.7 2.1 copy-done.12
  82.4 23.2 %mix.1 = (bf16[1024,2048]{1,0:T(8,128)(2,1)}, f32[1024,384]{1,0:T(8,128)S(1)}, f32[1024,384]{1,0:T(8,128)}, f32[1024,384]{1,0:T(8,128)}, f32[1024,384]{1,0:T(8,1...) custom-call(bf16[1024,2048]{1,0:T(8,128)(2,1)} %bitcast.93, ...), custom_call_target="tpu_custom_call" | custom-call | flops 4831838208 | bytes 31457280 | tf_op jit(solution)/shard_map/mix/pallas_call | solution.py:923
  105.7 1.2 copy-done.7
  106.8 0.9 copy-done.16
  107.7 2.2 copy-done.3
  109.9 44.4 %middle.1 = (f32[128,2048]{1,0:T(8,128)S(1)}, bf16[8,128,2048]{2,1,0:T(8,128)(2,1)S(1)}) custom-call(bf16[8,128,2048]{2,1,0:T(8,128)(2,1)S(1)} %bitcast.87, bf16[128,2048]{1,0:T(8,128)(2,1)S(1)} %copy-done.1, f32[1,2048]{1,0:T(1,128)S(1)} %squeeze.17.gain), custom_call_target="tpu_custom_call" | custom-call | flops 1000 | bytes 104857600 | tf_op jit(solution)/shard_map/middle/pallas_call | solution.py:480
  154.3 2.0 copy-done.13
  156.3 26.5 %feed.1 = (bf16[1024,2048]{1,0:T(8,128)(2,1)}, bf16[1024,2048]{1,0:T(8,128)(2,1)}, bf16[1024,768]{1,0:T(8,128)(2,1)}, bf16[1024,1536]{1,0:T(8,128)(2,1)}) custom-call(bf16[1024,2048]{1,0:T(8,128)(2,1)} %bitcast.94, bf16[1024,2048]{1,0:T(8,128)(2,1)} %bitcast.91, bf16[2048,2304]{1,0:T(8,128)(2,1)} %all-gather.2.cloned.1.call-done.w), custom_call_target="tpu_custom_call" | custom-call | flops 19327352832 | bytes 31457280 | tf_op jit(solution)/shard_map/feed/pallas_call | solution.py:1051
  182.8 1.4 copy-done.18
  184.2 15.6 %feedgrad.1 = bf16[2048,2304]{1,0:T(8,128)(2,1)} custom-call(bf16[1024,2048]{1,0:T(8,128)(2,1)} %bitcast.95, bf16[1024,1536]{1,0:T(8,128)(2,1)} %get-tuple-element.77.right, bf16[1024,2048]{1,0:T(8,128)(2,1)} %bitcast.92, bf16[1024,768]{1,0:T(8,128)(2,1)S(1)} %copy-done.18), custom_call_target="tpu_custom_call" | custom-call | flops 9663676416 | bytes 20971520 | tf_op jit(solution)/shard_map/feedgrad/pallas_call | solution.py:1072
  199.9 2.2 copy-done.4
  202.0 46.7 %turn.1 = (f32[128,2048]{1,0:T(8,128)S(1)}, f32[1,2048]{1,0:T(1,128)S(1)}, bf16[8,128,2048]{2,1,0:T(8,128)(2,1)S(1)}) custom-call(bf16[8,128,2048]{2,1,0:T(8,128)(2,1)S(1)} %bitcast.88, f32[128,2048]{1,0:T(8,128)S(1)} %get-tuple-element.54.middle, bf16[128,2048]{1,0:T(8,128)(2,1)S(1)} %copy-done.6, f32[1,2048]{1,0:T(1,128)S(1)} %squeeze.17.gain), custom_call_target="tpu_custom_call" | custom-call | flops 1000 | bytes 104857600 | tf_op jit(solution)/shard_map/turn/pallas_call | solution.py:533
  248.7 2.0 copy-done.2
  250.8 1.0 copy-done.8
  252.4 21.3 %unmix.1 = (bf16[1024,768]{1,0:T(8,128)(2,1)S(1)}, bf16[1024,2048]{1,0:T(8,128)(2,1)}, f32[2,384,384]{2,1,0:T(8,128)S(1)}, f32[8,384]{1,0:T(8,128)S(1)}) custom-call(bf16[1024,2048]{1,0:T(8,128)(2,1)} %bitcast.85, bf16[2048,1152]{1,0:T(8,128)(2,1)} %bitcast.84, bf16[2,384,384]{2,1,0:T(8,128)(2,1)S(1)} %pad_add_fusion.gates, ...), custom_call_target="tpu_custom_call" | custom-call | flops 4831838208 | bytes 31457280 | tf_op jit(solution)/shard_map/unmix/pallas_call | solution.py:1019
  273.6 1.1 copy-done.14
  277.1 11.0 %mixgrad.1 = bf16[2048,1152]{1,0:T(8,128)(2,1)} custom-call(bf16[1024,2048]{1,0:T(8,128)(2,1)} %get-tuple-element.64.left, bf16[1024,768]{1,0:T(8,128)(2,1)S(1)} %copy-done.15, bf16[1024,2048]{1,0:T(8,128)(2,1)} %bitcast.86, bf16[1024,384]{1,0:T(8,128)(2,1)S(1)} %copy-done.17), custom_call_target="tpu_custom_call" | custom-call | flops 4831838208 | bytes 20971520 | tf_op jit(solution)/shard_map/mixgrad/pallas_call | solution.py:1072
  288.1 58.4 %close.1 = (f32[128,2048]{1,0:T(8,128)}, bf16[128,2048]{1,0:T(8,128)(2,1)}, bf16[8,16,1152]{2,1,0:T(8,128)(2,1)}, f32[4,16,128]{2,1,0:T(8,128)}, f32[16,128]{1,0:T(8,128)}, /*index=5*/f32[8,128]{1,0:T(8,128)}) custom-call(bf16[8,128,2048]{2,1,0:T(8,128)(2,1)} %bitcast.100, bf16[8,128,2048]{2,1,0:T(8,128)(2,1)} %bitcast.99, ...), custom_call_target="tpu_custom_call" | custom-call | flops 1000 | bytes 104857600 | tf_op jit(solution)/shard_map/close/pallas_call | solution.py:747
  347.9 0.8 slice.97
  349.4 1.0 reshape.238
  350.9 0.9 reshape.244
  351.8 1.3 dynamic-slice_bitcast_fusion
  353.2 10.8 %swap.1 = bf16[8,16,2304]{2,1,0:T(8,128)(2,1)} custom-call(bf16[8,16,2304]{2,1,0:T(8,128)(2,1)} %bitcast.107), custom_call_target="tpu_custom_call" | custom-call | flops 1000 | bytes 1048576 | tf_op jit(solution)/shard_map/swap/pallas_call | solution.py:796
  364.0 1.6 reshape.247
  366.3 1.4 copy.77
  367.7 0.8 copy.84
  368.5 1.0 copy.85
  (115 shorter events, 13.0 us)
Async XLA Ops:
  7.2 5.2 %copy-start.20 = (bf16[16,18432]{1,0:T(8,128)(2,1)S(1)}, bf16[16,18432]{1,0:T(8,128)(2,1)}, u32[]{:S(2)}) copy-start(bf16[16,18432]{1,0:T(8,128)(2,1)} %param.14) | copy-start | bytes 1769476
  7.2 149.2 %all-gather.2.cloned.1.call-start = ((), (), s32[]{:S(2)}) async-start(), calls=%async_computation.1 | async-start | bytes 10027008 | tf_op jit(solution)/shard_map/all_gather | solution.py:1102
  12.5 1.2 copy-start.1
  12.5 1.2 copy-start.6
  73.4 2.2 copy-start
  75.6 2.0 copy-start.11
  77.7 2.1 copy-start.12
  79.7 273.4 %reduce-scatter.2.cloned.1.call-start = ((), (), s32[]{:S(2)}) async-start(), calls=%async_computation.2 | async-start | bytes 10027008 | tf_op jit(solution)/shard_map/reduce_scatter | solution.py:1126
  81.4 1.0 copy-start.9
  105.7 1.2 copy-start.7
  106.8 0.9 copy-start.16
  107.7 2.2 copy-start.3
  154.3 2.1 copy-start.13
  156.3 43.5 %copy-start.5 = (f32[128,2048]{1,0:T(8,128)}, f32[128,2048]{1,0:T(8,128)S(1)}, u32[]{:S(2)}) copy-start(f32[128,2048]{1,0:T(8,128)S(1)} %get-tuple-element.54.middle) | copy-start | bytes 3145732
  182.8 1.4 copy-start.18
  199.8 2.2 copy-start.4
  248.7 2.1 copy-start.2
  250.8 1.0 copy-start.8
  251.8 0.6 copy-start.10
  273.6 1.1 copy-start.14
  275.3 1.5 copy-start.15
  275.3 1.8 copy-start.17
  366.3 1.4 copy-start.21
  366.3 2.2 copy-start.19
Sparse Core Ops, SparseCore 0:
  79.9 72.3 all-gather.1
  200.0 83.7 reduce-scatter.1

commit v2 on v1

--- a/solution.py
+++ b/solution.py
@@ -91,12 +91,20 @@
 
 
 class Gather:
-    sems = 10
-
-    def __init__(self, me, own, full, send, recv):
-        self.me, self.own, self.full, self.send, self.recv = me, own, full, send, recv
-        self.sent = []
-        self.a, self.b = pl.ds(0, HALF), pl.ds(HALF, HALF)
+    @staticmethod
+    def scratch(n):
+        return [VMEM((G, n), bf16), DMA((10,)), DMA((10,)), DMA((SEQ,))]
+
+    def __init__(self, me, own, out, full, send, recv, keep):
+        self.me, self.own, self.out, self.full = me, own, out, full
+        self.send, self.recv, self.keep = send, recv, keep
+        self.sent, self.kept = [], []
+
+    def block(self, k, c, half=None):
+        base = self.me.slot(k, c) * T
+        if half is None:
+            return self.full.at[pl.ds(pl.multiple_of(base, T), T)]
+        return self.full.at[pl.ds(pl.multiple_of(base + half * HALF, HALF), HALF)]
 
     def push(self, n, src, dst, device):
         copy = remote(src, dst, self.send.at[n], self.recv.at[n], device)
@@ -106,45 +114,60 @@
     def arrived(self, n, dst):
         remote(dst, dst, self.send.at[n], self.recv.at[n], self.me.sibling()).wait_recv()
 
+    def store(self, k, c):
+        if self.out is None:
+            return
+        there = self.out.at[pl.ds(pl.multiple_of(self.me.slot(k, c) * T, T), T)]
+        copy = pltpu.make_async_copy(self.block(k, c), there, self.keep.at[len(self.kept)])
+        copy.start()
+        self.kept.append(copy)
+
     def start(self):
-        me, full = self.me, self.full
-        mine = me.sq
+        me = self.me
         right, left = me.z_peer(1), me.z_peer(3)
-        self.push(0, self.own.at[self.a], full.at[mine, self.a], right)
-        self.push(1, self.own.at[self.b], full.at[mine, self.b], left)
-        self.push(2, self.own.at[self.b], full.at[mine, self.b], right)
-        self.push(3, self.own.at[self.a], full.at[mine, self.a], left)
-        self.push(4, self.own, full.at[mine], me.sibling())
+        mine = self.block(0, me.c)
+        a, b = self.block(0, me.c, 0), self.block(0, me.c, 1)
+        self.push(0, a, a, right)
+        self.push(1, b, b, left)
+        self.push(2, b, b, right)
+        self.push(3, a, a, left)
+        self.push(4, mine, mine, me.sibling())
+        self.store(0, me.c)
 
     def forward(self):
-        me, full = self.me, self.full
+        me = self.me
         right, left = me.z_peer(1), me.z_peer(3)
-        from_left, from_right = me.slot(3, me.c), me.slot(1, me.c)
-        self.arrived(0, full.at[from_left, self.a])
-        self.push(5, full.at[from_left, self.a], full.at[from_left, self.a], right)
-        self.arrived(1, full.at[from_right, self.b])
-        self.push(6, full.at[from_right, self.b], full.at[from_right, self.b], left)
+        a, b = self.block(3, me.c, 0), self.block(1, me.c, 1)
+        self.arrived(0, a)
+        self.push(5, a, a, right)
+        self.arrived(1, b)
+        self.push(6, b, b, left)
 
     def across(self):
-        me, full = self.me, self.full
-        from_left, from_right, far = me.slot(3, me.c), me.slot(1, me.c), me.slot(2, me.c)
-        self.arrived(2, full.at[from_left, self.b])
-        self.push(7, full.at[from_left], full.at[from_left], me.sibling())
-        self.arrived(3, full.at[from_right, self.a])
-        self.push(8, full.at[from_right], full.at[from_right], me.sibling())
-        self.arrived(5, full.at[far, self.a])
-        self.arrived(6, full.at[far, self.b])
-        self.push(9, full.at[far], full.at[far], me.sibling())
+        me = self.me
+        self.arrived(2, self.block(3, me.c, 1))
+        whole = self.block(3, me.c)
+        self.push(7, whole, whole, me.sibling())
+        self.store(3, me.c)
+        self.arrived(3, self.block(1, me.c, 0))
+        whole = self.block(1, me.c)
+        self.push(8, whole, whole, me.sibling())
+        self.store(1, me.c)
+        self.arrived(5, self.block(2, me.c, 0))
+        self.arrived(6, self.block(2, me.c, 1))
+        whole = self.block(2, me.c)
+        self.push(9, whole, whole, me.sibling())
+        self.store(2, me.c)
 
     def finish(self):
-        me, full = self.me, self.full
-        other = 1 - me.c
-        self.arrived(4, full.at[me.slot(0, other)])
-        self.arrived(7, full.at[me.slot(3, other)])
-        self.arrived(8, full.at[me.slot(1, other)])
-        self.arrived(9, full.at[me.slot(2, other)])
+        other = 1 - self.me.c
+        for n, k in ((4, 0), (7, 3), (8, 1), (9, 2)):
+            self.arrived(n, self.block(k, other))
+            self.store(k, other)
         for copy in self.sent:
             copy.wait_send()
+        for copy in self.kept:
+            copy.wait()
 
 
 def add_rows(out, at, terms, rows, step=32):
@@ -188,6 +211,9 @@
         self.send, self.recv = send, recv
         self.sent = []
 
+    def piece(self, k, c):
+        return self.part.at[pl.ds(pl.multiple_of(self.me.slot(k, c) * T, T), T)]
+
     def push(self, n, src, dst, device):
         copy = remote(src, dst, self.send.at[n], self.recv.at[n], device)
         copy.start()
@@ -199,7 +225,7 @@
     def start(self):
         me = self.me
         for k in (2, 1, 3, 0):
-            self.push(k, self.part.at[me.slot(k, 1 - me.c)], self.other.at[k], me.sibling())
+            self.push(k, self.piece(k, 1 - me.c), self.other.at[k], me.sibling())
 
     def join(self):
         me = self.me
@@ -208,7 +234,7 @@
         for k in (2, 1, 3, 0):
             self.arrived(k, self.other.at[k])
             add_rows(
-                self.pair.at[k], 0, [reads(self.part.at[me.slot(k, me.c)]), reads(self.other.at[k])], T
+                self.pair.at[k], 0, [reads(self.piece(k, me.c)), reads(self.other.at[k])], T
             )
             if k == 2:
                 self.push(4, self.pair.at[2, a], self.through.at[0], right)
@@ -248,9 +274,9 @@
 
 def prologue_kernel(
     tok, cot, mix, feed, small, gates, chan,
-    tok_all, cot_all, mix_all, feed_own, small_all, gain_all, gate_all, chan_all,
-    gain_own, gate_own, chan_own, small_in,
-    ts, tr, cs, cr, ms, mr, fs, fr, ss, sr, p1s, p1r, p2s, p2r, gs, gr, es, er, hs, hr, ls,
+    tok_all, cot_all, mix_out, feed_own, small_all, gain_all, gate_all, chan_all,
+    gain_own, gate_own, chan_own, small_in, mix_all,
+    tf, ts, tr, tk, cf, cs, cr, ck, ms, mr, fs, fr, ss, sr, p1s, p1r, p2s, p2r, gs, gr, es, er, hs, hr, ls,
 ):
     me = Place()
     quarter, at = me.dp // 8, me.dp % 8
@@ -270,8 +296,8 @@
         pl.semaphore_signal(barrier, inc=1, device_id=chan_from, device_id_type=MESH)
 
     local = [
-        pltpu.make_async_copy(tok, tok_all.at[me.sq], ls.at[0]),
-        pltpu.make_async_copy(cot, cot_all.at[me.sq], ls.at[1]),
+        pltpu.make_async_copy(tok, tf.at[pl.ds(pl.multiple_of(me.sq * T, T), T)], ls.at[0]),
+        pltpu.make_async_copy(cot, cf.at[pl.ds(pl.multiple_of(me.sq * T, T), T)], ls.at[1]),
         pltpu.make_async_copy(mix.at[me.sq], mix_all.at[me.dp, me.sq], ls.at[2]),
         pltpu.make_async_copy(feed.at[me.sq], feed_own.at[me.sq], ls.at[3]),
         pltpu.make_async_copy(small, small_in.at[me.sq], ls.at[4]),
@@ -311,14 +337,15 @@
     def _():
         chan_local.start()
 
-    first = Gather(me, tok, tok_all, ts, tr)
+    local[0].wait()
+    first = Gather(me, tok, tok_all, tf, ts, tr, tk)
     first.start()
     for k in order:
         to = (me.sq + k) % SEQ
         sent.append(remote(feed.at[to], feed_own.at[me.sq], fs.at[k], fr.at[k], me.seq_peer(k)))
         sent[-1].start()
 
-    for copy in local:
+    for copy in local[1:]:
         copy.wait()
     for k in range(1, SEQ):
         source = (me.sq - k + SEQ) % SEQ
@@ -373,6 +400,8 @@
             sent[-1].start()
 
     first.forward()
+    second = Gather(me, cot, cot_all, cf, cs, cr, ck)
+    second.start()
 
     for j in (0, 2, 1, 3):
         if j:
@@ -390,8 +419,6 @@
             sent.append(remote(block, block, p2s.at[4 + j, k], p2r.at[4 + j, k], me.dp_peer(me.x_dp(k))))
             sent[-1].start()
 
-    second = Gather(me, cot, cot_all, cs, cr)
-    second.start()
     first.across()
     second.forward()
     first.finish()
@@ -414,8 +441,11 @@
             row = (me.x - k + 4) % 4 * 4 + (me.y - j + 4) % 4
             block = mix_all.at[row, hi]
             remote(block, block, p2s.at[4 + j, k], p2r.at[4 + j, k], me.sibling()).wait_recv()
+    keep = pltpu.make_async_copy(mix_all, mix_out, ls.at[7])
+    keep.start()
     for copy in sent:
         copy.wait_send()
+    keep.wait()
 
 
 def prologue(tokens, cot, mix, feed, small, gates, chan):
@@ -424,7 +454,7 @@
     return pl.pallas_call(
         prologue_kernel,
         out_shape=(
-            sds((SEQ, T, D), bf16), sds((SEQ, T, D), bf16), sds((DP, SEQ, 16, MW), bf16),
+            sds((G, D), bf16), sds((G, D), bf16), sds((DP, SEQ, 16, MW), bf16),
             sds((SEQ, 16, FW), bf16), sds((SEQ, 32, 128), bf16), sds((DP, 16, 128), bf16),
             sds((DP, 16, 512), bf16), sds((DP, 16, 256), bf16),
         ),
@@ -432,12 +462,12 @@
         out_specs=[hbm, hbm, hbm, hbm, vmem, vmem, vmem, vmem],
         scratch_shapes=[
             VMEM((16, 128), bf16), VMEM((16, 512), bf16), VMEM((16, 256), bf16), VMEM((SEQ, 32, 128), bf16),
-            DMA((10,)), DMA((10,)), DMA((10,)), DMA((10,)),
+            VMEM((DP, SEQ, 16, MW), bf16), *Gather.scratch(D), *Gather.scratch(D),
             DMA((SEQ,)), DMA((SEQ,)), DMA((SEQ,)), DMA((SEQ,)), DMA((SEQ,)), DMA((SEQ,)),
             DMA((8,)), DMA((8,)), DMA((8, 4)), DMA((8, 4)),
             DMA((1,)), DMA((1,)), DMA((3, DP)), DMA((3, DP)), DMA((2,)), DMA((2,)), DMA((8,)),
         ],
-        compiler_params=pltpu.CompilerParams(collective_id=1, has_side_effects=True, vmem_limit_bytes=32 << 20),
+        compiler_params=pltpu.CompilerParams(collective_id=1, has_side_effects=True, vmem_limit_bytes=62 << 20),
         cost_estimate=pl.CostEstimate(flops=1000, bytes_accessed=100 << 20, transcendentals=0),
         name="prologue",
     )(tokens, cot, mix, feed, small, gates, chan)
@@ -447,9 +477,11 @@
     return value * lax.rsqrt(jnp.mean(value * value, axis=-1, keepdims=True) + epsilon) * gain
 
 
-def middle_kernel(part, tok, gain, middle, norm_all, own, *rest):
-    scatter, (gs, gr, ls) = rest[:7], rest[7:]
+def middle_kernel(part, tok, gain, middle, norm_all, *rest):
+    scatter, gathering = rest[:7], rest[7:]
     me = Place()
+    mine = pl.multiple_of(me.sq * T, T)
+    own = gathering[0]
     barrier, count = greet(z_peers(me))
     pl.semaphore_wait(barrier, count)
     total = Scatter(me, part, *scatter)
@@ -460,18 +492,16 @@
 
     def body(i, carry):
         here = pl.ds(pl.multiple_of(i * 16, 16), 16)
-        own[here] = norm_rows(middle[here], gain[...]).astype(bf16)
+        there = pl.ds(pl.multiple_of(mine + i * 16, 16), 16)
+        own[there] = norm_rows(middle[here], gain[...]).astype(bf16)
         return carry
 
     lax.fori_loop(0, T // 16, body, 0)
-    keep = pltpu.make_async_copy(own, norm_all.at[me.sq], ls.at[0])
-    keep.start()
-    gather = Gather(me, own, norm_all, gs, gr)
+    gather = Gather(me, own, norm_all, *gathering)
     gather.start()
     gather.forward()
     gather.across()
     gather.finish()
-    keep.wait()
 
 
 def middle_call(part, tok, gain):
@@ -479,11 +509,11 @@
     hbm, vmem = pl.BlockSpec(memory_space=ANY), pl.BlockSpec(memory_space=VMEM)
     return pl.pallas_call(
         middle_kernel,
-        out_shape=(sds((T, D), f32), sds((SEQ, T, D), bf16)),
+        out_shape=(sds((T, D), f32), sds((G, D), bf16)),
         in_specs=[vmem, vmem, vmem],
         out_specs=[vmem, hbm],
-        scratch_shapes=[VMEM((T, D), bf16)] + Scatter.scratch(D) + [DMA((10,)), DMA((10,)), DMA((1,))],
-        compiler_params=pltpu.CompilerParams(collective_id=2, has_side_effects=True, vmem_limit_bytes=40 << 20),
+        scratch_shapes=Scatter.scratch(D) + Gather.scratch(D),
+        compiler_params=pltpu.CompilerParams(collective_id=2, has_side_effects=True, vmem_limit_bytes=62 << 20),
         cost_estimate=pl.CostEstimate(flops=1000, bytes_accessed=100 << 20, transcendentals=0),
         name="middle",
     )(part, tok, gain)
@@ -497,9 +527,11 @@
     return r * (scaled - normed * (inner * r)), incoming * normed
 
 
-def turn_kernel(part, middle, cot, gain, adj_middle, gain_grad, adj_all, adj, own, *rest):
-    scatter, (gs, gr, ls) = rest[:7], rest[7:]
+def turn_kernel(part, middle, cot, gain, adj_middle, gain_grad, adj_all, adj, *rest):
+    scatter, gathering = rest[:7], rest[7:]
     me = Place()
+    mine = pl.multiple_of(me.sq * T, T)
+    own = gathering[0]
     barrier, count = greet(z_peers(me))
     pl.semaphore_wait(barrier, count)
     total = Scatter(me, part, *scatter)
@@ -513,18 +545,15 @@
         pulled, terms = norm_pull(middle[here], gain[...], adj[here])
         value = cot[here].astype(f32) + pulled
         adj_middle[here] = value
-        own[here] = value.astype(bf16)
+        own[pl.ds(pl.multiple_of(mine + i * 16, 16), 16)] = value.astype(bf16)
         return carry + jnp.sum(terms, axis=0, keepdims=True)
 
     gain_grad[...] = lax.fori_loop(0, T // 16, body, jnp.zeros((1, D), f32))
-    keep = pltpu.make_async_copy(own, adj_all.at[me.sq], ls.at[0])
-    keep.start()
-    gather = Gather(me, own, adj_all, gs, gr)
+    gather = Gather(me, own, adj_all, *gathering)
     gather.start()
     gather.forward()
     gather.across()
     gather.finish()
-    keep.wait()
 
 
 def turn_call(part, middle, cot, gain):
@@ -532,26 +561,32 @@
     hbm, vmem = pl.BlockSpec(memory_space=ANY), pl.BlockSpec(memory_space=VMEM)
     return pl.pallas_call(
         turn_kernel,
-        out_shape=(sds((T, D), f32), sds((1, D), f32), sds((SEQ, T, D), bf16)),
+        out_shape=(sds((T, D), f32), sds((1, D), f32), sds((G, D), bf16)),
         in_specs=[vmem] * 4,
         out_specs=[vmem, vmem, hbm],
-        scratch_shapes=[VMEM((T, D), f32), VMEM((T, D), bf16)]
-        + Scatter.scratch(D)
-        + [DMA((10,)), DMA((10,)), DMA((1,))],
-        compiler_params=pltpu.CompilerParams(collective_id=3, has_side_effects=True, vmem_limit_bytes=40 << 20),
+        scratch_shapes=[VMEM((T, D), f32)] + Scatter.scratch(D) + Gather.scratch(D),
+        compiler_params=pltpu.CompilerParams(collective_id=3, has_side_effects=True, vmem_limit_bytes=62 << 20),
         cost_estimate=pl.CostEstimate(flops=1000, bytes_accessed=100 << 20, transcendentals=0),
         name="turn",
     )(part, middle, cot, gain)
 
 
 def close_kernel(
-    part, feed_part, mg, eg, tok, adj_middle, middle, gain, gain_two,
+    part, feed_part, normed_in, both_in, adj_in, mixed_in, eg, tok, adj_middle, middle, gain, gain_two,
     in_grad, act, mix_out, gate_out, chan_out, gain_out,
-    adj, r1, s1, r2, last, e_in, gate_sum, chan_sum, gp, gp_in, gain_sum, gain_in, *rest,
+    normed, both, adj_out, mixed, mg, adj, r1, s1, r2, last, e_in, gate_sum, chan_sum, gp, gp_in, gain_sum, gain_in, *rest,
 ):
     one, two = rest[:7], rest[7:14]
-    m1s, m1r, m2s, m2r, m3s, m3r, es, er, gs, gr, hs, hr, qs, qr, ls = rest[14:]
+    m1s, m1r, m2s, m2r, m3s, m3r, es, er, gs, gr, hs, hr, qs, qr, ls, ws = rest[14:]
     me = Place()
+    loads = [
+        pltpu.make_async_copy(src, dst, ws.at[n])
+        for n, (src, dst) in enumerate(
+            ((normed_in, normed), (both_in, both), (adj_in, adj_out), (mixed_in, mixed))
+        )
+    ]
+    for copy in loads:
+        copy.start()
     quarter, at = me.dp // 8, me.dp % 8
     gate_to = (8 * quarter + me.sq, at)
     gate_self = me.sq == at
@@ -583,13 +618,28 @@
     inner = Scatter(me, part, *one)
     outer = Scatter(me, feed_part, *two)
     inner.start()
-    for k in (2, 1, 3):
-        push(mg.at[:, (me.y + k) % 4, lo], r1.at[0, k - 1], m1s.at[k], m1r.at[k], me.dp_peer(me.y_dp(k)))
-        push(mg.at[(me.x + k) % 4, :, hi], r1.at[1, k - 1], m1s.at[4 + k], m1r.at[4 + k], me.dp_peer(me.x_dp(k)))
     for k in range(1, DP):
         to = (me.dp + k) % DP
         push(eg.at[to], e_in.at[k], es.at[k], er.at[k], me.dp_peer(to))
     inner.join()
+    for copy in loads:
+        copy.wait()
+
+    def tile(i, carry):
+        here = pl.ds(pl.multiple_of(i * 256, 256), 256)
+        left = tn(normed[:, here], both[...]).astype(bf16)
+        right = tn(adj_out[:, here], mixed[...]).astype(bf16)
+        for h in range(2):
+            for n in range(SEQ):
+                rows = slice(h * T + n * 16, h * T + (n + 1) * 16)
+                mg[i // 2, i % 2 * 2 + h, n, :, : 2 * WP] = left[rows]
+                mg[i // 2, i % 2 * 2 + h, n, :, 2 * WP :] = right[rows]
+        return carry
+
+    lax.fori_loop(0, 8, tile, 0)
+    for k in (2, 1, 3):
+        push(mg.at[:, (me.y + k) % 4, lo], r1.at[0, k - 1], m1s.at[k], m1r.at[k], me.dp_peer(me.y_dp(k)))
+        push(mg.at[(me.x + k) % 4, :, hi], r1.at[1, k - 1], m1s.at[4 + k], m1r.at[4 + k], me.dp_peer(me.x_dp(k)))
     outer.start()
     inner.relay()
     outer.join()
@@ -741,7 +791,7 @@
         copy.wait_send()
 
 
-def close_call(part, feed_part, mg, eg, tok, adj_middle, middle, gain, gain_two):
+def close_call(part, feed_part, normed, both, adj_out, mixed, eg, tok, adj_middle, middle, gain, gain_two):
     sds = jax.ShapeDtypeStruct
     vmem = pl.BlockSpec(memory_space=VMEM)
     return pl.pallas_call(
@@ -750,9 +800,11 @@
             sds((T, D), f32), sds((T, D), bf16), sds((SEQ, 16, MW), bf16),
             sds((4, 16, 128), f32), sds((16, 128), f32), sds((8, 128), f32),
         ),
-        in_specs=[vmem] * 9,
+        in_specs=[vmem] * 2 + [pl.BlockSpec(memory_space=ANY)] * 4 + [vmem] * 6,
         out_specs=[vmem] * 6,
         scratch_shapes=[
+            VMEM((G, D), bf16), VMEM((G, 2 * WP), bf16), VMEM((G, D), bf16), VMEM((G, WP), bf16),
+            VMEM((4, 4, SEQ, 16, MW), bf16),
             VMEM((T, D), f32),
             VMEM((2, 3, 4, 4, 16, MW), bf16), VMEM((2, 4, 4, 16, MW), bf16), VMEM((2, 3, 4, 16, MW), bf16),
             VMEM((SEQ, 16, MW), bf16), VMEM((DP, 5, 16, 128), bf16), VMEM((4, 16, 128), f32),
@@ -764,12 +816,12 @@
         + [
             DMA((8,)), DMA((8,)), DMA((8,)), DMA((8,)), DMA((8,)), DMA((8,)),
             DMA((DP,)), DMA((DP,)), DMA((DP,)), DMA((DP,)), DMA((2,)), DMA((2,)),
-            DMA((SEQ,)), DMA((SEQ,)), DMA((3,)),
+            DMA((SEQ,)), DMA((SEQ,)), DMA((3,)), DMA((4,)),
         ],
-        compiler_params=pltpu.CompilerParams(collective_id=4, has_side_effects=True, vmem_limit_bytes=60 << 20),
+        compiler_params=pltpu.CompilerParams(collective_id=4, has_side_effects=True, vmem_limit_bytes=62 << 20),
         cost_estimate=pl.CostEstimate(flops=1000, bytes_accessed=100 << 20, transcendentals=0),
         name="close",
-    )(part, feed_part, mg, eg, tok, adj_middle, middle, gain, gain_two)
+    )(part, feed_part, normed, both, adj_out, mixed, eg, tok, adj_middle, middle, gain, gain_two)
 
 
 def swap_kernel(src, dst, ss, sr, ls):
@@ -799,7 +851,7 @@
         in_specs=[hbm],
         out_specs=hbm,
         scratch_shapes=[DMA((SEQ,)), DMA((SEQ,)), DMA((1,))],
-        compiler_params=pltpu.CompilerParams(collective_id=5, has_side_effects=True),
+        compiler_params=pltpu.CompilerParams(collective_id=5, has_side_effects=True, vmem_limit_bytes=62 << 20),
         cost_estimate=pl.CostEstimate(flops=1000, bytes_accessed=1 << 20, transcendentals=0),
         name="swap",
     )(src)
@@ -932,7 +984,7 @@
             VMEM((CHUNK + 8, WP), f32), VMEM((CHUNK, WP), f32), VMEM((CHUNK, WP), f32),
             VMEM((CHUNK, WP), f32), VMEM((8, WP), f32),
         ],
-        compiler_params=pltpu.CompilerParams(vmem_limit_bytes=50 << 20),
+        compiler_params=pltpu.CompilerParams(vmem_limit_bytes=62 << 20),
         cost_estimate=pl.CostEstimate(flops=2 * G * D * MW, bytes_accessed=30 << 20, transcendentals=0),
         name="mix",
     )(tok, w, gates, terms, gain, meta)
@@ -1028,7 +1080,7 @@
         scratch_shapes=[
             VMEM((CHUNK + 8, WP), f32), VMEM((CHUNK, WP), f32), VMEM((CHUNK + 8, WP), f32), VMEM((8, WP), f32),
         ],
-        compiler_params=pltpu.CompilerParams(vmem_limit_bytes=50 << 20),
+        compiler_params=pltpu.CompilerParams(vmem_limit_bytes=62 << 20),
         cost_estimate=pl.CostEstimate(flops=2 * G * D * MW, bytes_accessed=30 << 20, transcendentals=0),
         name="unmix",
     )(adj_out, w, gates, terms, meta, *saved)
@@ -1054,7 +1106,7 @@
         out_shape=(sds((G, D), bf16), sds((G, D), bf16), sds((G, FL), bf16), sds((G, 2 * FL), bf16)),
         in_specs=[rows_spec(D), rows_spec(D), whole((D, FW))],
         out_specs=[rows_spec(D), rows_spec(D), rows_spec(FL), rows_spec(2 * FL)],
-        compiler_params=pltpu.CompilerParams(vmem_limit_bytes=60 << 20),
+        compiler_params=pltpu.CompilerParams(vmem_limit_bytes=62 << 20),
         cost_estimate=pl.CostEstimate(flops=4 * G * D * FW, bytes_accessed=30 << 20, transcendentals=0),
         name="feed",
     )(n2, cot, w)
@@ -1078,7 +1130,7 @@
             pl.BlockSpec((G, block), lambda i: (0, i)), whole(right_two.shape),
         ],
         out_specs=pl.BlockSpec((block, width), lambda i: (i, 0)),
-        compiler_params=pltpu.CompilerParams(vmem_limit_bytes=50 << 20),
+        compiler_params=pltpu.CompilerParams(vmem_limit_bytes=62 << 20),
         cost_estimate=pl.CostEstimate(flops=2 * G * D * width, bytes_accessed=20 << 20, transcendentals=0),
         name=name,
     )(left, right, left_two, right_two)
@@ -1116,26 +1168,22 @@
     ahead = [jnp.concatenate([behind[k - 1][k:], jnp.zeros((k,), bool)]) for k in range(1, CONV)]
     meta = jnp.stack([jnp.logical_not(behind[0])] + behind + ahead + [behind[0]], 1).astype(f32)
     w = mix_all.reshape(D, MW)
-    tok_group, cot_group = tok_all.reshape(G, D), cot_all.reshape(G, D)
+    tok_group, cot_group = tok_all, cot_all
 
     normed, *saved, mixed, part = mix_call(tok_group, w, gates, terms, gains[0], meta)
-    middle, norm_two = middle_call(part.reshape(SEQ, T, D), tokens, gains[1])
-    norm_two = norm_two.reshape(G, D)
+    middle, norm_two = middle_call(part, tokens, gains[1])
     feed_part, back_part, hidden, adj_gu = feed_call(norm_two, cot_group, feed_w)
     feed_grad = grad_call(norm_two, adj_gu, cot_group, hidden, "feedgrad")
     feed_sum = lax.psum_scatter(feed_grad, "dp", scatter_dimension=0, tiled=True)
-    adj_middle, gain_two, adj_all = turn_call(back_part.reshape(SEQ, T, D), middle, cotangent, gains[1])
-    adj_all = adj_all.reshape(G, D)
+    adj_middle, gain_two, adj_all = turn_call(back_part, middle, cotangent, gains[1])
     both, in_part, gate_grad, sums = unmix_call(adj_all, w, gates, terms, meta, saved)
-    mix_grad = grad_call(normed, both, adj_all, mixed, "mixgrad")
 
     gate_piece = jnp.stack([gate_grad[:, :BW, :BW], gate_grad[:, BW : 2 * BW, BW : 2 * BW]], 1)
     gate_piece = jnp.pad(gate_piece.reshape(DP, 40 * BW), ((0, 0), (0, 16 * 512 - 40 * BW))).reshape(DP, 4, 16, 128)
     chan_piece = jnp.pad(sums[:, :WL].T.reshape(DP, 160), ((0, 0), (0, 16 * 128 - 160))).reshape(DP, 1, 16, 128)
     extra = jnp.concatenate([gate_piece, chan_piece], 1).astype(bf16)
     input_gradient, activations, mix_out, gate_out, chan_out, gain_out = close_call(
-        in_part.reshape(SEQ, T, D), feed_part.reshape(SEQ, T, D), mix_grad.reshape(4, 4, SEQ, 16, MW), extra,
-        tokens, adj_middle, middle, gains[0], gain_two,
+        in_part, feed_part, normed, both, adj_all, mixed, extra, tokens, adj_middle, middle, gains[0], gain_two,
     )
     feed_out = swap_call(feed_sum.reshape(SEQ, 16, FW))
     mixer_gradient = (

time: 377 us -> 373 us (0.989)
  local copies, waits for them, and re-layouts: 41.6 us -> 25.4 us
  Pallas kernels: 317 us -> 324 us
  other arithmetic: 2.32 us -> 8.67 us
    unnamed x56 -> x20, local copies, waits for them, and re-layouts: 26.5 us -> 5.87 us
    pallas_call x2 -> x1, Pallas kernels: 26.5 us -> 16.1 us  [grad_call(): pl.pallas_call(grad_kernel, grid=(D // block,), out_shape=jax.ShapeDtypeS...]
    pallas_call x2, Pallas kernels: 104 us -> 112 us  [the longest x1 64.3 us: prologue(): pl.pallas_call(prologue_kernel, out_shape=(sds((G, D), bf16), sds((G, D),...]
    pallas_call x1, Pallas kernels: 58.4 us -> 64.9 us  [close_call(): pl.pallas_call(close_kernel, out_shape=(sds((T, D), f32), sds((T, D), bf1...]
  transfers between devices with their start and end apart: 2 -> 2, of which waited for: 0 -> 0; matrix products, arithmetic and copies ran while one was open for 3% -> 5% of each run, Pallas kernels for 54% -> 56%
where the time goes in v2:
time: 373 us; the launch traced here: 372 us
  Pallas kernels  324 us (87%)
  local copies, waits for them, and re-layouts  25.4 us (7%)
  between operations  14.4 us (4%)
  other arithmetic  8.67 us (2%)
    pallas_call x1, Pallas kernels, close_call(): pl.pallas_call(close_kernel, out_shape=(sds((T, D), f32), sds((T, D), bf1...  64.9 us
    pallas_call x1, Pallas kernels, prologue(): pl.pallas_call(prologue_kernel, out_shape=(sds((G, D), bf16), sds((G, D),...  64.3 us
    pallas_call x1, Pallas kernels, turn_call(): pl.pallas_call(turn_kernel, out_shape=(sds((T, D), f32), sds((1, D), f32)...  49.9 us
    pallas_call x1, Pallas kernels, middle_call(): pl.pallas_call(middle_kernel, out_shape=(sds((T, D), f32), sds((G, D), bf...  47.9 us
    pallas_call x1, Pallas kernels, feed_call(): pl.pallas_call(feed_kernel, grid=(STEPS,), out_shape=(sds((G, D), bf16),...  26 us
    pallas_call x1, Pallas kernels, mix_call(): pl.pallas_call(mix_kernel, grid=(STEPS,), out_shape=(sds((G, D), bf16), *...  23.2 us
    pallas_call x1, Pallas kernels, unmix_call(): pl.pallas_call(unmix_kernel, grid=(STEPS,), out_shape=(sds((G, 2 * WP), b...  21 us
    pallas_call x1, Pallas kernels, grad_call(): pl.pallas_call(grad_kernel, grid=(D // block,), out_shape=jax.ShapeDtypeS...  16.1 us
  transfers between devices with their start and end apart: 2, of which 0 were waited for; matrix products, arithmetic and copies ran while one was open for 5% of the time, Pallas kernels for 56%

profile of v2, /device:TPU:1, one launch (start us, length us, event | category | flops | bytes accessed | tf_op | source)
XLA Modules:
  0.0 372.4 jit_solution(12429146753260549522)
XLA Ops:
  8.1 0.8 copy.59
  10.3 0.8 reshape.189
  11.7 1.2 reshape.185
  13.3 1.0 reshape.186.mix
  14.7 1.4 reshape.188.feed
  16.8 64.3 %prologue.1 = (bf16[1024,2048]{1,0:T(8,128)(2,1)}, bf16[1024,2048]{1,0:T(8,128)(2,1)}, bf16[16,8,16,1152]{3,2,1,0:T(8,128)(2,1)}, bf16[8,16,2304]{2,1,0:T(8,128)...) custom-call(bf16[128,2048]{1,0:T(8,128)(2,1)} %tok.5, ...), custom_call_target="tpu_custom_call" | custom-call | flops 1000 | bytes 104857600 | tf_op jit(solution)/shard_map/prologue/pallas_call | solution.py:454
  81.3 0.7 slice_convert_fusion.2
  82.5 0.8 fusion.7
  83.7 0.9 copy.74
  84.8 0.9 slice_convert_fusion
  87.7 0.8 convert_element_type.105.meta
  88.7 0.9 pad_add_fusion.gates
  90.3 23.2 %mix.1 = (bf16[1024,2048]{1,0:T(8,128)(2,1)}, f32[1024,384]{1,0:T(8,128)}, f32[1024,384]{1,0:T(8,128)}, f32[1024,384]{1,0:T(8,128)}, f32[1024,384]{1,0:T(8,128)}...) custom-call(bf16[1024,2048]{1,0:T(8,128)(2,1)} %get-tuple-element.43.tok, ...), custom_call_target="tpu_custom_call" | custom-call | flops 4831838208 | bytes 31457280 | tf_op jit(solution)/shard_map/mix/pallas_call | solution.py:975
  113.5 47.9 %middle.1 = (f32[128,2048]{1,0:T(8,128)}, bf16[1024,2048]{1,0:T(8,128)(2,1)}) custom-call(bf16[1024,2048]{1,0:T(8,128)(2,1)} %get-tuple-element.49.part, bf16[128,2048]{1,0:T(8,128)(2,1)} %tok.5, f32[1,2048]{1,0:T(1,128)} %squeeze.17.gain), custom_call_target="tpu_custom_call" | custom-call | flops 1000 | bytes 104857600 | tf_op jit(solution)/shard_map/middle/pallas_call | solution.py:510
  161.4 26.0 %feed.1 = (bf16[1024,2048]{1,0:T(8,128)(2,1)}, bf16[1024,2048]{1,0:T(8,128)(2,1)}, bf16[1024,768]{1,0:T(8,128)(2,1)}, bf16[1024,1536]{1,0:T(8,128)(2,1)}) custom-call(bf16[1024,2048]{1,0:T(8,128)(2,1)} %get-tuple-element.50.n2.left, bf16[1024,2048]{1,0:T(8,128)(2,1)} %get-tuple-element.51.cot.left_two, bf16[2048,2304]{1,0:T(8,128)(2,1)} %all-gather.2.cloned.1.call-done.w), custom_call_target="tpu_custom_call" | custom-call | flops 19327352832 | bytes 31457280 | tf_op jit(solution)/shard_map/feed/pallas_call | solution.py:1103
  187.4 16.1 %feedgrad.1 = bf16[2048,2304]{1,0:T(8,128)(2,1)} custom-call(bf16[1024,2048]{1,0:T(8,128)(2,1)} %get-tuple-element.50.n2.left, bf16[1024,1536]{1,0:T(8,128)(2,1)} %get-tuple-element.77.right, bf16[1024,2048]{1,0:T(8,128)(2,1)} %get-tuple-element.51.cot.left_two, bf16[1024,768]{1,0:T(8,128)(2,1)} %get-tuple-element.78.right_two), custom_call_target="tpu_custom_call" | custom-call | flops 9663676416 | bytes 20971520 | tf_op jit(solution)/shard_map/feedgrad/pallas_call | solution.py:1124
  203.6 49.9 %turn.1 = (f32[128,2048]{1,0:T(8,128)}, f32[1,2048]{1,0:T(1,128)}, bf16[1024,2048]{1,0:T(8,128)(2,1)}) custom-call(bf16[1024,2048]{1,0:T(8,128)(2,1)} %get-tuple-element.53.part, f32[128,2048]{1,0:T(8,128)} %get-tuple-element.54.middle, bf16[128,2048]{1,0:T(8,128)(2,1)} %cot.3, f32[1,2048]{1,0:T(1,128)} %squeeze.17.gain), custom_call_target="tpu_custom_call" | custom-call | flops 1000 | bytes 104857600 | tf_op jit(solution)/shard_map/turn/pallas_call | solution.py:562
  253.4 21.0 %unmix.1 = (bf16[1024,768]{1,0:T(8,128)(2,1)}, bf16[1024,2048]{1,0:T(8,128)(2,1)}, f32[2,384,384]{2,1,0:T(8,128)}, f32[8,384]{1,0:T(8,128)}) custom-call(bf16[1024,2048]{1,0:T(8,128)(2,1)} %get-tuple-element.55.adj_out.adj_in, bf16[2048,1152]{1,0:T(8,128)(2,1)} %bitcast.76, bf16[2,384,384]{2,1,0:T(8,128)(2,1)} %pad_add_fusion.gates, ...), custom_call_target="tpu_custom_call" | custom-call | flops 4831838208 | bytes 31457280 | tf_op jit(solution)/shard_map/unmix/pallas_call | solution.py:1071
  274.4 0.7 fusion.2
  275.4 1.3 convert.35
  277.4 0.8 pad_maximum_fusion.1.eg
  278.1 64.9 %close.1 = (f32[128,2048]{1,0:T(8,128)}, bf16[128,2048]{1,0:T(8,128)(2,1)}, bf16[8,16,1152]{2,1,0:T(8,128)(2,1)}, f32[4,16,128]{2,1,0:T(8,128)}, f32[16,128]{1,0:T(8,128)}, /*index=5*/f32[8,128]{1,0:T(8,128)}) custom-call(bf16[1024,2048]{1,0:T(8,128)(2,1)} %get-tuple-element.62.part, bf16[1024,2048]{1,0:T(8,128)(2,1)} %get-tuple-element.63.feed_part, ...), custom_call_target="tpu_custom_call" | custom-call | flops 1000 | bytes 104857600 | tf_op jit(solution)/shard_map/close/pallas_call | solution.py:797
  343.0 0.8 slice.110
  344.4 0.8 slice.97
  345.9 1.0 reshape.202
  347.4 0.9 reshape.208
  348.4 1.3 dynamic-slice_bitcast_fusion
  349.7 10.4 %swap.1 = bf16[8,16,2304]{2,1,0:T(8,128)(2,1)} custom-call(bf16[8,16,2304]{2,1,0:T(8,128)(2,1)} %bitcast.85), custom_call_target="tpu_custom_call" | custom-call | flops 1000 | bytes 1048576 | tf_op jit(solution)/shard_map/swap/pallas_call | solution.py:848
  360.1 1.6 reshape.211
  362.4 1.4 copy.77
  363.8 0.8 copy.84
  364.6 1.0 copy.85
  (78 shorter events, 11.8 us)
Async XLA Ops:
  7.2 7.1 %copy-start.1 = (bf16[16,18432]{1,0:T(8,128)(2,1)S(1)}, bf16[16,18432]{1,0:T(8,128)(2,1)}, u32[]{:S(2)}) copy-start(bf16[16,18432]{1,0:T(8,128)(2,1)} %param.14) | copy-start | bytes 1769476
  7.2 154.2 %all-gather.2.cloned.1.call-start = ((), (), s32[]{:S(2)}) async-start(), calls=%async_computation.1 | async-start | bytes 10027008 | tf_op jit(solution)/shard_map/all_gather | solution.py:1154
  81.1 6.0 %copy-start.3 = (bf16[16,16,512]{2,1,0:T(8,128)(2,1)S(1)}, bf16[16,16,512]{2,1,0:T(8,128)(2,1)}, u32[]{:S(2)}) copy-start(bf16[16,16,512]{2,1,0:T(8,128)(2,1)} %get-tuple-element.45) | copy-start | bytes 786436
  81.1 268.6 %reduce-scatter.2.cloned.1.call-start = ((), (), s32[]{:S(2)}) async-start(), calls=%async_computation.2 | async-start | bytes 10027008 | tf_op jit(solution)/shard_map/reduce_scatter | solution.py:1177
  362.4 1.4 copy-start.2
  362.4 2.2 copy-start
Sparse Core Ops, SparseCore 0:
  81.2 72.4 all-gather.1
  203.7 84.7 reduce-scatter.1

commit v3 on v2

v3 whole, which is shorter than its diff:
```python
import functools

import jax
import jax.numpy as jnp
from jax import lax
from jax.experimental import pallas as pl
from jax.experimental.pallas import tpu as pltpu
from jax.sharding import PartitionSpec as P

D = 2048
W = 2560
FF = 6144
CONV = 4
BW = 160
SEQ = 8
DP = 16
T = 128
G = 1024
WL = W // SEQ
WP = 384
MW = 3 * WP
FL = FF // SEQ
FW = 3 * FL
HALF = T // 2
MINOR = 192

epsilon = 1e-06
rate_scale = 8.0
f32 = jnp.float32
bf16 = jnp.bfloat16
MESH = pl.DeviceIdType.MESH
ANY = pl.ANY
VMEM = pltpu.VMEM
DMA = pltpu.SemaphoreType.DMA


class Place:
    def __init__(self):
        self.dp = lax.axis_index("dp")
        self.sq = lax.axis_index("seq")
        self.x, self.y = self.dp // 4, self.dp % 4
        self.z, self.c = self.sq // 2, self.sq % 2

    def chip(self, k):
        return (self.z + k) % 4

    def slot(self, k, c):
        return 2 * self.chip(k) + c

    def z_peer(self, k):
        return (self.dp, 2 * self.chip(k) + self.c)

    def sibling(self):
        return (self.dp, 2 * self.z + 1 - self.c)

    def x_dp(self, k):
        return (self.x + k) % 4 * 4 + self.y

    def y_dp(self, k):
        return self.x * 4 + (self.y + k) % 4

    def dp_peer(self, dp):
        return (dp, self.sq)

    def seq_peer(self, k):
        return (self.dp, (self.sq + k) % SEQ)


def remote(src, dst, send, recv, device):
    return pltpu.make_async_remote_copy(
        src_ref=src, dst_ref=dst, send_sem=send, recv_sem=recv, device_id=device, device_id_type=MESH
    )


def greet(peers):
    barrier = pltpu.get_barrier_semaphore()
    for device in peers:
        pl.semaphore_signal(barrier, inc=1, device_id=device, device_id_type=MESH)
    return barrier, len(peers)


def z_peers(me):
    return [me.z_peer(1), me.z_peer(3), me.sibling()]


def ring_peers(me):
    return [me.dp_peer(me.x_dp(1)), me.dp_peer(me.x_dp(3)), me.dp_peer(me.y_dp(1)), me.dp_peer(me.y_dp(3))]


def dp_peers(me):
    return [me.dp_peer((me.dp + k) % DP) for k in range(1, DP)]


def seq_peers(me):
    return [me.seq_peer(k) for k in range(1, SEQ)]


class Gather:
    @staticmethod
    def scratch(n):
        return [VMEM((G, n), bf16), DMA((10,)), DMA((10,)), DMA((SEQ,))]

    def __init__(self, me, own, out, full, send, recv, keep):
        self.me, self.own, self.out, self.full = me, own, out, full
        self.send, self.recv, self.keep = send, recv, keep
        self.sent, self.kept = [], []

    def block(self, k, c, half=None):
        base = self.me.slot(k, c) * T
        if half is None:
            return self.full.at[pl.ds(pl.multiple_of(base, T), T)]
        return self.full.at[pl.ds(pl.multiple_of(base + half * HALF, HALF), HALF)]

    def push(self, n, src, dst, device):
        copy = remote(src, dst, self.send.at[n], self.recv.at[n], device)
        copy.start()
        self.sent.append(copy)

    def arrived(self, n, dst):
        remote(dst, dst, self.send.at[n], self.recv.at[n], self.me.sibling()).wait_recv()

    def store(self, k, c):
        if self.out is None:
            return
        there = self.out.at[pl.ds(pl.multiple_of(self.me.slot(k, c) * T, T), T)]
        copy = pltpu.make_async_copy(self.block(k, c), there, self.keep.at[len(self.kept)])
        copy.start()
        self.kept.append(copy)

    def start(self):
        me = self.me
        right, left = me.z_peer(1), me.z_peer(3)
        mine = self.block(0, me.c)
        a, b = self.block(0, me.c, 0), self.block(0, me.c, 1)
        self.push(0, a, a, right)
        self.push(1, b, b, left)
        self.push(2, b, b, right)
        self.push(3, a, a, left)
        self.push(4, mine, mine, me.sibling())
        self.store(0, me.c)

    def forward(self):
        me = self.me
        right, left = me.z_peer(1), me.z_peer(3)
        a, b = self.block(3, me.c, 0), self.block(1, me.c, 1)
        self.arrived(0, a)
        self.push(5, a, a, right)
        self.arrived(1, b)
        self.push(6, b, b, left)

    def hand_over(self, n, k):
        whole = self.block(k, self.me.c)
        self.push(n, whole, whole, self.me.sibling())
        self.store(k, self.me.c)

    def across_left(self):
        self.arrived(2, self.block(3, self.me.c, 1))
        self.hand_over(7, 3)

    def across_right(self):
        self.arrived(3, self.block(1, self.me.c, 0))
        self.hand_over(8, 1)

    def across_far(self):
        self.arrived(5, self.block(2, self.me.c, 0))
        self.arrived(6, self.block(2, self.me.c, 1))
        self.hand_over(9, 2)

    def across(self):
        self.across_left()
        self.across_right()
        self.across_far()

    def taken(self, n, k):
        self.arrived(n, self.block(k, 1 - self.me.c))
        self.store(k, 1 - self.me.c)

    def own_pair(self):
        self.taken(4, 0)

    def left_pair(self):
        self.taken(7, 3)

    def right_pair(self):
        self.taken(8, 1)

    def far_pair(self):
        self.taken(9, 2)

    def drain(self):
        for copy in self.sent:
            copy.wait_send()
        for copy in self.kept:
            copy.wait()

    def finish(self):
        self.own_pair()
        self.left_pair()
        self.right_pair()
        self.far_pair()
        self.drain()


class Spread:
    sems = 40

    def __init__(self, me, full, rows, send, recv):
        self.me, self.full, self.rows, self.send, self.recv = me, full, rows, send, recv

    def at(self, h, i, j):
        me = self.me
        dx, dy = (i, j) if h == 0 else (j, i)
        return (me.x + dx + 4) % 4 * 4 + (me.y + dy + 4) % 4

    def block(self, h, i, j, q=None):
        half = self.rows // 2
        base = self.at(h, i, j) * self.rows + h * half
        if q is None:
            return self.full.at[pl.ds(pl.multiple_of(base, 16), half)]
        return self.full.at[pl.ds(pl.multiple_of(base + q * (half // 2), 16), half // 2)]

    def push(self, h, n, block, i, j):
        n = 20 * h + n
        remote(block, block, self.send.at[n], self.recv.at[n], self.me.dp_peer(self.at(h, i, j))).start()

    def arrived(self, h, n, block):
        n = 20 * h + n
        remote(block, block, self.send.at[n], self.recv.at[n], self.me.sibling()).wait_recv()

    def second(self, t, i):
        for h in range(2):
            block = self.block(h, i, 0)
            self.push(h, 4 + 4 * t, block, 0, 1)
            self.push(h, 5 + 4 * t, block, 0, -1)

    def start(self):
        for h in range(2):
            block = self.block(h, 0, 0)
            self.push(h, 0, block, 1, 0)
            self.push(h, 1, block, -1, 0)
        self.second(0, 0)

    def turn(self):
        for h in range(2):
            self.arrived(h, 0, self.block(h, -1, 0))
            self.push(h, 2, self.block(h, -1, 0, 0), 1, 0)
            self.arrived(h, 1, self.block(h, 1, 0))
            self.push(h, 3, self.block(h, 1, 0, 1), -1, 0)
        self.second(1, -1)
        self.second(2, 1)

    def far(self):
        for h in range(2):
            self.arrived(h, 2, self.block(h, 2, 0, 0))
            self.arrived(h, 3, self.block(h, 2, 0, 1))
        self.second(3, 2)

    def hand_on(self, t):
        i = (0, -1, 1, 2)[t]
        for h in range(2):
            self.arrived(h, 4 + 4 * t, self.block(h, i, -1))
            self.push(h, 6 + 4 * t, self.block(h, i, -1, 0), 0, 1)
            self.arrived(h, 5 + 4 * t, self.block(h, i, 1))
            self.push(h, 7 + 4 * t, self.block(h, i, 1, 1), 0, -1)

    def finish(self):
        for t, i in enumerate((0, -1, 1, 2)):
            for h in range(2):
                self.arrived(h, 6 + 4 * t, self.block(h, i, 2, 0))
                self.arrived(h, 7 + 4 * t, self.block(h, i, 2, 1))

    def drain(self):
        for h in range(2):
            for n in range(20):
                handed = n in (2, 3) or (n >= 4 and n % 4 >= 2)
                block = self.block(h, 0, 0, 0 if handed else None)
                n = 20 * h + n
                remote(block, block, self.send.at[n], self.recv.at[n], self.me.sibling()).wait_send()


def add_rows(out, at, terms, rows, step=32):
    def body(i, carry):
        here = pl.ds(pl.multiple_of(i * step, step), step)
        total = terms[0](here)
        for term in terms[1:]:
            total = total + term(here)
        there = pl.ds(pl.multiple_of(at + i * step, step), step)
        out[there] = total.astype(out.dtype)
        return carry

    lax.fori_loop(0, rows // step, body, 0)


def reads(ref, start=0):
    def term(here):
        return ref[pl.ds(pl.multiple_of(here.start + start, 16), here.size)].astype(f32)

    return term


class Scatter:
    sems = 10

    @staticmethod
    def scratch(n):
        return [
            VMEM((4, T, n), bf16),
            VMEM((4, T, n), bf16),
            VMEM((2, HALF, n), bf16),
            VMEM((2, HALF, n), bf16),
            VMEM((4, HALF, n), bf16),
            DMA((10,)),
            DMA((10,)),
        ]

    def __init__(self, me, part, other, pair, through, passed, final, send, recv):
        self.me, self.part = me, part
        self.other, self.pair, self.through, self.passed, self.final = other, pair, through, passed, final
        self.send, self.recv = send, recv
        self.sent = []

    def piece(self, k, c):
        return self.part.at[pl.ds(pl.multiple_of(self.me.slot(k, c) * T, T), T)]

    def push(self, n, src, dst, device):
        copy = remote(src, dst, self.send.at[n], self.recv.at[n], device)
        copy.start()
        self.sent.append(copy)

    def arrived(self, n, dst):
        remote(dst, dst, self.send.at[n], self.recv.at[n], self.me.sibling()).wait_recv()

    def start(self):
        me = self.me
        for k in (2, 1, 3, 0):
            self.push(k, self.piece(k, 1 - me.c), self.other.at[k], me.sibling())

    def join(self):
        me = self.me
        a, b = pl.ds(0, HALF), pl.ds(HALF, HALF)
        right, left = me.z_peer(1), me.z_peer(3)
        for k in (2, 1, 3, 0):
            self.arrived(k, self.other.at[k])
            add_rows(
                self.pair.at[k], 0, [reads(self.piece(k, me.c)), reads(self.other.at[k])], T
            )
            if k == 2:
                self.push(4, self.pair.at[2, a], self.through.at[0], right)
                self.push(5, self.pair.at[2, b], self.through.at[1], left)
            if k == 1:
                self.push(6, self.pair.at[1, b], self.final.at[0], right)
            if k == 3:
                self.push(7, self.pair.at[3, a], self.final.at[1], left)

    def relay(self):
        me = self.me
        right, left = me.z_peer(1), me.z_peer(3)
        self.arrived(4, self.through.at[0])
        add_rows(self.passed.at[0], 0, [reads(self.through.at[0]), reads(self.pair.at[1])], HALF)
        self.push(8, self.passed.at[0], self.final.at[2], right)
        self.arrived(5, self.through.at[1])
        add_rows(self.passed.at[1], 0, [reads(self.through.at[1]), reads(self.pair.at[3], HALF)], HALF)
        self.push(9, self.passed.at[1], self.final.at[3], left)

    def finish(self, out, extra=None):
        for n, k in ((6, 0), (7, 1), (8, 2), (9, 3)):
            self.arrived(n, self.final.at[k])
        more = [] if extra is None else [reads(extra)]
        add_rows(
            out, 0, [reads(self.pair.at[0]), reads(self.final.at[1]), reads(self.final.at[2])] + more, HALF
        )
        more = [] if extra is None else [reads(extra, HALF)]
        add_rows(
            out,
            HALF,
            [reads(self.pair.at[0], HALF), reads(self.final.at[0]), reads(self.final.at[3])] + more,
            HALF,
        )
        for copy in self.sent:
            copy.wait_send()


def norm_rows(value, gain):
    return value * lax.rsqrt(jnp.mean(value * value, axis=-1, keepdims=True) + epsilon) * gain


def norm_pull(value, gain, incoming):
    r = lax.rsqrt(jnp.mean(value * value, axis=-1, keepdims=True) + epsilon)
    scaled = incoming * gain
    inner = jnp.mean(value * scaled, axis=-1, keepdims=True)
    normed = value * r
    return r * (scaled - normed * (inner * r)), incoming * normed


def turn_kernel(part, middle, cot, gain, adj_middle, gain_grad, adj_all, adj, *rest):
    scatter, gathering = rest[:7], rest[7:]
    me = Place()
    mine = pl.multiple_of(me.sq * T, T)
    own = gathering[0]
    barrier, count = greet(z_peers(me))
    pl.semaphore_wait(barrier, count)
    total = Scatter(me, part, *scatter)
    total.start()
    total.join()
    total.relay()
    total.finish(adj)

    def body(i, carry):
        here = pl.ds(pl.multiple_of(i * 16, 16), 16)
        pulled, terms = norm_pull(middle[here], gain[...], adj[here])
        value = cot[here].astype(f32) + pulled
        adj_middle[here] = value
        own[pl.ds(pl.multiple_of(mine + i * 16, 16), 16)] = value.astype(bf16)
        return carry + jnp.sum(terms, axis=0, keepdims=True)

    gain_grad[...] = lax.fori_loop(0, T // 16, body, jnp.zeros((1, D), f32))
    gather = Gather(me, own, adj_all, *gathering)
    gather.start()
    gather.forward()
    gather.across()
    gather.finish()


def turn_call(part, middle, cot, gain):
    sds = jax.ShapeDtypeStruct
    hbm, vmem = pl.BlockSpec(memory_space=ANY), pl.BlockSpec(memory_space=VMEM)
    return pl.pallas_call(
        turn_kernel,
        out_shape=(sds((T, D), f32), sds((1, D), f32), sds((G, D), bf16)),
        in_specs=[vmem] * 4,
        out_specs=[vmem, vmem, hbm],
        scratch_shapes=[VMEM((T, D), f32)] + Scatter.scratch(D) + Gather.scratch(D),
        compiler_params=pltpu.CompilerParams(collective_id=3, has_side_effects=True, vmem_limit_bytes=62 << 20),
        cost_estimate=pl.CostEstimate(flops=1000, bytes_accessed=100 << 20, transcendentals=0),
        name="turn",
    )(part, middle, cot, gain)


def close_kernel(
    part, feed_part, normed_in, both_in, adj_in, mixed_in, eg, sums, tok, adj_middle, middle, gain, gain_two,
    in_grad, act, mix_out, gate_out, chan_out, gain_out,
    normed, both, adj_out, mixed, mg, adj, r1, s1, r2, last, e_in, sums_in, gate_sum, chan_sum, gp, gp_in, gain_sum, gain_in, *rest,
):
    one, two = rest[:7], rest[7:14]
    m1s, m1r, m2s, m2r, m3s, m3r, es, er, us, ur, gs, gr, hs, hr, qs, qr, ls, ws = rest[14:]
    me = Place()
    loads = [
        pltpu.make_async_copy(src, dst, ws.at[n])
        for n, (src, dst) in enumerate(
            ((normed_in, normed), (both_in, both), (adj_in, adj_out), (mixed_in, mixed))
        )
    ]
    for copy in loads:
        copy.start()
    quarter, at = me.dp // 8, me.dp % 8
    gate_to = (8 * quarter + me.sq, at)
    gate_self = me.sq == at
    chan_from = (8 * (me.dp % 2) + me.sq, me.dp // 2)
    chan_to = (2 * me.sq + me.dp // 8, me.dp % 8)
    chan_self = jnp.logical_and(chan_from[0] == me.dp, chan_from[1] == me.sq)
    barrier, count = greet(seq_peers(me) + dp_peers(me))

    @pl.when(jnp.logical_not(gate_self))
    def _():
        pl.semaphore_signal(barrier, inc=1, device_id=gate_to, device_id_type=MESH)

    @pl.when(jnp.logical_not(chan_self))
    def _():
        pl.semaphore_signal(barrier, inc=1, device_id=chan_from, device_id_type=MESH)

    pl.semaphore_wait(barrier, count + jnp.where(gate_self, 0, 1) + jnp.where(chan_self, 0, 1))

    sent = []

    def push(src, dst, send, recv, device):
        sent.append(remote(src, dst, send, recv, device))
        sent[-1].start()

    def arrived(dst, send, recv):
        remote(dst, dst, send, recv, me.sibling()).wait_recv()

    lo, hi = pl.ds(0, 4), pl.ds(4, 4)
    inner = Scatter(me, part, *one)
    outer = Scatter(me, feed_part, *two)
    inner.start()
    for k in range(1, DP):
        to = (me.dp + k) % DP
        push(eg.at[to], e_in.at[k], es.at[k], er.at[k], me.dp_peer(to))
        push(sums, sums_in.at[k], us.at[k], ur.at[k], me.dp_peer(to))
    inner.join()
    for copy in loads:
        copy.wait()

    def tile(i, carry):
        here = pl.ds(pl.multiple_of(i * 256, 256), 256)
        left = tn(normed[:, here], both[...]).astype(bf16)
        right = tn(adj_out[:, here], mixed[...]).astype(bf16)
        for h in range(2):
            for n in range(SEQ):
                rows = slice(h * T + n * 16, h * T + (n + 1) * 16)
                mg[i // 2, i % 2 * 2 + h, n, :, : 2 * WP] = left[rows]
                mg[i // 2, i % 2 * 2 + h, n, :, 2 * WP :] = right[rows]
        return carry

    lax.fori_loop(0, 8, tile, 0)
    for k in (2, 1, 3):
        push(mg.at[:, (me.y + k) % 4, lo], r1.at[0, k - 1], m1s.at[k], m1r.at[k], me.dp_peer(me.y_dp(k)))
        push(mg.at[(me.x + k) % 4, :, hi], r1.at[1, k - 1], m1s.at[4 + k], m1r.at[4 + k], me.dp_peer(me.x_dp(k)))
    outer.start()
    inner.relay()
    outer.join()
    inner.finish(adj)

    def pull(i, carry):
        here = pl.ds(pl.multiple_of(i * 16, 16), 16)
        pulled, terms = norm_pull(tok[here].astype(f32), gain[...], adj[here])
        in_grad[here] = adj_middle[here] + pulled
        return carry + jnp.sum(terms, axis=0, keepdims=True)

    gain_one = lax.fori_loop(0, T // 16, pull, jnp.zeros((1, D), f32))
    gp[...] = jnp.zeros(gp.shape, f32)
    for k in range(DP):
        gp[k, 0:1] = gain_one[:, k * 128 : (k + 1) * 128]
        gp[k, 1:2] = gain_two[:, k * 128 : (k + 1) * 128]
    for k in range(1, DP):
        to = (me.dp + k) % DP
        push(gp.at[to], gp_in.at[k], gs.at[k], gr.at[k], me.dp_peer(to))
    outer.relay()

    for k in range(1, DP):
        arrived(e_in.at[k], es.at[k], er.at[k])
        arrived(sums_in.at[k], us.at[k], ur.at[k])

    def add_gates(i, carry):
        here = pl.ds(pl.multiple_of(i * 16, 16), 16)

        def step(k, total):
            return total + e_in[k, here].astype(f32)

        gate_sum[here] = lax.fori_loop(1, DP, step, eg[me.dp, here].astype(f32))
        return carry

    lax.fori_loop(0, 3, add_gates, 0)

    def add_sums(k, total):
        return total + sums_in[k]

    chan_sum[...] = lax.fori_loop(1, DP, add_sums, sums[...])
    gate_copy = remote(gate_sum, gate_out, hs.at[0], hr.at[0], gate_to)
    chan_copy = remote(chan_sum, chan_out, hs.at[1], hr.at[1], chan_to)
    gate_local = pltpu.make_async_copy(gate_sum, gate_out, ls.at[0])
    chan_local = pltpu.make_async_copy(chan_sum, chan_out, ls.at[1])

    @pl.when(jnp.logical_not(gate_self))
    def _():
        gate_copy.start()

    @pl.when(gate_self)
    def _():
        gate_local.start()

    @pl.when(jnp.logical_not(chan_self))
    def _():
        chan_copy.start()

    @pl.when(chan_self)
    def _():
        chan_local.start()

    for k in (1, 3, 2):
        arrived(r1.at[0, k - 1], m1s.at[k], m1r.at[k])
        arrived(r1.at[1, k - 1], m1s.at[4 + k], m1r.at[4 + k])
    for j in (2, 1, 3, 0):

        def first(i, carry, j=j):
            xx, yy = (me.x + j) % 4, (me.y + j) % 4
            total = mg[xx, me.y, i].astype(f32)
            for k in range(3):
                total = total + r1[0, k, xx, i].astype(f32)
            s1[0, j, i] = total.astype(bf16)
            total = mg[me.x, yy, 4 + i].astype(f32)
            for k in range(3):
                total = total + r1[1, k, yy, i].astype(f32)
            s1[1, j, i] = total.astype(bf16)
            return carry

        lax.fori_loop(0, 4, first, 0)
        if j:
            push(s1.at[0, j], r2.at[0, j - 1], m2s.at[j], m2r.at[j], me.dp_peer(me.x_dp(j)))
            push(s1.at[1, j], r2.at[1, j - 1], m2s.at[4 + j], m2r.at[4 + j], me.dp_peer(me.y_dp(j)))

    for k in range(1, DP):
        arrived(gp_in.at[k], gs.at[k], gr.at[k])

    def gains(k, total):
        return total + gp_in[k]

    gain_sum[...] = lax.fori_loop(1, DP, gains, gp[me.dp])
    for k in range(1, SEQ):
        push(gain_sum, gain_in.at[k], qs.at[k], qr.at[k], me.seq_peer(k))

    outer.finish(adj, middle)

    def lower(i, carry):
        here = pl.ds(pl.multiple_of(i * 16, 16), 16)
        act[here] = adj[here].astype(bf16)
        return carry

    lax.fori_loop(0, T // 16, lower, 0)

    for j in (1, 3, 2):
        arrived(r2.at[0, j - 1], m2s.at[j], m2r.at[j])
        arrived(r2.at[1, j - 1], m2s.at[4 + j], m2r.at[4 + j])

    def second(i, carry):
        for h in range(2):
            total = s1[h, 0, i].astype(f32)
            for k in range(3):
                total = total + r2[h, k, i].astype(f32)
            last[4 * h + i] = total.astype(bf16)
        return carry

    lax.fori_loop(0, 4, second, 0)
    keep = pltpu.make_async_copy(last.at[me.sq], mix_out.at[me.sq], ls.at[2])
    keep.start()
    for k in (4, 3, 5, 2, 6, 1, 7):
        to = (me.sq + k) % SEQ
        push(last.at[to], mix_out.at[me.sq], m3s.at[k], m3r.at[k], me.seq_peer(k))
    for k in range(1, SEQ):
        arrived(gain_in.at[k], qs.at[k], qr.at[k])
    total = gain_sum[...]
    for k in range(1, SEQ):
        total = total + gain_in[k]
    gain_out[...] = total

    @pl.when(jnp.logical_not(gate_self))
    def _():
        gate_copy.wait()

    @pl.when(gate_self)
    def _():
        gate_local.wait()

    @pl.when(jnp.logical_not(chan_self))
    def _():
        chan_copy.wait()

    @pl.when(chan_self)
    def _():
        chan_local.wait()

    for k in range(1, SEQ):
        arrived(mix_out.at[(me.sq - k + SEQ) % SEQ], m3s.at[k], m3r.at[k])
    keep.wait()
    for copy in sent:
        copy.wait_send()


def close_call(part, feed_part, normed, both, adj_out, mixed, eg, sums, tok, adj_middle, middle, gain, gain_two):
    sds = jax.ShapeDtypeStruct
    vmem = pl.BlockSpec(memory_space=VMEM)
    return pl.pallas_call(
        close_kernel,
        out_shape=(
            sds((T, D), f32), sds((T, D), bf16), sds((SEQ, 16, MW), bf16),
            sds((48, WP), f32), sds((8, WP), f32), sds((8, 128), f32),
        ),
        in_specs=[vmem] * 2 + [pl.BlockSpec(memory_space=ANY)] * 4 + [vmem] * 7,
        out_specs=[vmem] * 6,
        scratch_shapes=[
            VMEM((G, D), bf16), VMEM((G, 2 * WP), bf16), VMEM((G, D), bf16), VMEM((G, WP), bf16),
            VMEM((4, 4, SEQ, 16, MW), bf16),
            VMEM((T, D), f32),
            VMEM((2, 3, 4, 4, 16, MW), bf16), VMEM((2, 4, 4, 16, MW), bf16), VMEM((2, 3, 4, 16, MW), bf16),
            VMEM((SEQ, 16, MW), bf16), VMEM((DP, 48, WP), bf16), VMEM((DP, 8, WP), f32), VMEM((48, WP), f32),
            VMEM((8, WP), f32), VMEM((DP, 8, 128), f32), VMEM((DP, 8, 128), f32),
            VMEM((8, 128), f32), VMEM((SEQ, 8, 128), f32),
        ]
        + Scatter.scratch(D)
        + Scatter.scratch(D)
        + [
            DMA((8,)), DMA((8,)), DMA((8,)), DMA((8,)), DMA((8,)), DMA((8,)),
            DMA((DP,)), DMA((DP,)), DMA((DP,)), DMA((DP,)), DMA((DP,)), DMA((DP,)), DMA((2,)), DMA((2,)),
            DMA((SEQ,)), DMA((SEQ,)), DMA((3,)), DMA((4,)),
        ],
        compiler_params=pltpu.CompilerParams(collective_id=4, has_side_effects=True, vmem_limit_bytes=62 << 20),
        cost_estimate=pl.CostEstimate(flops=1000, bytes_accessed=100 << 20, transcendentals=0),
        name="close",
    )(part, feed_part, normed, both, adj_out, mixed, eg, sums, tok, adj_middle, middle, gain, gain_two)


def swap_kernel(src, dst, ss, sr, ls):
    me = Place()
    barrier, count = greet(seq_peers(me))
    keep = pltpu.make_async_copy(src.at[me.sq], dst.at[me.sq], ls.at[0])
    keep.start()
    pl.semaphore_wait(barrier, count)
    sent = []
    for k in (4, 3, 5, 2, 6, 1, 7):
        to = (me.sq + k) % SEQ
        sent.append(remote(src.at[to], dst.at[me.sq], ss.at[k], sr.at[k], me.seq_peer(k)))
        sent[-1].start()
    for k in range(1, SEQ):
        source = (me.sq - k + SEQ) % SEQ
        remote(dst.at[source], dst.at[source], ss.at[k], sr.at[k], me.sibling()).wait_recv()
    keep.wait()
    for copy in sent:
        copy.wait_send()


def swap_call(src, number, name):
    hbm = pl.BlockSpec(memory_space=ANY)
    return pl.pallas_call(
        swap_kernel,
        out_shape=jax.ShapeDtypeStruct(src.shape, src.dtype),
        in_specs=[hbm],
        out_specs=hbm,
        scratch_shapes=[DMA((SEQ,)), DMA((SEQ,)), DMA((1,))],
        compiler_params=pltpu.CompilerParams(collective_id=number, has_side_effects=True, vmem_limit_bytes=62 << 20),
        cost_estimate=pl.CostEstimate(flops=1000, bytes_accessed=1 << 20, transcendentals=0),
        name=name,
    )(src)


CHUNK = 256
STEPS = G // CHUNK
contract_last = (((1,), (1,)), ((), ()))
contract_first = (((0,), (0,)), ((), ()))
gelu_c = 0.7978845608028654
gelu_k = 0.044715


def gelu_parts(v):
    square = v * v
    t = jnp.tanh(gelu_c * (v + gelu_k * square * v))
    half = 0.5 * (1.0 + t)
    slope = half + 0.5 * v * (1.0 - t * t) * (gelu_c * (1.0 + 3.0 * gelu_k * square))
    return v * half, slope


def minus_expm1(z):
    series = -z * (1.0 + z * (1 / 2 + z * (1 / 6 + z * (1 / 24 + z * (1 / 120 + z * (1 / 720))))))
    return jnp.where(z > -0.25, series, 1.0 - jnp.exp(z))


def recur(conv, raw_a, raw_x, terms, start):
    recall = jax.nn.sigmoid(raw_a + terms[5:6])
    admit = jax.nn.sigmoid(raw_x + terms[6:7])
    lograte = terms[7:8] * recall
    decay = jnp.exp(lograte) * (1.0 - start)
    root = jnp.sqrt(minus_expm1(2.0 * lograte))
    scale = start + (1.0 - start) * root
    return recall, admit, lograte, decay, root, scale


def nt(left, right):
    return lax.dot_general(left, right, contract_last, preferred_element_type=f32)


def tn(left, right):
    return lax.dot_general(left, right, contract_first, preferred_element_type=f32)


def nn(left, right):
    return jnp.dot(left, right, preferred_element_type=f32)


def rows_spec(width, back=False):
    if back:
        return pl.BlockSpec((CHUNK, width), lambda i: (STEPS - 1 - i, 0))
    return pl.BlockSpec((CHUNK, width), lambda i: (i, 0))


def whole(shape):
    return pl.BlockSpec(shape, lambda i: (0,) * len(shape))


def rows_of(base, size):
    return pl.ds(pl.multiple_of(base, 16), size)


def lanes_of(base, size):
    return pl.ds(pl.multiple_of(base, 128), size)


def windows(lab, base):
    return lab[pl.ds(pl.multiple_of(base, 8), CHUNK + 16)]


def same(window, k):
    here = window[8 : 8 + CHUNK, 0:1]
    there = window[8 - k : 8 - k + CHUNK, 0:1]
    return (here == there).astype(f32)


def forward_kernel(
    tok, cot, mix, feed, small, gates, chan,
    cot_out, mix_out, normed_out, x_out, y_out, conv_out, prior_out, mixed_out,
    hidden_out, gu_out, back_out, ff_out, n2_out, gate_out, term_out, gain_out, lab_out, middle,
    mixw, feedw, part, xs, ys, convs, priors, mixeds, hiddens, gus,
    small_in, minor, gate_f,
    xpad, dec, drv, sts, carry, *rest,
):
    tg, cg, ng, sc = rest[:4], rest[4:8], rest[8:12], rest[12:19]
    ms, mr, fs, fr, ss, sr, ps, pr, qs, qr, es, er, hs, hr, ls, os = rest[19:]
    me = Place()
    quarter, at = me.dp // 8, me.dp % 8
    gate_to = (8 * quarter + me.sq, at)
    gate_self = me.sq == at
    chan_to = (8 * (me.dp % 2) + me.sq, me.dp // 2)
    chan_from = (2 * me.sq + me.dp // 8, me.dp % 8)
    chan_self = jnp.logical_and(chan_to[0] == me.dp, chan_to[1] == me.sq)
    barrier, count = greet(seq_peers(me) + ring_peers(me))

    @pl.when(jnp.logical_not(gate_self))
    def _():
        pl.semaphore_signal(barrier, inc=1, device_id=gate_to, device_id_type=MESH)

    @pl.when(jnp.logical_not(chan_self))
    def _():
        pl.semaphore_signal(barrier, inc=1, device_id=chan_from, device_id_type=MESH)

    tokg, cotg, n2g = tg[0], cg[0], ng[0]
    own_rows = rows_of(me.dp * T + me.sq * 16, 16)

    def feed_columns(p, j):
        return lanes_of(p * FF + j * FL, FL)

    local = [
        pltpu.make_async_copy(tok, tokg.at[rows_of(me.sq * T, T)], ls.at[0]),
        pltpu.make_async_copy(cot, cotg.at[rows_of(me.sq * T, T)], ls.at[1]),
        pltpu.make_async_copy(mix.at[me.sq], mixw.at[own_rows], ls.at[2]),
        pltpu.make_async_copy(small, small_in.at[me.sq], ls.at[3]),
    ] + [
        pltpu.make_async_copy(feed.at[:, feed_columns(p, me.sq)], feedw.at[own_rows, pl.ds(p * FL, FL)], ls.at[4 + p])
        for p in range(3)
    ]
    for copy in local:
        copy.start()

    pl.semaphore_wait(barrier, count + jnp.where(gate_self, 0, 1) + jnp.where(chan_self, 0, 1))

    sent = []

    def push(src, dst, send, recv, device):
        sent.append(remote(src, dst, send, recv, device))
        sent[-1].start()

    def arrived(dst, send, recv):
        remote(dst, dst, send, recv, me.sibling()).wait_recv()

    order = (4, 3, 5, 2, 6, 1, 7)
    for k in order:
        to = (me.sq + k) % SEQ
        push(mix.at[to], mixw.at[own_rows], ms.at[k], mr.at[k], me.seq_peer(k))
        push(small, small_in.at[me.sq], ss.at[k], sr.at[k], me.seq_peer(k))

    def minor_rows(dp, start, size):
        return minor.at[rows_of(dp * MINOR + start, size)]

    gate_copy = remote(gates, minor_rows(gate_to[0], 16, 96), hs.at[0], hr.at[0], gate_to)
    chan_copy = remote(chan, minor_rows(chan_to[0], 112, 48), hs.at[1], hr.at[1], chan_to)
    gate_local = pltpu.make_async_copy(gates, minor_rows(me.dp, 16, 96), ls.at[7])
    chan_local = pltpu.make_async_copy(chan, minor_rows(me.dp, 112, 48), ls.at[8])
    gate_here = remote(gates, minor_rows(me.dp, 16, 96), hs.at[0], hr.at[0], gate_to)
    chan_here = remote(chan, minor_rows(me.dp, 112, 48), hs.at[1], hr.at[1], chan_to)

    @pl.when(jnp.logical_not(gate_self))
    def _():
        gate_copy.start()

    @pl.when(gate_self)
    def _():
        gate_local.start()

    @pl.when(jnp.logical_not(chan_self))
    def _():
        chan_copy.start()

    @pl.when(chan_self)
    def _():
        chan_local.start()

    local[0].wait()
    tokens = Gather(me, None, None, *tg)
    tokens.start()
    for k in order:
        to = (me.sq + k) % SEQ
        for p in range(3):
            push(feed.at[:, feed_columns(p, to)], feedw.at[own_rows, pl.ds(p * FL, FL)],
                 fs.at[p, k], fr.at[p, k], me.seq_peer(k))
    for copy in local[1:]:
        copy.wait()

    def seq_rows(k):
        return rows_of(me.dp * T + (me.sq - k + SEQ) % SEQ * 16, 16)

    for k in range(1, SEQ):
        arrived(mixw.at[seq_rows(k)], ms.at[k], mr.at[k])

    mixes = Spread(me, mixw, T, ps, pr)
    feeds = Spread(me, feedw, T, qs, qr)
    minors = Spread(me, minor, MINOR, es, er)
    mixes.start()

    for k in range(1, SEQ):
        arrived(small_in.at[(me.sq - k + SEQ) % SEQ], ss.at[k], sr.at[k])
    gain = small_in[0, 0:16].astype(f32)
    for k in range(1, SEQ):
        gain = gain + small_in[k, 0:16].astype(f32)
    minor[rows_of(me.dp * MINOR, 16)] = gain.astype(bf16)
    minor[rows_of(me.dp * MINOR + 160, 32)] = jnp.zeros((32, 128), bf16)

    @pl.when(jnp.logical_not(gate_self))
    def _():
        gate_copy.wait_send()
        gate_here.wait_recv()

    @pl.when(gate_self)
    def _():
        gate_local.wait()

    @pl.when(jnp.logical_not(chan_self))
    def _():
        chan_copy.wait_send()
        chan_here.wait_recv()

    @pl.when(chan_self)
    def _():
        chan_local.wait()

    minors.start()
    tokens.forward()
    mixes.turn()
    minors.turn()
    cots = Gather(me, None, cot_out, *cg)
    cots.start()
    mixes.far()
    minors.far()

    lab_out[0:8] = jnp.full((8, 128), -1.0, f32)
    lab_out[G + 8 :] = jnp.full((8, 128), -2.0, f32)
    for k in range(SEQ):
        row = small_in[k, 16:32].astype(f32)[0:1]
        lab_out[8 + k * T : 8 + (k + 1) * T] = jnp.broadcast_to(row, (128, 128)).T

    tokens.across()
    for t in range(3):
        mixes.hand_on(t)
        minors.hand_on(t)
    minors.hand_on(3)
    mixes.hand_on(3)
    for k in range(1, SEQ):
        for p in range(3):
            arrived(feedw.at[seq_rows(k), pl.ds(p * FL, FL)], fs.at[p, k], fr.at[p, k])
    feeds.start()
    tokens.finish()
    minors.finish()
    terms = minor[112:160].astype(f32)
    for k in range(1, DP):
        terms = terms + minor[k * MINOR + 112 : k * MINOR + 160].astype(f32)
    for n in range(3):
        group = terms[16 * n : 16 * n + 16]
        lanes = slice(128 * n, 128 * n + 128)
        lane = lax.broadcasted_iota(jnp.int32, (1, 128), 1) + 128 * n
        term_out[:, lanes] = group
        term_out[7:8, lanes] = jnp.where(lane >= WL, -1.0, group[7:8] + group[9:10])
        term_out[8:9, lanes] = group[8:9] + group[10:11]
    gate_f[...] = jnp.zeros(gate_f.shape, f32)
    for k in range(DP):
        gain_out[:, k * 128 : (k + 1) * 128] = minor[k * MINOR : k * MINOR + 16].astype(f32)[0:8]
        base = k // 8 * WP + k % 8 * 40
        for n in range(2):
            lanes = k % 8 // 4 * 128 + n * 128
            start = k * MINOR + 16 + 48 * n
            gate_f[base : base + 40, lanes : lanes + 128] = minor[start : start + 48].astype(f32)[0:40]
    gate_out[0] = gate_f[:WP].astype(bf16)
    gate_out[1] = gate_f[WP:].astype(bf16)

    def normalise(i, c):
        here = pl.ds(pl.multiple_of(i * 16, 16), 16)
        tokg[here] = norm_rows(tokg[here].astype(f32), gain_out[0:1]).astype(bf16)
        return c

    lax.fori_loop(0, G // 16, normalise, 0)
    writes = [pltpu.make_async_copy(tokg, normed_out, os.at[0])]
    writes[0].start()
    cots.forward()
    cots.across()
    mixes.finish()
    writes.append(pltpu.make_async_copy(mixw, mix_out, os.at[1]))
    writes[1].start()

    xpad[0:8] = jnp.zeros((8, WP), f32)
    carry[...] = jnp.zeros((8, WP), f32)
    row = lax.broadcasted_iota(jnp.int32, (8, WP), 0)

    def mix_chunk(step, c):
        @pl.when(step == 1)
        def _():
            feeds.turn()

        @pl.when(step == 2)
        def _():
            feeds.far()

        @pl.when(step == 3)
        def _():
            feeds.hand_on(0)

        base = step * CHUNK
        rows = rows_of(base, CHUNK)
        both = nn(tokg[rows], mixw[:, : 2 * WP])
        x, y = both[:, :WP], both[:, WP:]
        xs[rows] = x
        ys[rows] = y
        xpad[8:] = x
        terms = term_out[...]
        window = windows(lab_out, base)
        start = 1.0 - same(window, 1)
        conv = terms[4:5] + terms[0:1] * x
        for k in range(1, CONV):
            conv = conv + terms[k : k + 1] * (same(window, k) * xpad[8 - k : 8 - k + CHUNK])
        xpad[0:8] = x[CHUNK - 8 :]
        convs[rows] = conv
        lowered = conv.astype(bf16)
        raw_a, raw_x = nn(lowered, gate_out[0]), nn(lowered, gate_out[1])
        recall, admit, lograte, decay, root, scale = recur(conv, raw_a, raw_x, terms, start)
        dec[...] = decay
        drv[...] = scale * admit * conv

        def scan(i, before):
            here = pl.ds(pl.multiple_of(i * 8, 8), 8)
            a, b = dec[here], drv[here]
            for s in (1, 2, 4):
                b = b + a * jnp.where(row >= s, pltpu.roll(b, s, 0), 0.0)
                a = a * jnp.where(row >= s, pltpu.roll(a, s, 0), 1.0)
            state = b + a * before
            sts[here] = state
            priors[pl.ds(pl.multiple_of(base + i * 8, 8), 8)] = jnp.where(row >= 1, pltpu.roll(state, 1, 0), before)
            return jnp.broadcast_to(state[7:8], (8, WP))

        carry[...] = lax.fori_loop(0, CHUNK // 8, scan, carry[...], unroll=4)
        value, _ = gelu_parts(ys[rows])
        mixed = (value * sts[...]).astype(bf16)
        mixeds[rows] = mixed
        part[rows] = nt(mixed, mixw[:, 2 * WP :]).astype(bf16)
        return c

    lax.fori_loop(0, STEPS, mix_chunk, 0)

    total = Scatter(me, part, *sc)
    total.start()
    for n, (src, dst) in enumerate(((xs, x_out), (ys, y_out), (convs, conv_out), (priors, prior_out), (mixeds, mixed_out))):
        writes.append(pltpu.make_async_copy(src, dst, os.at[2 + n]))
        writes[-1].start()
    total.join()
    feeds.hand_on(1)
    feeds.hand_on(2)
    total.relay()
    feeds.hand_on(3)
    total.finish(middle, tok)

    def second_norm(i, c):
        here = pl.ds(pl.multiple_of(i * 16, 16), 16)
        n2g[rows_of(me.sq * T + i * 16, 16)] = norm_rows(middle[here], gain_out[1:2]).astype(bf16)
        return c

    lax.fori_loop(0, T // 16, second_norm, 0)
    seconds = Gather(me, None, n2_out, *ng)
    seconds.start()
    cots.finish()
    writes[0].wait()
    feeds.finish()

    def feed_chunk(k, n):
        rows = rows_of(me.chip(k) * CHUNK, CHUNK)
        gu = nn(n2g[rows], feedw[:, : 2 * FL])
        gate, up = gu[:, :FL], gu[:, FL:]
        adj_hidden = nn(cotg[rows], feedw[:, 2 * FL :])
        value, slope = gelu_parts(gate)
        hidden = (value * up).astype(bf16)
        hiddens[rows] = hidden
        gus[rows, :FL] = (adj_hidden * up * slope).astype(bf16)
        gus[rows, FL:] = (adj_hidden * value).astype(bf16)
        tokg[rows] = nt(hidden, feedw[:, 2 * FL :]).astype(bf16)
        part[rows] = nt(gus[rows], feedw[:, : 2 * FL]).astype(bf16)

    def feed_store(k, n):
        rows = rows_of(me.chip(k) * CHUNK, CHUNK)
        for m, (src, dst) in enumerate(((hiddens, hidden_out), (gus, gu_out), (tokg, ff_out), (part, back_out))):
            writes.append(pltpu.make_async_copy(src.at[rows], dst.at[rows], os.at[7 + 4 * n + m]))
            writes[-1].start()

    seconds.own_pair()
    feed_chunk(0, 0)
    feed_store(0, 0)
    seconds.forward()
    seconds.across_left()
    seconds.across_right()
    seconds.left_pair()
    feed_chunk(3, 1)
    feed_store(3, 1)
    seconds.across_far()
    seconds.right_pair()
    feed_chunk(1, 2)
    feed_store(1, 2)
    seconds.far_pair()
    feed_chunk(2, 3)
    feed_store(2, 3)
    seconds.drain()
    for copy in writes[1:]:
        copy.wait()
    for copy in sent:
        copy.wait_send()
    mixes.drain()
    minors.drain()
    feeds.drain()


def forward_call(tok, cot, mix, feed, small, gates, chan):
    sds = jax.ShapeDtypeStruct
    hbm, vmem = pl.BlockSpec(memory_space=ANY), pl.BlockSpec(memory_space=VMEM)
    return pl.pallas_call(
        forward_kernel,
        out_shape=(
            sds((G, D), bf16), sds((D, MW), bf16), sds((G, D), bf16),
            sds((G, WP), f32), sds((G, WP), f32), sds((G, WP), f32), sds((G, WP), f32), sds((G, WP), bf16),
            sds((G, FL), bf16), sds((G, 2 * FL), bf16), sds((G, D), bf16), sds((G, D), bf16), sds((G, D), bf16),
            sds((2, WP, WP), bf16), sds((16, WP), f32), sds((8, D), f32), sds((G + 16, 128), f32), sds((T, D), f32),
        ),
        in_specs=[vmem, hbm, hbm, hbm, vmem, vmem, vmem],
        out_specs=[hbm] * 13 + [vmem] * 5,
        scratch_shapes=[
            VMEM((D, MW), bf16), VMEM((D, FW), bf16), VMEM((G, D), bf16),
            VMEM((G, WP), f32), VMEM((G, WP), f32), VMEM((G, WP), f32), VMEM((G, WP), f32), VMEM((G, WP), bf16),
            VMEM((G, FL), bf16), VMEM((G, 2 * FL), bf16),
            VMEM((SEQ, 32, 128), bf16), VMEM((DP * MINOR, 128), bf16), VMEM((2 * WP, WP), f32),
            VMEM((CHUNK + 8, WP), f32), VMEM((CHUNK, WP), f32), VMEM((CHUNK, WP), f32), VMEM((CHUNK, WP), f32),
            VMEM((8, WP), f32),
            *Gather.scratch(D), *Gather.scratch(D), *Gather.scratch(D), *Scatter.scratch(D),
            DMA((SEQ,)), DMA((SEQ,)), DMA((3, SEQ)), DMA((3, SEQ)), DMA((SEQ,)), DMA((SEQ,)),
            DMA((40,)), DMA((40,)), DMA((40,)), DMA((40,)), DMA((40,)), DMA((40,)),
            DMA((2,)), DMA((2,)), DMA((9,)), DMA((23,)),
        ],
        compiler_params=pltpu.CompilerParams(collective_id=1, has_side_effects=True, vmem_limit_bytes=63 << 20),
        cost_estimate=pl.CostEstimate(flops=30 * G * D * WP, bytes_accessed=100 << 20, transcendentals=0),
        name="forward",
    )(tok, cot, mix, feed, small, gates, chan)


def unmix_kernel(
    adj_out, w, gates, terms_ref, lab, x_in, y_in, conv_in, prior_in,
    both, part, gate_out, sums,
    dec, adj, acp, carry, gate_grad,
):
    step = pl.program_id(0)
    window = windows(lab, (STEPS - 1 - step) * CHUNK)

    @pl.when(step == 0)
    def _():
        dec[CHUNK:] = jnp.zeros((8, WP), f32)
        acp[CHUNK:] = jnp.zeros((8, WP), f32)
        carry[...] = jnp.zeros((8, WP), f32)
        gate_grad[...] = jnp.zeros(gate_grad.shape, f32)
        sums[...] = jnp.zeros(sums.shape, f32)

    @pl.when(step > 0)
    def _():
        dec[CHUNK:] = dec[0:8]
        acp[CHUNK:] = acp[0:8]

    terms = terms_ref[...]
    start = 1.0 - same(window, 1)
    conv, prior = conv_in[...], prior_in[...]
    lowered = conv.astype(bf16)
    raw_a, raw_x = nn(lowered, gates[0]), nn(lowered, gates[1])
    recall, admit, lograte, decay, root, scale = recur(conv, raw_a, raw_x, terms, start)
    dec[0:CHUNK] = decay
    states = decay * prior + scale * admit * conv
    adj_mixed = nn(adj_out[...], w[:, 2 * WP :])
    value, slope = gelu_parts(y_in[...])
    adj[...] = adj_mixed * value
    both[:, WP:] = (adj_mixed * states * slope).astype(bf16)
    row = lax.broadcasted_iota(jnp.int32, (8, WP), 0)

    def scan(i, after):
        at = pl.multiple_of((CHUNK // 8 - 1 - i) * 8, 8)
        here = pl.ds(at, 8)
        later = dec[pl.ds(pl.multiple_of(at + 8, 8), 8)]
        a = jnp.where(row < 7, pltpu.roll(dec[here], 7, 0), later[0:1])
        b = adj[here]
        for s in (1, 2, 4):
            b = b + a * jnp.where(row < 8 - s, pltpu.roll(b, 8 - s, 0), 0.0)
            a = a * jnp.where(row < 8 - s, pltpu.roll(a, 8 - s, 0), 1.0)
        value = b + a * after
        adj[here] = value
        return jnp.broadcast_to(value[0:1], (8, WP))

    carry[...] = lax.fori_loop(0, CHUNK // 8, scan, carry[...], unroll=4)
    adjoint = adj[...]
    flow = adjoint * admit * conv
    adj_lograte = adjoint * prior * decay - (1.0 - start) * flow * (jnp.exp(2.0 * lograte) / root)
    adj_ra = adj_lograte * terms[7:8] * (recall * (1.0 - recall))
    adj_rx = flow * scale * (1.0 - admit)

    def total(v):
        return jnp.sum(v, axis=0, keepdims=True)

    sums[5:6] += total(adj_ra)
    sums[6:7] += total(adj_rx)
    sums[7:8] += total(adj_lograte * recall) * terms[8:9]
    low_a, low_x = adj_ra.astype(bf16), adj_rx.astype(bf16)
    adj_conv = adjoint * scale * admit + nt(low_a, gates[0]) + nt(low_x, gates[1])
    gate_grad[0] += tn(lowered, low_a)
    gate_grad[1] += tn(lowered, low_x)
    acp[0:CHUNK] = adj_conv
    x = x_in[...]
    adj_x = terms[0:1] * adj_conv
    sums[4:5] += total(adj_conv)
    sums[0:1] += total(adj_conv * x)
    for k in range(1, CONV):
        moved = same(window, -k) * acp[k : k + CHUNK]
        adj_x = adj_x + terms[k : k + 1] * moved
        sums[k : k + 1] += total(moved * x)
    both[:, :WP] = adj_x.astype(bf16)
    part[...] = nt(both[...], w[:, : 2 * WP]).astype(bf16)

    @pl.when(step == STEPS - 1)
    def _():
        for k in range(DP):
            rows = gate_grad[k // 8, k % 8 * 40 : k % 8 * 40 + 40]
            gate_out[k] = jnp.concatenate([rows, jnp.zeros((8, WP), f32)], 0).astype(bf16)


def unmix_call(adj_out, w, gates, terms, lab, saved):
    sds = jax.ShapeDtypeStruct
    return pl.pallas_call(
        unmix_kernel,
        grid=(STEPS,),
        out_shape=(sds((G, 2 * WP), bf16), sds((G, D), bf16), sds((DP, 48, WP), bf16), sds((8, WP), f32)),
        in_specs=[
            rows_spec(D, True), whole((D, MW)), whole((2, WP, WP)), whole((16, WP)),
            whole((G + 16, 128)),
        ]
        + [rows_spec(WP, True)] * 4,
        out_specs=[rows_spec(2 * WP, True), rows_spec(D, True), whole((DP, 48, WP)), whole((8, WP))],
        scratch_shapes=[
            VMEM((CHUNK + 8, WP), f32), VMEM((CHUNK, WP), f32), VMEM((CHUNK + 8, WP), f32), VMEM((8, WP), f32),
            VMEM((2, WP, WP), f32),
        ],
        compiler_params=pltpu.CompilerParams(vmem_limit_bytes=62 << 20),
        cost_estimate=pl.CostEstimate(flops=2 * G * D * MW, bytes_accessed=30 << 20, transcendentals=0),
        name="unmix",
    )(adj_out, w, gates, terms, lab, *saved)


def grad_kernel(left, right, left_two, right_two, out):
    width = right.shape[1]
    out[:, :width] = tn(left[...], right[...]).astype(bf16)
    out[:, width:] = tn(left_two[...], right_two[...]).astype(bf16)


def grad_call(left, right, left_two, right_two, name):
    width = right.shape[1] + right_two.shape[1]
    block = 256
    return pl.pallas_call(
        grad_kernel,
        grid=(D // block,),
        out_shape=jax.ShapeDtypeStruct((D, width), bf16),
        in_specs=[
            pl.BlockSpec((G, block), lambda i: (0, i)), whole(right.shape),
            pl.BlockSpec((G, block), lambda i: (0, i)), whole(right_two.shape),
        ],
        out_specs=pl.BlockSpec((block, width), lambda i: (i, 0)),
        compiler_params=pltpu.CompilerParams(vmem_limit_bytes=62 << 20),
        cost_estimate=pl.CostEstimate(flops=2 * G * D * width, bytes_accessed=20 << 20, transcendentals=0),
        name=name,
    )(left, right, left_two, right_two)


def shards(tokens, segments, mixer_weights, norm_gains, gate_weights, channel_terms, feed_weights, cotangent):
    dp, sq = lax.axis_index("dp"), lax.axis_index("seq")
    mix = jnp.pad(mixer_weights.reshape(16, 3, SEQ, WL), ((0, 0), (0, 0), (0, 0), (0, WP - WL)))
    mix = mix.transpose(2, 0, 1, 3).reshape(SEQ, 16, MW)
    lane = lax.broadcasted_iota(jnp.int32, (2, 128), 1)
    gain_rows = jnp.where(lane // 16 == sq, jnp.tile(norm_gains.T, (1, SEQ)), jnp.zeros((), bf16))
    small = jnp.concatenate(
        [jnp.pad(gain_rows, ((0, 14), (0, 0))), jnp.pad(segments.astype(bf16)[None], ((0, 15), (0, 0)))], 0
    )
    gate_block = jnp.where(
        sq < 4,
        jnp.pad(gate_weights, ((0, 8), (0, 256 - BW))),
        jnp.pad(gate_weights, ((0, 8), (BW - 128, 2 * 128 - 2 * BW + 128))),
    )
    gate_block = jnp.concatenate([gate_block[:, :128], gate_block[:, 128:]], 0)
    channel = channel_terms.T.astype(f32)
    lam = channel[7:8]
    derived = jnp.concatenate([-rate_scale * jax.nn.softplus(-lam), rate_scale * jax.nn.sigmoid(-lam)], 0)
    coarse = lax.optimization_barrier(derived.astype(bf16)).astype(f32)
    columns = jnp.concatenate([channel[:7], coarse, derived - coarse], 0)
    piece = 8 * (dp % 2) + sq
    chan_block = lax.dynamic_update_slice(jnp.zeros((16, WP), f32), columns, (0, piece * 20)).astype(bf16)
    chan_block = jnp.concatenate([chan_block[:, n * 128 : n * 128 + 128] for n in range(3)], 0)
    (
        cot_all, w, normed, *saved, mixed, hidden, adj_gu, back_part, feed_part, norm_two,
        gates, terms, gains, lab, middle,
    ) = forward_call(tokens, cotangent, mix, feed_weights, small, gate_block, chan_block)
    feed_grad = grad_call(norm_two, adj_gu, cot_all, hidden, "feedgrad")
    feed_sum = lax.psum_scatter(feed_grad, "dp", scatter_dimension=0, tiled=True)
    adj_middle, gain_two, adj_all = turn_call(back_part, middle, cotangent, gains[1:2])
    both, in_part, gate_grad, sums = unmix_call(adj_all, w, gates, terms, lab, saved)
    input_gradient, activations, mix_out, gate_out, chan_out, gain_out = close_call(
        in_part, feed_part, normed, both, adj_all, mixed, gate_grad, sums, tokens,
        adj_middle, middle, gains[0:1], gain_two,
    )
    feed_out = swap_call(feed_sum.reshape(SEQ, 16, FW), 5, "swap")
    mixer_gradient = (
        mix_out.reshape(SEQ, 16, 3, WP)[..., :WL].transpose(1, 2, 0, 3).reshape(16, 3 * W).astype(f32)
    )
    feed_gradient = feed_out.reshape(SEQ, 16, 3, FL).transpose(1, 2, 0, 3).reshape(16, 3 * FF).astype(f32)
    gate_gradient = jnp.where(sq < 4, gate_out[:40, :BW], gate_out[:40, BW : 2 * BW])
    channel_gradient = lax.dynamic_slice(chan_out, (0, piece * 20), (8, 20)).T
    gain_gradient = lax.dynamic_slice(gain_out, (0, sq * 16), (2, 16)).T
    return (activations, input_gradient, mixer_gradient, gain_gradient, gate_gradient, channel_gradient, feed_gradient)


def solution(mesh):
    one = P(("dp", "seq"))
    two = P(("dp", "seq"), None)
    placed = (two, one, two, two, two, two, two, two)
    return jax.shard_map(shards, mesh=mesh, in_specs=placed, out_specs=(two,) * 7, check_vma=False)
```

time: 373 us -> 344 us (0.922); the launches traced: 372 us -> 338 us
  Pallas kernels: 324 us -> 302 us
  local copies, waits for them, and re-layouts: 25.4 us -> 16 us
  other arithmetic: 8.67 us -> 4.92 us
    pallas_call x4 -> x1, Pallas kernels: 161 us -> 136 us  [forward_call(): pl.pallas_call(forward_kernel, out_shape=(sds((G, D), bf16), sds((D, MW),...]
    reshape x10 -> x0, local copies, waits for them, and re-layouts: 5.44 us -> none  [the longest x2 1.72 us: shards(): feed_weights.reshape(16, 3, SEQ, FL).transpose(2, 0, 1, 3)]
  transfers between devices with their start and end apart: 2 -> 1, of which waited for: 0 -> 0; matrix products, arithmetic and copies ran while one was open for 5% -> 2% of each run, Pallas kernels for 56% -> 41%
where the time goes in v3:
time: 344 us; the launch traced here: 338 us
  Pallas kernels  302 us (88%)
  local copies, waits for them, and re-layouts  16 us (5%)
  between operations  14.7 us (4%)
  other arithmetic  4.92 us (1%)
    pallas_call x1, Pallas kernels, forward_call(): pl.pallas_call(forward_kernel, out_shape=(sds((G, D), bf16), sds((D, MW),...  136 us
    pallas_call x1, Pallas kernels, close_call(): pl.pallas_call(close_kernel, out_shape=(sds((T, D), f32), sds((T, D), bf1...  68.3 us
    pallas_call x1, Pallas kernels, turn_call(): pl.pallas_call(turn_kernel, out_shape=(sds((T, D), f32), sds((1, D), f32)...  49.6 us
    pallas_call x1, Pallas kernels, unmix_call(): pl.pallas_call(unmix_kernel, grid=(STEPS,), out_shape=(sds((G, 2 * WP), b...  21.7 us
    pallas_call x1, Pallas kernels, grad_call(): pl.pallas_call(grad_kernel, grid=(D // block,), out_shape=jax.ShapeDtypeS...  16.1 us
    pallas_call x1, Pallas kernels, swap_call(): pl.pallas_call(swap_kernel, out_shape=jax.ShapeDtypeStruct(src.shape, src...  10.5 us
  transfers between devices with their start and end apart: 1, of which 0 were waited for; matrix products, arithmetic and copies ran while one was open for 2% of the time, Pallas kernels for 41%

profile of v3, /device:TPU:1, one launch (start us, length us, event | category | flops | bytes accessed | tf_op | source)
XLA Modules:
  0.0 337.9 jit_solution(8626422220016171130)
XLA Ops:
  7.2 0.7 convert_bitcast_fusion.1
  8.0 0.7 convert_bitcast_fusion.2
  8.7 0.7 tile.4
  9.3 0.1 tile.10
  9.5 0.7 dynamic_update_slice.3
  10.1 0.9 pad_select_fusion
  11.0 1.2 reshape.39
  12.2 0.2 copy.19
  12.4 0.2 pad_bitcast_fusion
  12.6 1.0 reshape.40.mix
  13.6 0.6 fusion.2.small
  14.2 0.6 pad_maximum_fusion.gates
  14.8 0.6 pad_maximum_fusion.1.chan
  15.4 136.1 %forward.1 = (bf16[1024,2048]{1,0:T(8,128)(2,1)}, bf16[2048,1152]{1,0:T(8,128)(2,1)}, bf16[1024,2048]{1,0:T(8,128)(2,1)}, f32[1024,384]{1,0:T(8,128)}, f32[1024,...) custom-call(bf16[128,2048]{1,0:T(8,128)(2,1)} %tok.3, ...), custom_call_target="tpu_custom_call" | custom-call | flops 24159191040 | bytes 104857600 | tf_op jit(solution)/shard_map/forward/pallas_call | solution.py:1124
  151.4 16.1 %feedgrad.1 = bf16[2048,2304]{1,0:T(8,128)(2,1)} custom-call(bf16[1024,2048]{1,0:T(8,128)(2,1)} %get-tuple-element.65.left, bf16[1024,1536]{1,0:T(8,128)(2,1)} %get-tuple-element.66.right, bf16[1024,2048]{1,0:T(8,128)(2,1)} %get-tuple-element.67.left_two, bf16[1024,768]{1,0:T(8,128)(2,1)} %get-tuple-element.68.right_two), custom_call_target="tpu_custom_call" | custom-call | flops 9663676416 | bytes 20971520 | tf_op jit(solution)/shard_map/feedgrad/pallas_call | solution.py:1267
  167.6 1.5 fusion.6
  169.1 49.6 %turn.1 = (f32[128,2048]{1,0:T(8,128)}, f32[1,2048]{1,0:T(1,128)}, bf16[1024,2048]{1,0:T(8,128)(2,1)}) custom-call(bf16[1024,2048]{1,0:T(8,128)(2,1)} %get-tuple-element.38.part, f32[128,2048]{1,0:T(8,128)} %get-tuple-element.39.middle, bf16[128,2048]{1,0:T(8,128)(2,1)} %cot.3, f32[1,2048]{1,0:T(1,128)} %get-tuple-element.70.gain), custom_call_target="tpu_custom_call" | custom-call | flops 1000 | bytes 104857600 | tf_op jit(solution)/shard_map/turn/pallas_call | solution.py:427
  218.7 21.7 %unmix.1 = (bf16[1024,768]{1,0:T(8,128)(2,1)}, bf16[1024,2048]{1,0:T(8,128)(2,1)}, bf16[16,48,384]{2,1,0:T(8,128)(2,1)}, f32[8,384]{1,0:T(8,128)}) custom-call(bf16[1024,2048]{1,0:T(8,128)(2,1)} %get-tuple-element.41.adj_out.adj_in, bf16[2048,1152]{1,0:T(8,128)(2,1)} %get-tuple-element.42.w, bf16[2,384,384]{2,1,0:T(8,128)(2,1)} %get-tuple-element.43.gates, ...), custom_call_target="tpu_custom_call" | custom-call | flops 4831838208 | bytes 31457280 | tf_op jit(solution)/shard_map/unmix/pallas_call | solution.py:1238
  240.4 68.3 %close.1 = (f32[128,2048]{1,0:T(8,128)}, bf16[128,2048]{1,0:T(8,128)(2,1)}, bf16[8,16,1152]{2,1,0:T(8,128)(2,1)}, f32[48,384]{1,0:T(8,128)}, f32[8,384]{1,0:T(8,128)}, /*index=5*/f32[8,128]{1,0:T(8,128)}) custom-call(bf16[1024,2048]{1,0:T(8,128)(2,1)} %get-tuple-element.50.part, bf16[1024,2048]{1,0:T(8,128)(2,1)} %get-tuple-element.51.feed_part, ...), custom_call_target="tpu_custom_call" | custom-call | flops 1000 | bytes 104857600 | tf_op jit(solution)/shard_map/close/pallas_call | solution.py:662
  308.7 1.1 reshape.41
  309.8 0.1 convert_bitcast_fusion
  309.9 0.3 copy.20
  310.3 0.9 reshape.43
  311.2 1.3 dynamic-slice_bitcast_fusion.1
  312.5 1.4 dynamic-slice_bitcast_fusion
  313.9 0.7 slice_select_fusion
  314.6 10.5 %swap.1 = bf16[8,16,2304]{2,1,0:T(8,128)(2,1)} custom-call(bf16[8,16,2304]{2,1,0:T(8,128)(2,1)} %bitcast.23), custom_call_target="tpu_custom_call" | custom-call | flops 1000 | bytes 1048576 | tf_op jit(solution)/shard_map/swap/pallas_call | solution.py:713
  325.1 1.7 reshape.45
  326.8 0.7 copy.21
  327.5 1.4 copy.22
  328.8 0.8 copy.26
  329.6 1.0 copy.27
  (20 shorter events, 0.2 us)
Async XLA Ops:
  7.2 307.4 %reduce-scatter.2.cloned.1.call-start = ((), (), s32[]{:S(2)}) async-start(), calls=%async_computation.1 | async-start | bytes 10027008 | tf_op jit(solution)/shard_map/reduce_scatter | solution.py:1310
  308.7 5.2 %copy-start.2 = (f32[48,384]{1,0:T(8,128)S(1)}, f32[48,384]{1,0:T(8,128)}, u32[]{:S(2)}) copy-start(f32[48,384]{1,0:T(8,128)} %get-tuple-element.63) | copy-start | bytes 221188
  325.1 3.8 %copy-start.1 = (bf16[128,2048]{1,0:T(8,128)(2,1)S(1)}, bf16[128,2048]{1,0:T(8,128)(2,1)}, u32[]{:S(2)}) copy-start(bf16[128,2048]{1,0:T(8,128)(2,1)} %get-tuple-element.87) | copy-start | bytes 1572868
  326.8 2.9 copy-start
Sparse Core Ops, SparseCore 0:
  167.7 84.1 reduce-scatter.1

commit v4 on v3

--- a/solution.py
+++ b/solution.py
@@ -305,7 +305,6 @@
     def scratch(n):
         return [
             VMEM((4, T, n), bf16),
-            VMEM((4, T, n), bf16),
             VMEM((2, HALF, n), bf16),
             VMEM((2, HALF, n), bf16),
             VMEM((4, HALF, n), bf16),
@@ -313,19 +312,20 @@
             DMA((10,)),
         ]
 
-    def __init__(self, me, part, other, pair, through, passed, final, send, recv):
+    def __init__(self, me, part, other, through, passed, final, send, recv):
         self.me, self.part = me, part
-        self.other, self.pair, self.through, self.passed, self.final = other, pair, through, passed, final
+        self.other, self.through, self.passed, self.final = other, through, passed, final
         self.send, self.recv = send, recv
-        self.sent = []
 
     def piece(self, k, c):
         return self.part.at[pl.ds(pl.multiple_of(self.me.slot(k, c) * T, T), T)]
 
+    def pair(self, k, q):
+        base = self.me.slot(k, self.me.c) * T + q * HALF
+        return self.part.at[pl.ds(pl.multiple_of(base, HALF), HALF)]
+
     def push(self, n, src, dst, device):
-        copy = remote(src, dst, self.send.at[n], self.recv.at[n], device)
-        copy.start()
-        self.sent.append(copy)
+        remote(src, dst, self.send.at[n], self.recv.at[n], device).start()
 
     def arrived(self, n, dst):
         remote(dst, dst, self.send.at[n], self.recv.at[n], self.me.sibling()).wait_recv()
@@ -337,47 +337,102 @@
 
     def join(self):
         me = self.me
-        a, b = pl.ds(0, HALF), pl.ds(HALF, HALF)
         right, left = me.z_peer(1), me.z_peer(3)
         for k in (2, 1, 3, 0):
             self.arrived(k, self.other.at[k])
             add_rows(
-                self.pair.at[k], 0, [reads(self.piece(k, me.c)), reads(self.other.at[k])], T
+                self.piece(k, me.c), 0, [reads(self.piece(k, me.c)), reads(self.other.at[k])], T
             )
             if k == 2:
-                self.push(4, self.pair.at[2, a], self.through.at[0], right)
-                self.push(5, self.pair.at[2, b], self.through.at[1], left)
+                self.push(4, self.pair(2, 0), self.through.at[0], right)
+                self.push(5, self.pair(2, 1), self.through.at[1], left)
             if k == 1:
-                self.push(6, self.pair.at[1, b], self.final.at[0], right)
+                self.push(6, self.pair(1, 1), self.final.at[0], right)
             if k == 3:
-                self.push(7, self.pair.at[3, a], self.final.at[1], left)
+                self.push(7, self.pair(3, 0), self.final.at[1], left)
 
     def relay(self):
         me = self.me
         right, left = me.z_peer(1), me.z_peer(3)
         self.arrived(4, self.through.at[0])
-        add_rows(self.passed.at[0], 0, [reads(self.through.at[0]), reads(self.pair.at[1])], HALF)
+        add_rows(self.passed.at[0], 0, [reads(self.through.at[0]), reads(self.pair(1, 0))], HALF)
         self.push(8, self.passed.at[0], self.final.at[2], right)
         self.arrived(5, self.through.at[1])
-        add_rows(self.passed.at[1], 0, [reads(self.through.at[1]), reads(self.pair.at[3], HALF)], HALF)
+        add_rows(self.passed.at[1], 0, [reads(self.through.at[1]), reads(self.pair(3, 1))], HALF)
         self.push(9, self.passed.at[1], self.final.at[3], left)
 
     def finish(self, out, extra=None):
+        me = self.me
         for n, k in ((6, 0), (7, 1), (8, 2), (9, 3)):
             self.arrived(n, self.final.at[k])
         more = [] if extra is None else [reads(extra)]
         add_rows(
-            out, 0, [reads(self.pair.at[0]), reads(self.final.at[1]), reads(self.final.at[2])] + more, HALF
+            out, 0, [reads(self.pair(0, 0)), reads(self.final.at[1]), reads(self.final.at[2])] + more, HALF
         )
         more = [] if extra is None else [reads(extra, HALF)]
         add_rows(
             out,
             HALF,
-            [reads(self.pair.at[0], HALF), reads(self.final.at[0]), reads(self.final.at[3])] + more,
+            [reads(self.pair(0, 1)), reads(self.final.at[0]), reads(self.final.at[3])] + more,
             HALF,
         )
-        for copy in self.sent:
-            copy.wait_send()
+        for n in range(10):
+            size = self.other.at[n] if n < 4 else self.final.at[0]
+            remote(size, size, self.send.at[n], self.recv.at[n], me.sibling()).wait_send()
+
+
+class RingSum:
+    @staticmethod
+    def scratch(shape):
+        return [
+            VMEM((2, *shape), bf16), VMEM((2, *shape), bf16), VMEM((4, *shape), bf16), DMA((6,)), DMA((6,)),
+        ]
+
+    def __init__(self, me, right, left, piece, through, passed, final, send, recv):
+        self.me, self.right, self.left, self.piece = me, right, left, piece
+        self.through, self.passed, self.final, self.send, self.recv = through, passed, final, send, recv
+
+    def push(self, n, src, dst, device):
+        remote(src, dst, self.send.at[n], self.recv.at[n], device).start()
+
+    def arrived(self, n, dst):
+        remote(dst, dst, self.send.at[n], self.recv.at[n], self.me.sibling()).wait_recv()
+
+    def start(self):
+        self.push(0, self.piece(2, 0), self.through.at[0], self.right)
+        self.push(1, self.piece(2, 1), self.through.at[1], self.left)
+        self.push(2, self.piece(1, 1), self.final.at[0], self.right)
+        self.push(3, self.piece(3, 0), self.final.at[1], self.left)
+
+    def add(self, out, terms):
+        count, rows = terms[0].shape[0], terms[0].shape[1]
+
+        def body(i, carry):
+            m, here = i // (rows // 16), pl.ds(pl.multiple_of(i % (rows // 16) * 16, 16), 16)
+            total = terms[0][m, here].astype(f32)
+            for term in terms[1:]:
+                total = total + term[m, here].astype(f32)
+            out[m, here] = total.astype(out.dtype)
+            return carry
+
+        lax.fori_loop(0, count * (rows // 16), body, 0)
+
+    def relay(self):
+        self.arrived(0, self.through.at[0])
+        self.add(self.passed.at[0], [self.through.at[0], self.piece(1, 0)])
+        self.push(4, self.passed.at[0], self.final.at[2], self.right)
+        self.arrived(1, self.through.at[1])
+        self.add(self.passed.at[1], [self.through.at[1], self.piece(3, 1)])
+        self.push(5, self.passed.at[1], self.final.at[3], self.left)
+
+    def finish(self, out):
+        for n, k in ((2, 0), (3, 1), (4, 2), (5, 3)):
+            self.arrived(n, self.final.at[k])
+        self.add(out(0), [self.piece(0, 0), self.final.at[1], self.final.at[2]])
+        self.add(out(1), [self.piece(0, 1), self.final.at[0], self.final.at[3]])
+        for n in range(6):
+            size = self.final.at[0]
+            remote(size, size, self.send.at[n], self.recv.at[n], self.me.sibling()).wait_send()
 
 
 def norm_rows(value, gain):
@@ -390,336 +445,6 @@
     inner = jnp.mean(value * scaled, axis=-1, keepdims=True)
     normed = value * r
     return r * (scaled - normed * (inner * r)), incoming * normed
-
-
-def turn_kernel(part, middle, cot, gain, adj_middle, gain_grad, adj_all, adj, *rest):
-    scatter, gathering = rest[:7], rest[7:]
-    me = Place()
-    mine = pl.multiple_of(me.sq * T, T)
-    own = gathering[0]
-    barrier, count = greet(z_peers(me))
-    pl.semaphore_wait(barrier, count)
-    total = Scatter(me, part, *scatter)
-    total.start()
-    total.join()
-    total.relay()
-    total.finish(adj)
-
-    def body(i, carry):
-        here = pl.ds(pl.multiple_of(i * 16, 16), 16)
-        pulled, terms = norm_pull(middle[here], gain[...], adj[here])
-        value = cot[here].astype(f32) + pulled
-        adj_middle[here] = value
-        own[pl.ds(pl.multiple_of(mine + i * 16, 16), 16)] = value.astype(bf16)
-        return carry + jnp.sum(terms, axis=0, keepdims=True)
-
-    gain_grad[...] = lax.fori_loop(0, T // 16, body, jnp.zeros((1, D), f32))
-    gather = Gather(me, own, adj_all, *gathering)
-    gather.start()
-    gather.forward()
-    gather.across()
-    gather.finish()
-
-
-def turn_call(part, middle, cot, gain):
-    sds = jax.ShapeDtypeStruct
-    hbm, vmem = pl.BlockSpec(memory_space=ANY), pl.BlockSpec(memory_space=VMEM)
-    return pl.pallas_call(
-        turn_kernel,
-        out_shape=(sds((T, D), f32), sds((1, D), f32), sds((G, D), bf16)),
-        in_specs=[vmem] * 4,
-        out_specs=[vmem, vmem, hbm],
-        scratch_shapes=[VMEM((T, D), f32)] + Scatter.scratch(D) + Gather.scratch(D),
-        compiler_params=pltpu.CompilerParams(collective_id=3, has_side_effects=True, vmem_limit_bytes=62 << 20),
-        cost_estimate=pl.CostEstimate(flops=1000, bytes_accessed=100 << 20, transcendentals=0),
-        name="turn",
-    )(part, middle, cot, gain)
-
-
-def close_kernel(
-    part, feed_part, normed_in, both_in, adj_in, mixed_in, eg, sums, tok, adj_middle, middle, gain, gain_two,
-    in_grad, act, mix_out, gate_out, chan_out, gain_out,
-    normed, both, adj_out, mixed, mg, adj, r1, s1, r2, last, e_in, sums_in, gate_sum, chan_sum, gp, gp_in, gain_sum, gain_in, *rest,
-):
-    one, two = rest[:7], rest[7:14]
-    m1s, m1r, m2s, m2r, m3s, m3r, es, er, us, ur, gs, gr, hs, hr, qs, qr, ls, ws = rest[14:]
-    me = Place()
-    loads = [
-        pltpu.make_async_copy(src, dst, ws.at[n])
-        for n, (src, dst) in enumerate(
-            ((normed_in, normed), (both_in, both), (adj_in, adj_out), (mixed_in, mixed))
-        )
-    ]
-    for copy in loads:
-        copy.start()
-    quarter, at = me.dp // 8, me.dp % 8
-    gate_to = (8 * quarter + me.sq, at)
-    gate_self = me.sq == at
-    chan_from = (8 * (me.dp % 2) + me.sq, me.dp // 2)
-    chan_to = (2 * me.sq + me.dp // 8, me.dp % 8)
-    chan_self = jnp.logical_and(chan_from[0] == me.dp, chan_from[1] == me.sq)
-    barrier, count = greet(seq_peers(me) + dp_peers(me))
-
-    @pl.when(jnp.logical_not(gate_self))
-    def _():
-        pl.semaphore_signal(barrier, inc=1, device_id=gate_to, device_id_type=MESH)
-
-    @pl.when(jnp.logical_not(chan_self))
-    def _():
-        pl.semaphore_signal(barrier, inc=1, device_id=chan_from, device_id_type=MESH)
-
-    pl.semaphore_wait(barrier, count + jnp.where(gate_self, 0, 1) + jnp.where(chan_self, 0, 1))
-
-    sent = []
-
-    def push(src, dst, send, recv, device):
-        sent.append(remote(src, dst, send, recv, device))
-        sent[-1].start()
-
-    def arrived(dst, send, recv):
-        remote(dst, dst, send, recv, me.sibling()).wait_recv()
-
-    lo, hi = pl.ds(0, 4), pl.ds(4, 4)
-    inner = Scatter(me, part, *one)
-    outer = Scatter(me, feed_part, *two)
-    inner.start()
-    for k in range(1, DP):
-        to = (me.dp + k) % DP
-        push(eg.at[to], e_in.at[k], es.at[k], er.at[k], me.dp_peer(to))
-        push(sums, sums_in.at[k], us.at[k], ur.at[k], me.dp_peer(to))
-    inner.join()
-    for copy in loads:
-        copy.wait()
-
-    def tile(i, carry):
-        here = pl.ds(pl.multiple_of(i * 256, 256), 256)
-        left = tn(normed[:, here], both[...]).astype(bf16)
-        right = tn(adj_out[:, here], mixed[...]).astype(bf16)
-        for h in range(2):
-            for n in range(SEQ):
-                rows = slice(h * T + n * 16, h * T + (n + 1) * 16)
-                mg[i // 2, i % 2 * 2 + h, n, :, : 2 * WP] = left[rows]
-                mg[i // 2, i % 2 * 2 + h, n, :, 2 * WP :] = right[rows]
-        return carry
-
-    lax.fori_loop(0, 8, tile, 0)
-    for k in (2, 1, 3):
-        push(mg.at[:, (me.y + k) % 4, lo], r1.at[0, k - 1], m1s.at[k], m1r.at[k], me.dp_peer(me.y_dp(k)))
-        push(mg.at[(me.x + k) % 4, :, hi], r1.at[1, k - 1], m1s.at[4 + k], m1r.at[4 + k], me.dp_peer(me.x_dp(k)))
-    outer.start()
-    inner.relay()
-    outer.join()
-    inner.finish(adj)
-
-    def pull(i, carry):
-        here = pl.ds(pl.multiple_of(i * 16, 16), 16)
-        pulled, terms = norm_pull(tok[here].astype(f32), gain[...], adj[here])
-        in_grad[here] = adj_middle[here] + pulled
-        return carry + jnp.sum(terms, axis=0, keepdims=True)
-
-    gain_one = lax.fori_loop(0, T // 16, pull, jnp.zeros((1, D), f32))
-    gp[...] = jnp.zeros(gp.shape, f32)
-    for k in range(DP):
-        gp[k, 0:1] = gain_one[:, k * 128 : (k + 1) * 128]
-        gp[k, 1:2] = gain_two[:, k * 128 : (k + 1) * 128]
-    for k in range(1, DP):
-        to = (me.dp + k) % DP
-        push(gp.at[to], gp_in.at[k], gs.at[k], gr.at[k], me.dp_peer(to))
-    outer.relay()
-
-    for k in range(1, DP):
-        arrived(e_in.at[k], es.at[k], er.at[k])
-        arrived(sums_in.at[k], us.at[k], ur.at[k])
-
-    def add_gates(i, carry):
-        here = pl.ds(pl.multiple_of(i * 16, 16), 16)
-
-        def step(k, total):
-            return total + e_in[k, here].astype(f32)
-
-        gate_sum[here] = lax.fori_loop(1, DP, step, eg[me.dp, here].astype(f32))
-        return carry
-
-    lax.fori_loop(0, 3, add_gates, 0)
-
-    def add_sums(k, total):
-        return total + sums_in[k]
-
-    chan_sum[...] = lax.fori_loop(1, DP, add_sums, sums[...])
-    gate_copy = remote(gate_sum, gate_out, hs.at[0], hr.at[0], gate_to)
-    chan_copy = remote(chan_sum, chan_out, hs.at[1], hr.at[1], chan_to)
-    gate_local = pltpu.make_async_copy(gate_sum, gate_out, ls.at[0])
-    chan_local = pltpu.make_async_copy(chan_sum, chan_out, ls.at[1])
-
-    @pl.when(jnp.logical_not(gate_self))
-    def _():
-        gate_copy.start()
-
-    @pl.when(gate_self)
-    def _():
-        gate_local.start()
-
-    @pl.when(jnp.logical_not(chan_self))
-    def _():
-        chan_copy.start()
-
-    @pl.when(chan_self)
-    def _():
-        chan_local.start()
-
-    for k in (1, 3, 2):
-        arrived(r1.at[0, k - 1], m1s.at[k], m1r.at[k])
-        arrived(r1.at[1, k - 1], m1s.at[4 + k], m1r.at[4 + k])
-    for j in (2, 1, 3, 0):
-
-        def first(i, carry, j=j):
-            xx, yy = (me.x + j) % 4, (me.y + j) % 4
-            total = mg[xx, me.y, i].astype(f32)
-            for k in range(3):
-                total = total + r1[0, k, xx, i].astype(f32)
-            s1[0, j, i] = total.astype(bf16)
-            total = mg[me.x, yy, 4 + i].astype(f32)
-            for k in range(3):
-                total = total + r1[1, k, yy, i].astype(f32)
-            s1[1, j, i] = total.astype(bf16)
-            return carry
-
-        lax.fori_loop(0, 4, first, 0)
-        if j:
-            push(s1.at[0, j], r2.at[0, j - 1], m2s.at[j], m2r.at[j], me.dp_peer(me.x_dp(j)))
-            push(s1.at[1, j], r2.at[1, j - 1], m2s.at[4 + j], m2r.at[4 + j], me.dp_peer(me.y_dp(j)))
-
-    for k in range(1, DP):
-        arrived(gp_in.at[k], gs.at[k], gr.at[k])
-
-    def gains(k, total):
-        return total + gp_in[k]
-
-    gain_sum[...] = lax.fori_loop(1, DP, gains, gp[me.dp])
-    for k in range(1, SEQ):
-        push(gain_sum, gain_in.at[k], qs.at[k], qr.at[k], me.seq_peer(k))
-
-    outer.finish(adj, middle)
-
-    def lower(i, carry):
-        here = pl.ds(pl.multiple_of(i * 16, 16), 16)
-        act[here] = adj[here].astype(bf16)
-        return carry
-
-    lax.fori_loop(0, T // 16, lower, 0)
-
-    for j in (1, 3, 2):
-        arrived(r2.at[0, j - 1], m2s.at[j], m2r.at[j])
-        arrived(r2.at[1, j - 1], m2s.at[4 + j], m2r.at[4 + j])
-
-    def second(i, carry):
-        for h in range(2):
-            total = s1[h, 0, i].astype(f32)
-            for k in range(3):
-                total = total + r2[h, k, i].astype(f32)
-            last[4 * h + i] = total.astype(bf16)
-        return carry
-
-    lax.fori_loop(0, 4, second, 0)
-    keep = pltpu.make_async_copy(last.at[me.sq], mix_out.at[me.sq], ls.at[2])
-    keep.start()
-    for k in (4, 3, 5, 2, 6, 1, 7):
-        to = (me.sq + k) % SEQ
-        push(last.at[to], mix_out.at[me.sq], m3s.at[k], m3r.at[k], me.seq_peer(k))
-    for k in range(1, SEQ):
-        arrived(gain_in.at[k], qs.at[k], qr.at[k])
-    total = gain_sum[...]
-    for k in range(1, SEQ):
-        total = total + gain_in[k]
-    gain_out[...] = total
-
-    @pl.when(jnp.logical_not(gate_self))
-    def _():
-        gate_copy.wait()
-
-    @pl.when(gate_self)
-    def _():
-        gate_local.wait()
-
-    @pl.when(jnp.logical_not(chan_self))
-    def _():
-        chan_copy.wait()
-
-    @pl.when(chan_self)
-    def _():
-        chan_local.wait()
-
-    for k in range(1, SEQ):
-        arrived(mix_out.at[(me.sq - k + SEQ) % SEQ], m3s.at[k], m3r.at[k])
-    keep.wait()
-    for copy in sent:
-        copy.wait_send()
-
-
-def close_call(part, feed_part, normed, both, adj_out, mixed, eg, sums, tok, adj_middle, middle, gain, gain_two):
-    sds = jax.ShapeDtypeStruct
-    vmem = pl.BlockSpec(memory_space=VMEM)
-    return pl.pallas_call(
-        close_kernel,
-        out_shape=(
-            sds((T, D), f32), sds((T, D), bf16), sds((SEQ, 16, MW), bf16),
-            sds((48, WP), f32), sds((8, WP), f32), sds((8, 128), f32),
-        ),
-        in_specs=[vmem] * 2 + [pl.BlockSpec(memory_space=ANY)] * 4 + [vmem] * 7,
-        out_specs=[vmem] * 6,
-        scratch_shapes=[
-            VMEM((G, D), bf16), VMEM((G, 2 * WP), bf16), VMEM((G, D), bf16), VMEM((G, WP), bf16),
-            VMEM((4, 4, SEQ, 16, MW), bf16),
-            VMEM((T, D), f32),
-            VMEM((2, 3, 4, 4, 16, MW), bf16), VMEM((2, 4, 4, 16, MW), bf16), VMEM((2, 3, 4, 16, MW), bf16),
-            VMEM((SEQ, 16, MW), bf16), VMEM((DP, 48, WP), bf16), VMEM((DP, 8, WP), f32), VMEM((48, WP), f32),
-            VMEM((8, WP), f32), VMEM((DP, 8, 128), f32), VMEM((DP, 8, 128), f32),
-            VMEM((8, 128), f32), VMEM((SEQ, 8, 128), f32),
-        ]
-        + Scatter.scratch(D)
-        + Scatter.scratch(D)
-        + [
-            DMA((8,)), DMA((8,)), DMA((8,)), DMA((8,)), DMA((8,)), DMA((8,)),
-            DMA((DP,)), DMA((DP,)), DMA((DP,)), DMA((DP,)), DMA((DP,)), DMA((DP,)), DMA((2,)), DMA((2,)),
-            DMA((SEQ,)), DMA((SEQ,)), DMA((3,)), DMA((4,)),
-        ],
-        compiler_params=pltpu.CompilerParams(collective_id=4, has_side_effects=True, vmem_limit_bytes=62 << 20),
-        cost_estimate=pl.CostEstimate(flops=1000, bytes_accessed=100 << 20, transcendentals=0),
-        name="close",
-    )(part, feed_part, normed, both, adj_out, mixed, eg, sums, tok, adj_middle, middle, gain, gain_two)
-
-
-def swap_kernel(src, dst, ss, sr, ls):
-    me = Place()
-    barrier, count = greet(seq_peers(me))
-    keep = pltpu.make_async_copy(src.at[me.sq], dst.at[me.sq], ls.at[0])
-    keep.start()
-    pl.semaphore_wait(barrier, count)
-    sent = []
-    for k in (4, 3, 5, 2, 6, 1, 7):
-        to = (me.sq + k) % SEQ
-        sent.append(remote(src.at[to], dst.at[me.sq], ss.at[k], sr.at[k], me.seq_peer(k)))
-        sent[-1].start()
-    for k in range(1, SEQ):
-        source = (me.sq - k + SEQ) % SEQ
-        remote(dst.at[source], dst.at[source], ss.at[k], sr.at[k], me.sibling()).wait_recv()
-    keep.wait()
-    for copy in sent:
-        copy.wait_send()
-
-
-def swap_call(src, number, name):
-    hbm = pl.BlockSpec(memory_space=ANY)
-    return pl.pallas_call(
-        swap_kernel,
-        out_shape=jax.ShapeDtypeStruct(src.shape, src.dtype),
-        in_specs=[hbm],
-        out_specs=hbm,
-        scratch_shapes=[DMA((SEQ,)), DMA((SEQ,)), DMA((1,))],
-        compiler_params=pltpu.CompilerParams(collective_id=number, has_side_effects=True, vmem_limit_bytes=62 << 20),
-        cost_estimate=pl.CostEstimate(flops=1000, bytes_accessed=1 << 20, transcendentals=0),
-        name=name,
-    )(src)
 
 
 CHUNK = 256
@@ -765,16 +490,6 @@
     return jnp.dot(left, right, preferred_element_type=f32)
 
 
-def rows_spec(width, back=False):
-    if back:
-        return pl.BlockSpec((CHUNK, width), lambda i: (STEPS - 1 - i, 0))
-    return pl.BlockSpec((CHUNK, width), lambda i: (i, 0))
-
-
-def whole(shape):
-    return pl.BlockSpec(shape, lambda i: (0,) * len(shape))
-
-
 def rows_of(base, size):
     return pl.ds(pl.multiple_of(base, 16), size)
 
@@ -801,8 +516,8 @@
     small_in, minor, gate_f,
     xpad, dec, drv, sts, carry, *rest,
 ):
-    tg, cg, ng, sc = rest[:4], rest[4:8], rest[8:12], rest[12:19]
-    ms, mr, fs, fr, ss, sr, ps, pr, qs, qr, es, er, hs, hr, ls, os = rest[19:]
+    tg, cg, ng, sc = rest[:4], rest[4:8], rest[8:12], rest[12:18]
+    ms, mr, fs, fr, ss, sr, ps, pr, qs, qr, es, er, hs, hr, ls, os = rest[18:]
     me = Place()
     quarter, at = me.dp // 8, me.dp % 8
     gate_to = (8 * quarter + me.sq, at)
@@ -1143,140 +858,463 @@
             DMA((40,)), DMA((40,)), DMA((40,)), DMA((40,)), DMA((40,)), DMA((40,)),
             DMA((2,)), DMA((2,)), DMA((9,)), DMA((23,)),
         ],
-        compiler_params=pltpu.CompilerParams(collective_id=1, has_side_effects=True, vmem_limit_bytes=63 << 20),
+        compiler_params=pltpu.CompilerParams(collective_id=1, has_side_effects=True, vmem_limit_bytes=(63 << 20) + (900 << 10)),
         cost_estimate=pl.CostEstimate(flops=30 * G * D * WP, bytes_accessed=100 << 20, transcendentals=0),
         name="forward",
     )(tok, cot, mix, feed, small, gates, chan)
 
 
-def unmix_kernel(
-    adj_out, w, gates, terms_ref, lab, x_in, y_in, conv_in, prior_in,
-    both, part, gate_out, sums,
-    dec, adj, acp, carry, gate_grad,
+def turn_kernel(
+    back_in, ff_in, n2_in, cot_in, hid_in, gu_in, x_in, y_in, conv_in, prior_in, w_in,
+    middle, cot, gains, gates, terms_ref, lab,
+    adj_all, s1_out, both_out, part_out, adj_middle, act, gain_grad, extra,
+    part, ffp, mg, s1, both, dec, adjs, acp, carry, gate_grad, sums, *rest,
 ):
-    step = pl.program_id(0)
-    window = windows(lab, (STEPS - 1 - step) * CHUNK)
-
-    @pl.when(step == 0)
-    def _():
+    one, two, gathering, ring_a, ring_b = rest[:6], rest[6:12], rest[12:16], rest[16:21], rest[21:26]
+    ls, os = rest[26:]
+    me = Place()
+    first = [pltpu.make_async_copy(back_in, part, ls.at[0]), pltpu.make_async_copy(ff_in, ffp, ls.at[1])]
+    first[0].start()
+    barrier, count = greet(z_peers(me) + ring_peers(me))
+    pl.semaphore_wait(barrier, count)
+    xs, ys = (me.dp_peer(me.x_dp(1)), me.dp_peer(me.x_dp(3))), (me.dp_peer(me.y_dp(1)), me.dp_peer(me.y_dp(3)))
+    upper = RingSum(
+        me, *ys, lambda k, q: mg.at[:, (me.y + k) % 4, pl.ds(q * 32, 32)], *ring_a
+    )
+    lower = RingSum(
+        me, *xs, lambda k, q: mg.at[(me.x + k) % 4, :, pl.ds(HALF + q * 32, 32)], *ring_b
+    )
+    mine = me.sq * T
+
+    def grads(n2, cots, gu, hid):
+        loads = [
+            pltpu.make_async_copy(src, dst, ls.at[2 + n])
+            for n, (src, dst) in enumerate(((n2_in, n2), (cot_in, cots), (gu_in, gu), (hid_in, hid)))
+        ]
+        first[0].wait()
+        inner = Scatter(me, part, *one)
+        inner.start()
+        for copy in loads:
+            copy.start()
+        first[1].start()
+        inner.join()
+        for copy in loads:
+            copy.wait()
+
+        def tile(i, c):
+            here = pl.ds(pl.multiple_of(i * 256, 256), 256)
+            left = tn(n2[:, here], gu[...]).astype(bf16)
+            right = tn(cots[:, here], hid[...]).astype(bf16)
+            for h in range(2):
+                mg[i // 2, i % 2 * 2 + h, :, : 2 * FL] = left[h * T : (h + 1) * T]
+                mg[i // 2, i % 2 * 2 + h, :, 2 * FL :] = right[h * T : (h + 1) * T]
+
+            @pl.when(i == 3)
+            def _():
+                inner.relay()
+
+            return c
+
+        lax.fori_loop(0, 8, tile, 0)
+        upper.start()
+        lower.start()
+        inner.finish(adj_middle)
+
+    pl.run_scoped(grads, VMEM((G, D), bf16), VMEM((G, D), bf16), VMEM((G, 2 * FL), bf16), VMEM((G, FL), bf16))
+
+    def pull(i, c):
+        here = pl.ds(pl.multiple_of(i * 16, 16), 16)
+        pulled, terms = norm_pull(middle[here], gains[1:2], adj_middle[here])
+        value = cot[here].astype(f32) + pulled
+        adj_middle[here] = value
+        gathering[0][rows_of(mine + i * 16, 16)] = value.astype(bf16)
+        return c + jnp.sum(terms, axis=0, keepdims=True)
+
+    gain_grad[...] = lax.fori_loop(0, T // 16, pull, jnp.zeros((1, D), f32))
+    gather = Gather(me, None, adj_all, *gathering)
+    gather.start()
+    first[1].wait()
+    outer = Scatter(me, ffp, *two)
+
+    def unmix(x_all, y_all, conv_all, prior_all, w):
+        loads = [
+            pltpu.make_async_copy(src, dst, ls.at[2 + n])
+            for n, (src, dst) in enumerate(
+                ((x_in, x_all), (y_in, y_all), (conv_in, conv_all), (prior_in, prior_all), (w_in, w))
+            )
+        ]
+        for copy in loads:
+            copy.start()
+        gather.forward()
+        upper.relay()
+        lower.relay()
+        gather.across()
         dec[CHUNK:] = jnp.zeros((8, WP), f32)
         acp[CHUNK:] = jnp.zeros((8, WP), f32)
         carry[...] = jnp.zeros((8, WP), f32)
         gate_grad[...] = jnp.zeros(gate_grad.shape, f32)
         sums[...] = jnp.zeros(sums.shape, f32)
-
-    @pl.when(step > 0)
-    def _():
-        dec[CHUNK:] = dec[0:8]
-        acp[CHUNK:] = acp[0:8]
-
-    terms = terms_ref[...]
-    start = 1.0 - same(window, 1)
-    conv, prior = conv_in[...], prior_in[...]
-    lowered = conv.astype(bf16)
-    raw_a, raw_x = nn(lowered, gates[0]), nn(lowered, gates[1])
-    recall, admit, lograte, decay, root, scale = recur(conv, raw_a, raw_x, terms, start)
-    dec[0:CHUNK] = decay
-    states = decay * prior + scale * admit * conv
-    adj_mixed = nn(adj_out[...], w[:, 2 * WP :])
-    value, slope = gelu_parts(y_in[...])
-    adj[...] = adj_mixed * value
-    both[:, WP:] = (adj_mixed * states * slope).astype(bf16)
-    row = lax.broadcasted_iota(jnp.int32, (8, WP), 0)
-
-    def scan(i, after):
-        at = pl.multiple_of((CHUNK // 8 - 1 - i) * 8, 8)
-        here = pl.ds(at, 8)
-        later = dec[pl.ds(pl.multiple_of(at + 8, 8), 8)]
-        a = jnp.where(row < 7, pltpu.roll(dec[here], 7, 0), later[0:1])
-        b = adj[here]
-        for s in (1, 2, 4):
-            b = b + a * jnp.where(row < 8 - s, pltpu.roll(b, 8 - s, 0), 0.0)
-            a = a * jnp.where(row < 8 - s, pltpu.roll(a, 8 - s, 0), 1.0)
-        value = b + a * after
-        adj[here] = value
-        return jnp.broadcast_to(value[0:1], (8, WP))
-
-    carry[...] = lax.fori_loop(0, CHUNK // 8, scan, carry[...], unroll=4)
-    adjoint = adj[...]
-    flow = adjoint * admit * conv
-    adj_lograte = adjoint * prior * decay - (1.0 - start) * flow * (jnp.exp(2.0 * lograte) / root)
-    adj_ra = adj_lograte * terms[7:8] * (recall * (1.0 - recall))
-    adj_rx = flow * scale * (1.0 - admit)
-
-    def total(v):
-        return jnp.sum(v, axis=0, keepdims=True)
-
-    sums[5:6] += total(adj_ra)
-    sums[6:7] += total(adj_rx)
-    sums[7:8] += total(adj_lograte * recall) * terms[8:9]
-    low_a, low_x = adj_ra.astype(bf16), adj_rx.astype(bf16)
-    adj_conv = adjoint * scale * admit + nt(low_a, gates[0]) + nt(low_x, gates[1])
-    gate_grad[0] += tn(lowered, low_a)
-    gate_grad[1] += tn(lowered, low_x)
-    acp[0:CHUNK] = adj_conv
-    x = x_in[...]
-    adj_x = terms[0:1] * adj_conv
-    sums[4:5] += total(adj_conv)
-    sums[0:1] += total(adj_conv * x)
-    for k in range(1, CONV):
-        moved = same(window, -k) * acp[k : k + CHUNK]
-        adj_x = adj_x + terms[k : k + 1] * moved
-        sums[k : k + 1] += total(moved * x)
-    both[:, :WP] = adj_x.astype(bf16)
-    part[...] = nt(both[...], w[:, : 2 * WP]).astype(bf16)
-
-    @pl.when(step == STEPS - 1)
-    def _():
-        for k in range(DP):
-            rows = gate_grad[k // 8, k % 8 * 40 : k % 8 * 40 + 40]
-            gate_out[k] = jnp.concatenate([rows, jnp.zeros((8, WP), f32)], 0).astype(bf16)
-
-
-def unmix_call(adj_out, w, gates, terms, lab, saved):
+        for copy in loads:
+            copy.wait()
+        gather.finish()
+        outer.start()
+        row = lax.broadcasted_iota(jnp.int32, (8, WP), 0)
+
+        def chunk(step, c):
+            @pl.when(step == 1)
+            def _():
+                outer.join()
+
+            @pl.when(step == 3)
+            def _():
+                outer.relay()
+
+            base = (STEPS - 1 - step) * CHUNK
+            rows = rows_of(base, CHUNK)
+            window = windows(lab, base)
+            terms = terms_ref[...]
+            start = 1.0 - same(window, 1)
+            conv, prior = conv_all[rows], prior_all[rows]
+            lowered = conv.astype(bf16)
+            raw_a, raw_x = nn(lowered, gates[0]), nn(lowered, gates[1])
+            recall, admit, lograte, decay, root, scale = recur(conv, raw_a, raw_x, terms, start)
+            dec[0:CHUNK] = decay
+            states = decay * prior + scale * admit * conv
+            adj_mixed = nn(gathering[0][rows], w[:, 2 * WP :])
+            value, slope = gelu_parts(y_all[rows])
+            adjs[...] = adj_mixed * value
+            both[rows, WP:] = (adj_mixed * states * slope).astype(bf16)
+
+            def scan(i, after):
+                at = pl.multiple_of((CHUNK // 8 - 1 - i) * 8, 8)
+                here = pl.ds(at, 8)
+                later = dec[pl.ds(pl.multiple_of(at + 8, 8), 8)]
+                a = jnp.where(row < 7, pltpu.roll(dec[here], 7, 0), later[0:1])
+                b = adjs[here]
+                for s in (1, 2, 4):
+                    b = b + a * jnp.where(row < 8 - s, pltpu.roll(b, 8 - s, 0), 0.0)
+                    a = a * jnp.where(row < 8 - s, pltpu.roll(a, 8 - s, 0), 1.0)
+                value = b + a * after
+                adjs[here] = value
+                return jnp.broadcast_to(value[0:1], (8, WP))
+
+            carry[...] = lax.fori_loop(0, CHUNK // 8, scan, carry[...], unroll=4)
+            adjoint = adjs[...]
+            flow = adjoint * admit * conv
+            adj_lograte = adjoint * prior * decay - (1.0 - start) * flow * (jnp.exp(2.0 * lograte) / root)
+            adj_ra = adj_lograte * terms[7:8] * (recall * (1.0 - recall))
+            adj_rx = flow * scale * (1.0 - admit)
+
+            def total(v):
+                return jnp.sum(v, axis=0, keepdims=True)
+
+            sums[5:6] += total(adj_ra)
+            sums[6:7] += total(adj_rx)
+            sums[7:8] += total(adj_lograte * recall) * terms[8:9]
+            low_a, low_x = adj_ra.astype(bf16), adj_rx.astype(bf16)
+            adj_conv = adjoint * scale * admit + nt(low_a, gates[0]) + nt(low_x, gates[1])
+            gate_grad[0] += tn(lowered, low_a)
+            gate_grad[1] += tn(lowered, low_x)
+            acp[0:CHUNK] = adj_conv
+            x = x_all[rows]
+            adj_x = terms[0:1] * adj_conv
+            sums[4:5] += total(adj_conv)
+            sums[0:1] += total(adj_conv * x)
+            for k in range(1, CONV):
+                moved = same(window, -k) * acp[k : k + CHUNK]
+                adj_x = adj_x + terms[k : k + 1] * moved
+                sums[k : k + 1] += total(moved * x)
+            dec[CHUNK:] = dec[0:8]
+            acp[CHUNK:] = acp[0:8]
+            both[rows, :WP] = adj_x.astype(bf16)
+            part[rows] = nt(both[rows], w[:, : 2 * WP]).astype(bf16)
+            return c
+
+        lax.fori_loop(0, STEPS, chunk, 0)
+
+    wide = VMEM((G, WP), f32)
+    pl.run_scoped(unmix, wide, wide, wide, wide, VMEM((D, MW), bf16))
+    writes = [pltpu.make_async_copy(part, part_out, os.at[0]), pltpu.make_async_copy(both, both_out, os.at[1])]
+    for copy in writes:
+        copy.start()
+    for k in range(DP):
+        rows = slice(k % 8 * 40, k % 8 * 40 + 40)
+        for n in range(2):
+            lanes = slice(k % 8 // 4 * 128 + n * 128, k % 8 // 4 * 128 + n * 128 + 128)
+            piece = jnp.concatenate([gate_grad[k // 8, rows, lanes], jnp.zeros((8, 128), f32)], 0)
+            extra[k, 48 * n : 48 * n + 48] = piece.astype(bf16)
+            lanes = slice(channel_window(k) + n * 128, channel_window(k) + n * 128 + 128)
+            piece = jnp.concatenate([sums[:, lanes], jnp.zeros((8, 128), f32)], 0)
+            extra[k, 96 + 16 * n : 112 + 16 * n] = piece.astype(bf16)
+    upper.finish(lambda q: s1.at[0, :, pl.ds(q * 32, 32)])
+    lower.finish(lambda q: s1.at[1, :, pl.ds(q * 32, 32)])
+    writes.append(pltpu.make_async_copy(s1, s1_out, os.at[2]))
+    writes[2].start()
+    outer.finish(act, middle)
+    for copy in writes:
+        copy.wait()
+
+
+def channel_window(k):
+    return min(k * 20 // 128, 1) * 128
+
+
+def turn_call(back, ff, n2, cots, hid, gu, saved, w, middle, cot, gains, gates, terms, lab):
     sds = jax.ShapeDtypeStruct
+    hbm, vmem = pl.BlockSpec(memory_space=ANY), pl.BlockSpec(memory_space=VMEM)
     return pl.pallas_call(
-        unmix_kernel,
-        grid=(STEPS,),
-        out_shape=(sds((G, 2 * WP), bf16), sds((G, D), bf16), sds((DP, 48, WP), bf16), sds((8, WP), f32)),
-        in_specs=[
-            rows_spec(D, True), whole((D, MW)), whole((2, WP, WP)), whole((16, WP)),
-            whole((G + 16, 128)),
-        ]
-        + [rows_spec(WP, True)] * 4,
-        out_specs=[rows_spec(2 * WP, True), rows_spec(D, True), whole((DP, 48, WP)), whole((8, WP))],
+        turn_kernel,
+        out_shape=(
+            sds((G, D), bf16), sds((2, 4, HALF, FW), bf16), sds((G, 2 * WP), bf16), sds((G, D), bf16),
+            sds((T, D), f32), sds((T, D), bf16), sds((1, D), f32), sds((DP, 128, 128), bf16),
+        ),
+        in_specs=[hbm] * 11 + [vmem] * 6,
+        out_specs=[hbm] * 4 + [vmem] * 4,
         scratch_shapes=[
+            VMEM((G, D), bf16), VMEM((G, D), bf16), VMEM((4, 4, T, FW), bf16),
+            VMEM((2, 4, HALF, FW), bf16), VMEM((G, 2 * WP), bf16),
             VMEM((CHUNK + 8, WP), f32), VMEM((CHUNK, WP), f32), VMEM((CHUNK + 8, WP), f32), VMEM((8, WP), f32),
-            VMEM((2, WP, WP), f32),
+            VMEM((2, WP, WP), f32), VMEM((8, WP), f32),
+            *Scatter.scratch(D), *Scatter.scratch(D), *Gather.scratch(D),
+            *RingSum.scratch((4, 32, FW)), *RingSum.scratch((4, 32, FW)), DMA((8,)), DMA((3,)),
         ],
-        compiler_params=pltpu.CompilerParams(vmem_limit_bytes=62 << 20),
-        cost_estimate=pl.CostEstimate(flops=2 * G * D * MW, bytes_accessed=30 << 20, transcendentals=0),
-        name="unmix",
-    )(adj_out, w, gates, terms, lab, *saved)
-
-
-def grad_kernel(left, right, left_two, right_two, out):
-    width = right.shape[1]
-    out[:, :width] = tn(left[...], right[...]).astype(bf16)
-    out[:, width:] = tn(left_two[...], right_two[...]).astype(bf16)
-
-
-def grad_call(left, right, left_two, right_two, name):
-    width = right.shape[1] + right_two.shape[1]
-    block = 256
+        compiler_params=pltpu.CompilerParams(collective_id=2, has_side_effects=True, vmem_limit_bytes=(63 << 20) + (900 << 10)),
+        cost_estimate=pl.CostEstimate(flops=30 * G * D * WP, bytes_accessed=100 << 20, transcendentals=0),
+        name="turn",
+    )(back, ff, n2, cots, hid, gu, *saved, w, middle, cot, gains, gates, terms, lab)
+
+
+def close_kernel(
+    part_in, normed_in, both_in, adj_in, mixed_in, extra_in, s1_in, tok, adj_middle, gains, gain_two,
+    in_grad, mix_out, feed_out, gate_out, chan_out, gain_out,
+    part, normed, both, adj_out, mixed, mg, s1f, s1, lastf, last, adj, gp, gp_in, gain_sum, gain_in, *rest,
+):
+    one, fa, fb, ma, mb, na, nb = rest[:6], *(rest[6 + 5 * n : 11 + 5 * n] for n in range(6))
+    m3s, m3r, f3s, f3r, gs, gr, hs, hr, qs, qr, ls, ws = rest[36:]
+    me = Place()
+    loads = [
+        pltpu.make_async_copy(src, dst, ws.at[n])
+        for n, (src, dst) in enumerate(
+            ((part_in, part), (s1_in, s1f), (normed_in, normed), (both_in, both), (adj_in, adj_out),
+             (mixed_in, mixed), (extra_in, mg.at[:, :, :, pl.ds(MW, 128)]))
+        )
+    ]
+    for copy in loads:
+        copy.start()
+    quarter, at = me.dp // 8, me.dp % 8
+    gate_to = (8 * quarter + me.sq, at)
+    gate_self = me.sq == at
+    chan_from = (8 * (me.dp % 2) + me.sq, me.dp // 2)
+    chan_to = (2 * me.sq + me.dp // 8, me.dp % 8)
+    chan_self = jnp.logical_and(chan_from[0] == me.dp, chan_from[1] == me.sq)
+    barrier, count = greet(seq_peers(me) + dp_peers(me))
+
+    @pl.when(jnp.logical_not(gate_self))
+    def _():
+        pl.semaphore_signal(barrier, inc=1, device_id=gate_to, device_id_type=MESH)
+
+    @pl.when(jnp.logical_not(chan_self))
+    def _():
+        pl.semaphore_signal(barrier, inc=1, device_id=chan_from, device_id_type=MESH)
+
+    pl.semaphore_wait(barrier, count + jnp.where(gate_self, 0, 1) + jnp.where(chan_self, 0, 1))
+
+    sent = []
+
+    def push(src, dst, send, recv, device):
+        sent.append(remote(src, dst, send, recv, device))
+        sent[-1].start()
+
+    def arrived(dst, send, recv):
+        remote(dst, dst, send, recv, me.sibling()).wait_recv()
+
+    xs, ys = (me.dp_peer(me.x_dp(1)), me.dp_peer(me.x_dp(3))), (me.dp_peer(me.y_dp(1)), me.dp_peer(me.y_dp(3)))
+    feed_up = RingSum(me, *xs, lambda k, q: s1f.at[0, pl.ds((me.x + k) % 4, 1), pl.ds(q * 32, 32)], *fa)
+    feed_low = RingSum(me, *ys, lambda k, q: s1f.at[1, pl.ds((me.y + k) % 4, 1), pl.ds(q * 32, 32)], *fb)
+    mix_up = RingSum(me, *ys, lambda k, q: mg.at[:, (me.y + k) % 4, pl.ds(q * 32, 32)], *ma)
+    mix_low = RingSum(me, *xs, lambda k, q: mg.at[(me.x + k) % 4, :, pl.ds(HALF + q * 32, 32)], *mb)
+    last_up = RingSum(me, *xs, lambda k, q: s1.at[0, pl.ds((me.x + k) % 4, 1), pl.ds(q * 32, 32)], *na)
+    last_low = RingSum(me, *ys, lambda k, q: s1.at[1, pl.ds((me.y + k) % 4, 1), pl.ds(q * 32, 32)], *nb)
+
+    inner = Scatter(me, part, *one)
+    loads[0].wait()
+    inner.start()
+    loads[1].wait()
+    feed_up.start()
+    feed_low.start()
+    inner.join()
+    for copy in loads[2:]:
+        copy.wait()
+
+    def tile(i, carry):
+        here = pl.ds(pl.multiple_of(i * 256, 256), 256)
+        left = tn(normed[:, here], both[...]).astype(bf16)
+        right = tn(adj_out[:, here], mixed[...]).astype(bf16)
+        for h in range(2):
+            mg[i // 2, i % 2 * 2 + h, :, : 2 * WP] = left[h * T : (h + 1) * T]
+            mg[i // 2, i % 2 * 2 + h, :, 2 * WP : MW] = right[h * T : (h + 1) * T]
+
+        @pl.when(i == 4)
+        def _():
+            inner.relay()
+            feed_up.relay()
+            feed_low.relay()
+
+        return carry
+
+    lax.fori_loop(0, 8, tile, 0)
+    mix_up.start()
+    mix_low.start()
+    inner.finish(adj)
+
+    def pull(i, carry):
+        here = pl.ds(pl.multiple_of(i * 16, 16), 16)
+        pulled, terms = norm_pull(tok[here].astype(f32), gains[0:1], adj[here])
+        in_grad[here] = adj_middle[here] + pulled
+        return carry + jnp.sum(terms, axis=0, keepdims=True)
+
+    gain_one = lax.fori_loop(0, T // 16, pull, jnp.zeros((1, D), f32))
+    gp[...] = jnp.zeros(gp.shape, f32)
+    for k in range(DP):
+        gp[k, 0:1] = gain_one[:, k * 128 : (k + 1) * 128]
+        gp[k, 1:2] = gain_two[:, k * 128 : (k + 1) * 128]
+    for k in range(1, DP):
+        to = (me.dp + k) % DP
+        push(gp.at[to], gp_in.at[k], gs.at[k], gr.at[k], me.dp_peer(to))
+
+    feed_up.finish(lambda q: lastf.at[:, pl.ds(q * 32, 32)])
+    feed_low.finish(lambda q: lastf.at[:, pl.ds(HALF + q * 32, 32)])
+
+    def feed_columns(p, j):
+        return lanes_of(p * FF + j * FL, FL)
+
+    keeps = [
+        pltpu.make_async_copy(
+            lastf.at[0, rows_of(me.sq * 16, 16), pl.ds(p * FL, FL)], feed_out.at[:, feed_columns(p, me.sq)], ls.at[p]
+        )
+        for p in range(3)
+    ]
+    for copy in keeps:
+        copy.start()
+    order = (4, 3, 5, 2, 6, 1, 7)
+    for k in order:
+        to = (me.sq + k) % SEQ
+        for p in range(3):
+            push(lastf.at[0, rows_of(to * 16, 16), pl.ds(p * FL, FL)], feed_out.at[:, feed_columns(p, me.sq)],
+                 f3s.at[p, k], f3r.at[p, k], me.seq_peer(k))
+
+    mix_up.relay()
+    mix_low.relay()
+
+    for k in range(1, DP):
+        arrived(gp_in.at[k], gs.at[k], gr.at[k])
+
+    def sum_gains(k, total):
+        return total + gp_in[k]
+
+    gain_sum[...] = lax.fori_loop(1, DP, sum_gains, gp[me.dp])
+    for k in range(1, SEQ):
+        push(gain_sum, gain_in.at[k], qs.at[k], qr.at[k], me.seq_peer(k))
+
+    mix_up.finish(lambda q: s1.at[0, :, pl.ds(q * 32, 32)])
+    last_up.start()
+    mix_low.finish(lambda q: s1.at[1, :, pl.ds(q * 32, 32)])
+    last_low.start()
+    for k in range(1, SEQ):
+        arrived(gain_in.at[k], qs.at[k], qr.at[k])
+    total = gain_sum[...]
+    for k in range(1, SEQ):
+        total = total + gain_in[k]
+    gain_out[...] = total
+    last_up.relay()
+    last_low.relay()
+    last_up.finish(lambda q: last.at[:, pl.ds(q * 32, 32)])
+    last_low.finish(lambda q: last.at[:, pl.ds(HALF + q * 32, 32)])
+
+    columns = pl.ds(0, MW)
+    keeps.append(pltpu.make_async_copy(last.at[0, rows_of(me.sq * 16, 16), columns], mix_out.at[me.sq], ls.at[3]))
+    keeps[-1].start()
+    for k in order:
+        to = (me.sq + k) % SEQ
+        push(last.at[0, rows_of(to * 16, 16), columns], mix_out.at[me.sq], m3s.at[k], m3r.at[k], me.seq_peer(k))
+    gate_sum, chan_sum = last.at[0, pl.ds(0, 96), pl.ds(MW, 128)], last.at[0, pl.ds(96, 32), pl.ds(MW, 128)]
+    gate_copy = remote(gate_sum, gate_out, hs.at[0], hr.at[0], gate_to)
+    chan_copy = remote(chan_sum, chan_out, hs.at[1], hr.at[1], chan_to)
+    gate_local = pltpu.make_async_copy(gate_sum, gate_out, ls.at[4])
+    chan_local = pltpu.make_async_copy(chan_sum, chan_out, ls.at[5])
+
+    @pl.when(jnp.logical_not(gate_self))
+    def _():
+        gate_copy.start()
+
+    @pl.when(gate_self)
+    def _():
+        gate_local.start()
+
+    @pl.when(jnp.logical_not(chan_self))
+    def _():
+        chan_copy.start()
+
+    @pl.when(chan_self)
+    def _():
+        chan_local.start()
+
+    for k in range(1, SEQ):
+        source = (me.sq - k + SEQ) % SEQ
+        for p in range(3):
+            arrived(feed_out.at[:, feed_columns(p, source)], f3s.at[p, k], f3r.at[p, k])
+        arrived(mix_out.at[source], m3s.at[k], m3r.at[k])
+
+    @pl.when(jnp.logical_not(gate_self))
+    def _():
+        gate_copy.wait()
+
+    @pl.when(gate_self)
+    def _():
+        gate_local.wait()
+
+    @pl.when(jnp.logical_not(chan_self))
+    def _():
+        chan_copy.wait()
+
+    @pl.when(chan_self)
+    def _():
+        chan_local.wait()
+
+    for copy in keeps:
+        copy.wait()
+    for copy in sent:
+        copy.wait_send()
+
+
+def close_call(part, normed, both, adj_out, mixed, extra, s1, tok, adj_middle, gains, gain_two):
+    sds = jax.ShapeDtypeStruct
+    hbm, vmem = pl.BlockSpec(memory_space=ANY), pl.BlockSpec(memory_space=VMEM)
+    wide = MW + 128
     return pl.pallas_call(
-        grad_kernel,
-        grid=(D // block,),
-        out_shape=jax.ShapeDtypeStruct((D, width), bf16),
-        in_specs=[
-            pl.BlockSpec((G, block), lambda i: (0, i)), whole(right.shape),
-            pl.BlockSpec((G, block), lambda i: (0, i)), whole(right_two.shape),
+        close_kernel,
+        out_shape=(
+            sds((T, D), f32), sds((SEQ, 16, MW), bf16), sds((16, 3 * FF), bf16),
+            sds((96, 128), bf16), sds((32, 128), bf16), sds((8, 128), f32),
+        ),
+        in_specs=[hbm] * 7 + [vmem] * 4,
+        out_specs=[vmem] * 6,
+        scratch_shapes=[
+            VMEM((G, D), bf16), VMEM((G, D), bf16), VMEM((G, 2 * WP), bf16), VMEM((G, D), bf16), VMEM((G, WP), bf16),
+            VMEM((4, 4, T, wide), bf16), VMEM((2, 4, HALF, FW), bf16), VMEM((2, 4, HALF, wide), bf16),
+            VMEM((1, T, FW), bf16), VMEM((1, T, wide), bf16), VMEM((T, D), f32),
+            VMEM((DP, 8, 128), f32), VMEM((DP, 8, 128), f32), VMEM((8, 128), f32), VMEM((SEQ, 8, 128), f32),
+            *Scatter.scratch(D),
+            *RingSum.scratch((1, 32, FW)), *RingSum.scratch((1, 32, FW)),
+            *RingSum.scratch((4, 32, wide)), *RingSum.scratch((4, 32, wide)),
+            *RingSum.scratch((1, 32, wide)), *RingSum.scratch((1, 32, wide)),
+            DMA((8,)), DMA((8,)), DMA((3, 8)), DMA((3, 8)), DMA((DP,)), DMA((DP,)), DMA((2,)), DMA((2,)),
+            DMA((SEQ,)), DMA((SEQ,)), DMA((6,)), DMA((7,)),
         ],
-        out_specs=pl.BlockSpec((block, width), lambda i: (i, 0)),
-        compiler_params=pltpu.CompilerParams(vmem_limit_bytes=62 << 20),
-        cost_estimate=pl.CostEstimate(flops=2 * G * D * width, bytes_accessed=20 << 20, transcendentals=0),
-        name=name,
-    )(left, right, left_two, right_two)
+        compiler_params=pltpu.CompilerParams(collective_id=4, has_side_effects=True, vmem_limit_bytes=62 << 20),
+        cost_estimate=pl.CostEstimate(flops=5 * G * D * WP, bytes_accessed=100 << 20, transcendentals=0),
+        name="close",
+    )(part, normed, both, adj_out, mixed, extra, s1, tok, adj_middle, gains, gain_two)
 
 
 def shards(tokens, segments, mixer_weights, norm_gains, gate_weights, channel_terms, feed_weights, cotangent):
@@ -1306,21 +1344,21 @@
         cot_all, w, normed, *saved, mixed, hidden, adj_gu, back_part, feed_part, norm_two,
         gates, terms, gains, lab, middle,
     ) = forward_call(tokens, cotangent, mix, feed_weights, small, gate_block, chan_block)
-    feed_grad = grad_call(norm_two, adj_gu, cot_all, hidden, "feedgrad")
-    feed_sum = lax.psum_scatter(feed_grad, "dp", scatter_dimension=0, tiled=True)
-    adj_middle, gain_two, adj_all = turn_call(back_part, middle, cotangent, gains[1:2])
-    both, in_part, gate_grad, sums = unmix_call(adj_all, w, gates, terms, lab, saved)
-    input_gradient, activations, mix_out, gate_out, chan_out, gain_out = close_call(
-        in_part, feed_part, normed, both, adj_all, mixed, gate_grad, sums, tokens,
-        adj_middle, middle, gains[0:1], gain_two,
+    adj_all, s1, both, in_part, adj_middle, activations, gain_two, extra = turn_call(
+        back_part, feed_part, norm_two, cot_all, hidden, adj_gu, saved, w, middle, cotangent, gains, gates, terms, lab
     )
-    feed_out = swap_call(feed_sum.reshape(SEQ, 16, FW), 5, "swap")
+    input_gradient, mix_out, feed_out, gate_out, chan_out, gain_out = close_call(
+        in_part, normed, both, adj_all, mixed, extra.reshape(4, 4, 128, 128), s1, tokens, adj_middle, gains, gain_two
+    )
     mixer_gradient = (
         mix_out.reshape(SEQ, 16, 3, WP)[..., :WL].transpose(1, 2, 0, 3).reshape(16, 3 * W).astype(f32)
     )
-    feed_gradient = feed_out.reshape(SEQ, 16, 3, FL).transpose(1, 2, 0, 3).reshape(16, 3 * FF).astype(f32)
-    gate_gradient = jnp.where(sq < 4, gate_out[:40, :BW], gate_out[:40, BW : 2 * BW])
-    channel_gradient = lax.dynamic_slice(chan_out, (0, piece * 20), (8, 20)).T
+    feed_gradient = feed_out.astype(f32)
+    gate_out = jnp.concatenate([gate_out[:40], gate_out[48:88]], 1).astype(f32)
+    gate_gradient = jnp.where(sq < 4, gate_out[:, :BW], gate_out[:, BW - 128 : 2 * BW - 128])
+    chan_out = jnp.concatenate([chan_out[:8], chan_out[16:24]], 1).astype(f32)
+    window = jnp.minimum(piece * 20 // 128, 1) * 128
+    channel_gradient = lax.dynamic_slice(chan_out, (0, piece * 20 - window), (8, 20)).T
     gain_gradient = lax.dynamic_slice(gain_out, (0, sq * 16), (2, 16)).T
     return (activations, input_gradient, mixer_gradient, gain_gradient, gate_gradient, channel_gradient, feed_gradient)
 

time: 344 us -> 289 us (0.84); the launches traced: 338 us -> 289 us
  Pallas kernels: 302 us -> 271 us
  between operations: 14.7 us -> 0.82 us
  local copies, waits for them, and re-layouts: 16 us -> 10.7 us
    pallas_call x5 -> x2, Pallas kernels: 166 us -> 135 us  [the longest x1 74 us: turn_call(): pl.pallas_call(turn_kernel, out_shape=(sds((G, D), bf16), sds((2, 4, HALF...]
  transfers between devices with their start and end apart: 1 -> 0, of which waited for: 0 -> 0; matrix products, arithmetic and copies ran while one was open for 2% -> 0% of each run, Pallas kernels for 41% -> 0%
where the time goes in v4:
time: 289 us
  Pallas kernels  271 us (94%)
  local copies, waits for them, and re-layouts  10.7 us (4%)
  other arithmetic  6.69 us (2%)
    pallas_call x1, Pallas kernels, forward_call(): pl.pallas_call(forward_kernel, out_shape=(sds((G, D), bf16), sds((D, MW),...  136 us
    pallas_call x1, Pallas kernels, turn_call(): pl.pallas_call(turn_kernel, out_shape=(sds((G, D), bf16), sds((2, 4, HALF...  74 us
    pallas_call x1, Pallas kernels, close_call(): pl.pallas_call(close_kernel, out_shape=(sds((T, D), f32), sds((SEQ, 16, M...  60.7 us

profile of v4, /device:TPU:1, one launch (start us, length us, event | category | flops | bytes accessed | tf_op | source)
XLA Modules:
  0.0 289.0 jit_solution(16723737268342066510)
XLA Ops:
  0.7 0.7 convert_bitcast_fusion.3
  1.4 0.7 convert_bitcast_fusion.1
  2.1 0.7 tile.4
  2.8 0.1 tile.10
  2.9 0.6 fusion.2.small
  3.5 0.6 dynamic_update_slice.3
  4.1 0.6 pad_maximum_fusion.1.chan
  4.7 0.9 pad_select_fusion
  5.6 0.6 pad_maximum_fusion.gates
  6.2 1.2 reshape.33
  7.4 0.2 copy.18
  7.5 0.2 pad_bitcast_fusion
  7.7 1.0 reshape.34.mix
  8.7 136.1 %forward.1 = (bf16[1024,2048]{1,0:T(8,128)(2,1)}, bf16[2048,1152]{1,0:T(8,128)(2,1)}, bf16[1024,2048]{1,0:T(8,128)(2,1)}, f32[1024,384]{1,0:T(8,128)}, f32[1024,...) custom-call(bf16[128,2048]{1,0:T(8,128)(2,1)} %tok.3, ...), custom_call_target="tpu_custom_call" | custom-call | flops 24159191040 | bytes 104857600 | tf_op jit(solution)/shard_map/forward/pallas_call | solution.py:839
  144.8 74.0 %turn.1 = (bf16[1024,2048]{1,0:T(8,128)(2,1)}, bf16[2,4,64,2304]{3,2,1,0:T(8,128)(2,1)}, bf16[1024,768]{1,0:T(8,128)(2,1)}, bf16[1024,2048]{1,0:T(8,128)(2,1)}, ...) custom-call(bf16[1024,2048]{1,0:T(8,128)(2,1)} %get-tuple-element.39.back_in, ...), custom_call_target="tpu_custom_call" | custom-call | flops 24159191040 | bytes 104857600 | tf_op jit(solution)/shard_map/turn/pallas_call | solution.py:1065
  218.8 60.7 %close.1 = (f32[128,2048]{1,0:T(8,128)}, bf16[8,16,1152]{2,1,0:T(8,128)(2,1)}, bf16[16,18432]{1,0:T(8,128)(2,1)}, bf16[96,128]{1,0:T(8,128)(2,1)}, bf16[32,128]{1,0:T(8,128)(2,1)}, /*index=5*/f32[8,128]{1,0:T(8,128)}) custom-call(bf16[1024,2048]{1,0:T(8,128)(2,1)} %get-tuple-element.56.part_in, bf16[1024,2048]{1,0:T(8,128)(2,1)} %get-tuple-element.57.normed_in, ...), custom_call_target="tpu_custom_call" | custom-call | flops 4026531840 | bytes 104857600 | tf_op jit(solution)/shard_map/close/pallas_call | solution.py:1294
  279.5 0.0 copy-start.1
  279.5 1.4 dynamic-slice_bitcast_fusion
  280.8 0.7 fusion.10
  281.5 0.7 convert_bitcast_fusion.2
  282.2 0.7 fusion.7
  282.9 0.7 slice_select_fusion
  283.6 1.0 reshape.36
  284.7 0.0 copy-start
  284.7 0.1 convert_bitcast_fusion
  284.8 0.3 copy.19
  285.2 0.9 reshape.37
  286.1 0.0 copy-done.1
  286.1 1.1 convert_element_type.57
  287.2 0.0 copy-done.2
  287.2 0.8 copy.23
  288.0 1.0 copy.24
  (14 shorter events, 0.1 us)
Async XLA Ops:
  279.5 6.7 %copy-start.1 = (bf16[16,18432]{1,0:T(8,128)(2,1)S(1)}, bf16[16,18432]{1,0:T(8,128)(2,1)}, u32[]{:S(2)}) copy-start(bf16[16,18432]{1,0:T(8,128)(2,1)} %get-tuple-element.70) | copy-start | bytes 1769476
  282.9 4.3 %copy-start.2 = (bf16[128,2048]{1,0:T(8,128)(2,1)S(1)}, bf16[128,2048]{1,0:T(8,128)(2,1)}, u32[]{:S(2)}) copy-start(bf16[128,2048]{1,0:T(8,128)(2,1)} %get-tuple-element.91) | copy-start | bytes 1572868
  284.7 3.3 %copy-start = (f32[128,2048]{1,0:T(8,128)S(1)}, f32[128,2048]{1,0:T(8,128)}, u32[]{:S(2)}) copy-start(f32[128,2048]{1,0:T(8,128)} %get-tuple-element.92) | copy-start | bytes 3145732

commit v5 on v4

--- a/solution.py
+++ b/solution.py
@@ -103,7 +103,6 @@
     def __init__(self, me, own, out, full, send, recv, keep):
         self.me, self.own, self.out, self.full = me, own, out, full
         self.send, self.recv, self.keep = send, recv, keep
-        self.sent, self.kept = [], []
 
     def block(self, k, c, half=None):
         base = self.me.slot(k, c) * T
@@ -112,20 +111,19 @@
         return self.full.at[pl.ds(pl.multiple_of(base + half * HALF, HALF), HALF)]
 
     def push(self, n, src, dst, device):
-        copy = remote(src, dst, self.send.at[n], self.recv.at[n], device)
-        copy.start()
-        self.sent.append(copy)
+        remote(src, dst, self.send.at[n], self.recv.at[n], device).start()
 
     def arrived(self, n, dst):
         remote(dst, dst, self.send.at[n], self.recv.at[n], self.me.sibling()).wait_recv()
 
-    def store(self, k, c):
-        if self.out is None:
-            return
+    def kept(self, k, other):
+        c = 1 - self.me.c if other else self.me.c
         there = self.out.at[pl.ds(pl.multiple_of(self.me.slot(k, c) * T, T), T)]
-        copy = pltpu.make_async_copy(self.block(k, c), there, self.keep.at[len(self.kept)])
-        copy.start()
-        self.kept.append(copy)
+        return pltpu.make_async_copy(self.block(k, c), there, self.keep.at[2 * k + other])
+
+    def store(self, k, other):
+        if self.out is not None:
+            self.kept(k, other).start()
 
     def start(self):
         me = self.me
@@ -137,7 +135,7 @@
         self.push(2, b, b, right)
         self.push(3, a, a, left)
         self.push(4, mine, mine, me.sibling())
-        self.store(0, me.c)
+        self.store(0, 0)
 
     def forward(self):
         me = self.me
@@ -151,7 +149,7 @@
     def hand_over(self, n, k):
         whole = self.block(k, self.me.c)
         self.push(n, whole, whole, self.me.sibling())
-        self.store(k, self.me.c)
+        self.store(k, 0)
 
     def across_left(self):
         self.arrived(2, self.block(3, self.me.c, 1))
@@ -173,7 +171,7 @@
 
     def taken(self, n, k):
         self.arrived(n, self.block(k, 1 - self.me.c))
-        self.store(k, 1 - self.me.c)
+        self.store(k, 1)
 
     def own_pair(self):
         self.taken(4, 0)
@@ -188,10 +186,14 @@
         self.taken(9, 2)
 
     def drain(self):
-        for copy in self.sent:
-            copy.wait_send()
-        for copy in self.kept:
-            copy.wait()
+        for n in range(10):
+            part = n in (0, 1, 2, 3, 5, 6)
+            size = self.block(0, self.me.c, 0) if part else self.block(0, self.me.c)
+            remote(size, size, self.send.at[n], self.recv.at[n], self.me.sibling()).wait_send()
+        if self.out is not None:
+            for k in range(4):
+                self.kept(k, 0).wait()
+                self.kept(k, 1).wait()
 
     def finish(self):
         self.own_pair()
@@ -508,12 +510,18 @@
     return (here == there).astype(f32)
 
 
+def log_one_plus(x):
+    z = x / (2.0 + x)
+    s = z * z
+    return 2.0 * z * (1.0 + s * (1 / 3 + s * (1 / 5 + s * (1 / 7 + s * (1 / 9 + s * (1 / 11 + s * (1 / 13)))))))
+
+
 def forward_kernel(
-    tok, cot, mix, feed, small, gates, chan,
+    tok, cot, mixer, feed, numbers, gain_in, gate_in, chan_in,
     cot_out, mix_out, normed_out, x_out, y_out, conv_out, prior_out, mixed_out,
     hidden_out, gu_out, back_out, ff_out, n2_out, gate_out, term_out, gain_out, lab_out, middle,
     mixw, feedw, part, xs, ys, convs, priors, mixeds, hiddens, gus,
-    small_in, minor, gate_f,
+    mix, small, gates, chan, small_in, minor, gate_f,
     xpad, dec, drv, sts, carry, *rest,
 ):
     tg, cg, ng, sc = rest[:4], rest[4:8], rest[8:12], rest[12:18]
@@ -544,14 +552,37 @@
     local = [
         pltpu.make_async_copy(tok, tokg.at[rows_of(me.sq * T, T)], ls.at[0]),
         pltpu.make_async_copy(cot, cotg.at[rows_of(me.sq * T, T)], ls.at[1]),
-        pltpu.make_async_copy(mix.at[me.sq], mixw.at[own_rows], ls.at[2]),
-        pltpu.make_async_copy(small, small_in.at[me.sq], ls.at[3]),
     ] + [
         pltpu.make_async_copy(feed.at[:, feed_columns(p, me.sq)], feedw.at[own_rows, pl.ds(p * FL, FL)], ls.at[4 + p])
         for p in range(3)
     ]
     for copy in local:
         copy.start()
+
+    for j in range(SEQ):
+        for p in range(3):
+            value = mixer[:, p * W + j * WL : p * W + (j + 1) * WL]
+            mix[j, :, p * WP : (p + 1) * WP] = jnp.concatenate([value, jnp.zeros((16, WP - WL), bf16)], 1)
+    row = jnp.concatenate([gain_in[...].astype(f32), jnp.zeros((2, 112), f32)], 1)
+    row = pltpu.roll(row, me.sq * 16, 1)
+    small[0:16] = jnp.concatenate([row, jnp.zeros((14, 128), f32)], 0).astype(bf16)
+    small[16:32] = jnp.concatenate([numbers[...].astype(f32), jnp.zeros((15, 128), f32)], 0).astype(bf16)
+    value = gate_in[...].astype(f32)
+    value = jnp.where(
+        me.sq < 4,
+        jnp.concatenate([value, jnp.zeros((40, 256 - BW), f32)], 1),
+        jnp.concatenate([jnp.zeros((40, BW - 128), f32), value, jnp.zeros((40, 384 - 2 * BW), f32)], 1),
+    )
+    for n in range(2):
+        half = jnp.concatenate([value[:, n * 128 : n * 128 + 128], jnp.zeros((8, 128), f32)], 0)
+        gates[n * 48 : n * 48 + 48] = half.astype(bf16)
+    value = jnp.concatenate([chan_in[...].astype(f32), jnp.zeros((8, WP - 20), f32)], 1)
+    value = pltpu.roll(value, (8 * (me.dp % 2) + me.sq) * 20, 1)
+    for n in range(3):
+        part_rows = jnp.concatenate([value[:, n * 128 : n * 128 + 128], jnp.zeros((8, 128), f32)], 0)
+        chan[n * 16 : n * 16 + 16] = part_rows.astype(bf16)
+    mixw[own_rows] = mix[me.sq]
+    small_in[me.sq] = small[...]
 
     pl.semaphore_wait(barrier, count + jnp.where(gate_self, 0, 1) + jnp.where(chan_self, 0, 1))
 
@@ -610,13 +641,9 @@
     def seq_rows(k):
         return rows_of(me.dp * T + (me.sq - k + SEQ) % SEQ * 16, 16)
 
-    for k in range(1, SEQ):
-        arrived(mixw.at[seq_rows(k)], ms.at[k], mr.at[k])
-
     mixes = Spread(me, mixw, T, ps, pr)
     feeds = Spread(me, feedw, T, qs, qr)
     minors = Spread(me, minor, MINOR, es, er)
-    mixes.start()
 
     for k in range(1, SEQ):
         arrived(small_in.at[(me.sq - k + SEQ) % SEQ], ss.at[k], sr.at[k])
@@ -645,13 +672,10 @@
         chan_local.wait()
 
     minors.start()
+    for k in range(1, SEQ):
+        arrived(mixw.at[seq_rows(k)], ms.at[k], mr.at[k])
+    mixes.start()
     tokens.forward()
-    mixes.turn()
-    minors.turn()
-    cots = Gather(me, None, cot_out, *cg)
-    cots.start()
-    mixes.far()
-    minors.far()
 
     lab_out[0:8] = jnp.full((8, 128), -1.0, f32)
     lab_out[G + 8 :] = jnp.full((8, 128), -2.0, f32)
@@ -659,31 +683,71 @@
         row = small_in[k, 16:32].astype(f32)[0:1]
         lab_out[8 + k * T : 8 + (k + 1) * T] = jnp.broadcast_to(row, (128, 128)).T
 
-    tokens.across()
-    for t in range(3):
-        mixes.hand_on(t)
+    minors.turn()
+    mixes.turn()
+    cots = Gather(me, None, cot_out, *cg)
+    cots.start()
+    minors.far()
+    mixes.far()
+    tokens.across_left()
+    tokens.across_right()
+    for t in range(4):
         minors.hand_on(t)
-    minors.hand_on(3)
+    mixes.hand_on(0)
+    tokens.across_far()
+    minors.finish()
+    for k in range(DP):
+        gain_out[:, k * 128 : (k + 1) * 128] = minor[k * MINOR : k * MINOR + 16].astype(f32)[0:8]
+
+    def normed_copy(k, other):
+        c = 1 - me.c if other else me.c
+        rows = rows_of(me.slot(k, c) * T, T)
+        return pltpu.make_async_copy(part.at[rows], normed_out.at[rows], os.at[23 + 2 * k + other])
+
+    def normalise(k, other):
+        base = me.slot(k, 1 - me.c if other else me.c) * T
+
+        def body(i, c):
+            here = rows_of(base + i * 16, 16)
+            part[here] = norm_rows(tokg[here].astype(f32), gain_out[0:1]).astype(bf16)
+            return c
+
+        lax.fori_loop(0, T // 16, body, 0)
+        normed_copy(k, other).start()
+
+    normalise(0, 0)
+    tokens.own_pair()
+    normalise(0, 1)
+    mixes.hand_on(1)
+    mixes.hand_on(2)
+    normalise(3, 0)
+    normalise(1, 0)
+    tokens.left_pair()
+    normalise(3, 1)
+    tokens.right_pair()
+    normalise(1, 1)
     mixes.hand_on(3)
     for k in range(1, SEQ):
         for p in range(3):
             arrived(feedw.at[seq_rows(k), pl.ds(p * FL, FL)], fs.at[p, k], fr.at[p, k])
     feeds.start()
-    tokens.finish()
-    minors.finish()
+    normalise(2, 0)
+    tokens.far_pair()
+    normalise(2, 1)
+    tokens.drain()
     terms = minor[112:160].astype(f32)
     for k in range(1, DP):
         terms = terms + minor[k * MINOR + 112 : k * MINOR + 160].astype(f32)
     for n in range(3):
         group = terms[16 * n : 16 * n + 16]
         lanes = slice(128 * n, 128 * n + 128)
-        lane = lax.broadcasted_iota(jnp.int32, (1, 128), 1) + 128 * n
         term_out[:, lanes] = group
-        term_out[7:8, lanes] = jnp.where(lane >= WL, -1.0, group[7:8] + group[9:10])
-        term_out[8:9, lanes] = group[8:9] + group[10:11]
+        lam = group[7:8]
+        small_exp = jnp.exp(-jnp.abs(lam))
+        term_out[7:8, lanes] = -rate_scale * (jnp.maximum(-lam, 0.0) + log_one_plus(small_exp))
+        term_out[8:9, lanes] = rate_scale * jax.nn.sigmoid(-lam)
     gate_f[...] = jnp.zeros(gate_f.shape, f32)
     for k in range(DP):
-        gain_out[:, k * 128 : (k + 1) * 128] = minor[k * MINOR : k * MINOR + 16].astype(f32)[0:8]
         base = k // 8 * WP + k % 8 * 40
         for n in range(2):
             lanes = k % 8 // 4 * 128 + n * 128
@@ -691,20 +755,12 @@
             gate_f[base : base + 40, lanes : lanes + 128] = minor[start : start + 48].astype(f32)[0:40]
     gate_out[0] = gate_f[:WP].astype(bf16)
     gate_out[1] = gate_f[WP:].astype(bf16)
-
-    def normalise(i, c):
-        here = pl.ds(pl.multiple_of(i * 16, 16), 16)
-        tokg[here] = norm_rows(tokg[here].astype(f32), gain_out[0:1]).astype(bf16)
-        return c
-
-    lax.fori_loop(0, G // 16, normalise, 0)
-    writes = [pltpu.make_async_copy(tokg, normed_out, os.at[0])]
+    for k in range(4):
+        normed_copy(k, 0).wait()
+        normed_copy(k, 1).wait()
+    mixes.finish()
+    writes = [pltpu.make_async_copy(mixw, mix_out, os.at[1])]
     writes[0].start()
-    cots.forward()
-    cots.across()
-    mixes.finish()
-    writes.append(pltpu.make_async_copy(mixw, mix_out, os.at[1]))
-    writes[1].start()
 
     xpad[0:8] = jnp.zeros((8, WP), f32)
     carry[...] = jnp.zeros((8, WP), f32)
@@ -713,6 +769,7 @@
     def mix_chunk(step, c):
         @pl.when(step == 1)
         def _():
+            cots.forward()
             feeds.turn()
 
         @pl.when(step == 2)
@@ -721,11 +778,12 @@
 
         @pl.when(step == 3)
         def _():
+            cots.across()
             feeds.hand_on(0)
 
         base = step * CHUNK
         rows = rows_of(base, CHUNK)
-        both = nn(tokg[rows], mixw[:, : 2 * WP])
+        both = nn(part[rows], mixw[:, : 2 * WP])
         x, y = both[:, :WP], both[:, WP:]
         xs[rows] = x
         ys[rows] = y
@@ -785,7 +843,6 @@
     seconds = Gather(me, None, n2_out, *ng)
     seconds.start()
     cots.finish()
-    writes[0].wait()
     feeds.finish()
 
     def feed_chunk(k, n):
@@ -824,7 +881,7 @@
     feed_chunk(2, 3)
     feed_store(2, 3)
     seconds.drain()
-    for copy in writes[1:]:
+    for copy in writes:
         copy.wait()
     for copy in sent:
         copy.wait_send()
@@ -833,7 +890,7 @@
     feeds.drain()
 
 
-def forward_call(tok, cot, mix, feed, small, gates, chan):
+def forward_call(tok, cot, mixer, feed, numbers, gain, gates, chan):
     sds = jax.ShapeDtypeStruct
     hbm, vmem = pl.BlockSpec(memory_space=ANY), pl.BlockSpec(memory_space=VMEM)
     return pl.pallas_call(
@@ -844,24 +901,25 @@
             sds((G, FL), bf16), sds((G, 2 * FL), bf16), sds((G, D), bf16), sds((G, D), bf16), sds((G, D), bf16),
             sds((2, WP, WP), bf16), sds((16, WP), f32), sds((8, D), f32), sds((G + 16, 128), f32), sds((T, D), f32),
         ),
-        in_specs=[vmem, hbm, hbm, hbm, vmem, vmem, vmem],
+        in_specs=[vmem, hbm, vmem, hbm, vmem, vmem, vmem, vmem],
         out_specs=[hbm] * 13 + [vmem] * 5,
         scratch_shapes=[
             VMEM((D, MW), bf16), VMEM((D, FW), bf16), VMEM((G, D), bf16),
             VMEM((G, WP), f32), VMEM((G, WP), f32), VMEM((G, WP), f32), VMEM((G, WP), f32), VMEM((G, WP), bf16),
             VMEM((G, FL), bf16), VMEM((G, 2 * FL), bf16),
+            VMEM((SEQ, 16, MW), bf16), VMEM((32, 128), bf16), VMEM((96, 128), bf16), VMEM((48, 128), bf16),
             VMEM((SEQ, 32, 128), bf16), VMEM((DP * MINOR, 128), bf16), VMEM((2 * WP, WP), f32),
             VMEM((CHUNK + 8, WP), f32), VMEM((CHUNK, WP), f32), VMEM((CHUNK, WP), f32), VMEM((CHUNK, WP), f32),
             VMEM((8, WP), f32),
             *Gather.scratch(D), *Gather.scratch(D), *Gather.scratch(D), *Scatter.scratch(D),
             DMA((SEQ,)), DMA((SEQ,)), DMA((3, SEQ)), DMA((3, SEQ)), DMA((SEQ,)), DMA((SEQ,)),
             DMA((40,)), DMA((40,)), DMA((40,)), DMA((40,)), DMA((40,)), DMA((40,)),
-            DMA((2,)), DMA((2,)), DMA((9,)), DMA((23,)),
+            DMA((2,)), DMA((2,)), DMA((9,)), DMA((31,)),
         ],
         compiler_params=pltpu.CompilerParams(collective_id=1, has_side_effects=True, vmem_limit_bytes=(63 << 20) + (900 << 10)),
         cost_estimate=pl.CostEstimate(flops=30 * G * D * WP, bytes_accessed=100 << 20, transcendentals=0),
         name="forward",
-    )(tok, cot, mix, feed, small, gates, chan)
+    )(tok, cot, mixer, feed, numbers, gain, gates, chan)
 
 
 def turn_kernel(
@@ -1317,50 +1375,63 @@
     )(part, normed, both, adj_out, mixed, extra, s1, tok, adj_middle, gains, gain_two)
 
 
+def finish_kernel(mix, feed, gate, chan, gain, mix_out, feed_out, gate_out, chan_out, gain_out):
+    me = Place()
+    for p in range(3):
+        for j in range(SEQ):
+            value = mix[j, :, p * WP : (p + 1) * WP].astype(f32)
+            mix_out[:, p * W + j * WL : p * W + (j + 1) * WL] = value[:, :WL]
+
+    def widen(i, c):
+        here = lanes_of(i * 2048, 2048)
+        feed_out[:, here] = feed[:, here].astype(f32)
+        return c
+
+    lax.fori_loop(0, 9, widen, 0)
+    value = jnp.concatenate([gate[0:48].astype(f32)[0:40], gate[48:96].astype(f32)[0:40]], 1)
+    gate_out[...] = jnp.where(me.sq < 4, value[:, :BW], value[:, BW - 128 : 2 * BW - 128])
+    value = jnp.concatenate([chan[0:16].astype(f32)[0:8], chan[16:32].astype(f32)[0:8]], 1)
+    first = (8 * (me.dp % 2) + me.sq) * 20
+    first = first - jnp.where(first >= 128, 128, 0)
+    chan_out[...] = pltpu.roll(value, (256 - first) % 256, 1)[:, :20]
+    gain_out[...] = pltpu.roll(gain[...], (128 - me.sq * 16) % 128, 1)[0:2, 0:16]
+
+
+def finish_call(mix, feed, gate, chan, gain):
+    sds = jax.ShapeDtypeStruct
+    vmem = pl.BlockSpec(memory_space=VMEM)
+    return pl.pallas_call(
+        finish_kernel,
+        out_shape=(
+            sds((16, 3 * W), f32), sds((16, 3 * FF), f32),
+            sds((40, BW), f32), sds((8, 20), f32), sds((2, 16), f32),
+        ),
+        in_specs=[vmem] * 5,
+        out_specs=[vmem] * 5,
+        compiler_params=pltpu.CompilerParams(vmem_limit_bytes=62 << 20),
+        name="finish",
+    )(mix, feed, gate, chan, gain)
+
+
 def shards(tokens, segments, mixer_weights, norm_gains, gate_weights, channel_terms, feed_weights, cotangent):
-    dp, sq = lax.axis_index("dp"), lax.axis_index("seq")
-    mix = jnp.pad(mixer_weights.reshape(16, 3, SEQ, WL), ((0, 0), (0, 0), (0, 0), (0, WP - WL)))
-    mix = mix.transpose(2, 0, 1, 3).reshape(SEQ, 16, MW)
-    lane = lax.broadcasted_iota(jnp.int32, (2, 128), 1)
-    gain_rows = jnp.where(lane // 16 == sq, jnp.tile(norm_gains.T, (1, SEQ)), jnp.zeros((), bf16))
-    small = jnp.concatenate(
-        [jnp.pad(gain_rows, ((0, 14), (0, 0))), jnp.pad(segments.astype(bf16)[None], ((0, 15), (0, 0)))], 0
-    )
-    gate_block = jnp.where(
-        sq < 4,
-        jnp.pad(gate_weights, ((0, 8), (0, 256 - BW))),
-        jnp.pad(gate_weights, ((0, 8), (BW - 128, 2 * 128 - 2 * BW + 128))),
-    )
-    gate_block = jnp.concatenate([gate_block[:, :128], gate_block[:, 128:]], 0)
-    channel = channel_terms.T.astype(f32)
-    lam = channel[7:8]
-    derived = jnp.concatenate([-rate_scale * jax.nn.softplus(-lam), rate_scale * jax.nn.sigmoid(-lam)], 0)
-    coarse = lax.optimization_barrier(derived.astype(bf16)).astype(f32)
-    columns = jnp.concatenate([channel[:7], coarse, derived - coarse], 0)
-    piece = 8 * (dp % 2) + sq
-    chan_block = lax.dynamic_update_slice(jnp.zeros((16, WP), f32), columns, (0, piece * 20)).astype(bf16)
-    chan_block = jnp.concatenate([chan_block[:, n * 128 : n * 128 + 128] for n in range(3)], 0)
     (
         cot_all, w, normed, *saved, mixed, hidden, adj_gu, back_part, feed_part, norm_two,
         gates, terms, gains, lab, middle,
-    ) = forward_call(tokens, cotangent, mix, feed_weights, small, gate_block, chan_block)
+    ) = forward_call(
+        tokens, cotangent, mixer_weights, feed_weights, segments[None], norm_gains.T, gate_weights, channel_terms.T
+    )
     adj_all, s1, both, in_part, adj_middle, activations, gain_two, extra = turn_call(
         back_part, feed_part, norm_two, cot_all, hidden, adj_gu, saved, w, middle, cotangent, gains, gates, terms, lab
     )
     input_gradient, mix_out, feed_out, gate_out, chan_out, gain_out = close_call(
         in_part, normed, both, adj_all, mixed, extra.reshape(4, 4, 128, 128), s1, tokens, adj_middle, gains, gain_two
     )
-    mixer_gradient = (
-        mix_out.reshape(SEQ, 16, 3, WP)[..., :WL].transpose(1, 2, 0, 3).reshape(16, 3 * W).astype(f32)
+    mixer_gradient, feed_gradient, gate_gradient, channel_gradient, gain_gradient = finish_call(
+        mix_out, feed_out, gate_out, chan_out, gain_out
     )
-    feed_gradient = feed_out.astype(f32)
-    gate_out = jnp.concatenate([gate_out[:40], gate_out[48:88]], 1).astype(f32)
-    gate_gradient = jnp.where(sq < 4, gate_out[:, :BW], gate_out[:, BW - 128 : 2 * BW - 128])
-    chan_out = jnp.concatenate([chan_out[:8], chan_out[16:24]], 1).astype(f32)
-    window = jnp.minimum(piece * 20 // 128, 1) * 128
-    channel_gradient = lax.dynamic_slice(chan_out, (0, piece * 20 - window), (8, 20)).T
-    gain_gradient = lax.dynamic_slice(gain_out, (0, sq * 16), (2, 16)).T
-    return (activations, input_gradient, mixer_gradient, gain_gradient, gate_gradient, channel_gradient, feed_gradient)
+    return (
+        activations, input_gradient, mixer_gradient, gain_gradient.T, gate_gradient, channel_gradient.T, feed_gradient
+    )
 
 
 def solution(mesh):

time: 289 us -> 273 us (0.945)
  local copies, waits for them, and re-layouts: 10.7 us -> 3.09 us
  other arithmetic: 6.69 us -> 0 us
    pallas_call x1, Pallas kernels: 136 us -> 131 us  [forward_call(): pl.pallas_call(forward_kernel, out_shape=(sds((G, D), bf16), sds((D, MW),...]
    reshape x4 -> x0, local copies, waits for them, and re-layouts: 3.35 us -> none  [the longest x2 1.34 us: shards(): mixer_weights.reshape(16, 3, SEQ, WL)]
where the time goes in v5:
time: 273 us
  Pallas kernels  269 us (99%)
  local copies, waits for them, and re-layouts  3.09 us (1%)
    pallas_call x1, Pallas kernels, forward_call(): pl.pallas_call(forward_kernel, out_shape=(sds((G, D), bf16), sds((D, MW),...  131 us
    pallas_call x1, Pallas kernels, turn_call(): pl.pallas_call(turn_kernel, out_shape=(sds((G, D), bf16), sds((2, 4, HALF...  74.3 us
    pallas_call x1, Pallas kernels, close_call(): pl.pallas_call(close_kernel, out_shape=(sds((T, D), f32), sds((SEQ, 16, M...  61.1 us

profile of v5, /device:TPU:1, one launch (start us, length us, event | category | flops | bytes accessed | tf_op | source)
XLA Modules:
  0.0 272.7 jit_solution(15714668679764335956)
XLA Ops:
  0.6 131.1 %forward.1 = (bf16[1024,2048]{1,0:T(8,128)(2,1)}, bf16[2048,1152]{1,0:T(8,128)(2,1)}, bf16[1024,2048]{1,0:T(8,128)(2,1)}, f32[1024,384]{1,0:T(8,128)}, f32[1024,...) custom-call(bf16[128,2048]{1,0:T(8,128)(2,1)} %tok.3, ...), custom_call_target="tpu_custom_call" | custom-call | flops 24159191040 | bytes 104857600 | tf_op jit(solution)/shard_map/forward/pallas_call | solution.py:896
  131.7 74.3 %turn.1 = (bf16[1024,2048]{1,0:T(8,128)(2,1)}, bf16[2,4,64,2304]{3,2,1,0:T(8,128)(2,1)}, bf16[1024,768]{1,0:T(8,128)(2,1)}, bf16[1024,2048]{1,0:T(8,128)(2,1)}, ...) custom-call(bf16[1024,2048]{1,0:T(8,128)(2,1)} %get-tuple-element.44.back_in, ...), custom_call_target="tpu_custom_call" | custom-call | flops 24159191040 | bytes 104857600 | tf_op jit(solution)/shard_map/turn/pallas_call | solution.py:1123
  206.0 0.0 copy-start
  206.0 61.1 %close.1 = (f32[128,2048]{1,0:T(8,128)}, bf16[8,16,1152]{2,1,0:T(8,128)(2,1)}, bf16[16,18432]{1,0:T(8,128)(2,1)}, bf16[96,128]{1,0:T(8,128)(2,1)}, bf16[32,128]{1,0:T(8,128)(2,1)}, /*index=5*/f32[8,128]{1,0:T(8,128)}) custom-call(bf16[1024,2048]{1,0:T(8,128)(2,1)} %get-tuple-element.61.part_in, bf16[1024,2048]{1,0:T(8,128)(2,1)} %get-tuple-element.62.normed_in, ...), custom_call_target="tpu_custom_call" | custom-call | flops 4026531840 | bytes 104857600 | tf_op jit(solution)/shard_map/close/pallas_call | solution.py:1352
  267.1 2.6 finish.1
  269.7 0.0 copy-done
  269.7 0.8 copy.17
  270.5 2.3 copy.18
Async XLA Ops:
  206.0 63.7 %copy-start = (bf16[128,2048]{1,0:T(8,128)(2,1)S(1)}, bf16[128,2048]{1,0:T(8,128)(2,1)}, u32[]{:S(2)}) copy-start(bf16[128,2048]{1,0:T(8,128)(2,1)} %get-tuple-element.88) | copy-start | bytes 1572868

commit v6 on v5

--- a/solution.py
+++ b/solution.py
@@ -401,8 +401,14 @@
         remote(dst, dst, self.send.at[n], self.recv.at[n], self.me.sibling()).wait_recv()
 
     def start(self):
+        self.start_far()
+        self.start_near()
+
+    def start_far(self):
         self.push(0, self.piece(2, 0), self.through.at[0], self.right)
         self.push(1, self.piece(2, 1), self.through.at[1], self.left)
+
+    def start_near(self):
         self.push(2, self.piece(1, 1), self.final.at[0], self.right)
         self.push(3, self.piece(3, 0), self.final.at[1], self.left)
 
@@ -630,11 +636,6 @@
     local[0].wait()
     tokens = Gather(me, None, None, *tg)
     tokens.start()
-    for k in order:
-        to = (me.sq + k) % SEQ
-        for p in range(3):
-            push(feed.at[:, feed_columns(p, to)], feedw.at[own_rows, pl.ds(p * FL, FL)],
-                 fs.at[p, k], fr.at[p, k], me.seq_peer(k))
     for copy in local[1:]:
         copy.wait()
 
@@ -676,6 +677,11 @@
         arrived(mixw.at[seq_rows(k)], ms.at[k], mr.at[k])
     mixes.start()
     tokens.forward()
+    for k in order:
+        to = (me.sq + k) % SEQ
+        for p in range(3):
+            push(feed.at[:, feed_columns(p, to)], feedw.at[own_rows, pl.ds(p * FL, FL)],
+                 fs.at[p, k], fr.at[p, k], me.seq_peer(k))
 
     lab_out[0:8] = jnp.full((8, 128), -1.0, f32)
     lab_out[G + 8 :] = jnp.full((8, 128), -2.0, f32)
@@ -685,8 +691,6 @@
 
     minors.turn()
     mixes.turn()
-    cots = Gather(me, None, cot_out, *cg)
-    cots.start()
     minors.far()
     mixes.far()
     tokens.across_left()
@@ -695,6 +699,8 @@
         minors.hand_on(t)
     mixes.hand_on(0)
     tokens.across_far()
+    cots = Gather(me, None, cot_out, *cg)
+    cots.start()
     minors.finish()
     for k in range(DP):
         gain_out[:, k * 128 : (k + 1) * 128] = minor[k * MINOR : k * MINOR + 16].astype(f32)[0:8]
@@ -712,7 +718,7 @@
             part[here] = norm_rows(tokg[here].astype(f32), gain_out[0:1]).astype(bf16)
             return c
 
-        lax.fori_loop(0, T // 16, body, 0)
+        lax.fori_loop(0, T // 16, body, 0, unroll=2)
         normed_copy(k, other).start()
 
     normalise(0, 0)
@@ -839,7 +845,7 @@
         n2g[rows_of(me.sq * T + i * 16, 16)] = norm_rows(middle[here], gain_out[1:2]).astype(bf16)
         return c
 
-    lax.fori_loop(0, T // 16, second_norm, 0)
+    lax.fori_loop(0, T // 16, second_norm, 0, unroll=2)
     seconds = Gather(me, None, n2_out, *ng)
     seconds.start()
     cots.finish()
@@ -988,7 +994,7 @@
         gathering[0][rows_of(mine + i * 16, 16)] = value.astype(bf16)
         return c + jnp.sum(terms, axis=0, keepdims=True)
 
-    gain_grad[...] = lax.fori_loop(0, T // 16, pull, jnp.zeros((1, D), f32))
+    gain_grad[...] = lax.fori_loop(0, T // 16, pull, jnp.zeros((1, D), f32), unroll=2)
     gather = Gather(me, None, adj_all, *gathering)
     gather.start()
     first[1].wait()
@@ -1157,8 +1163,7 @@
              (mixed_in, mixed), (extra_in, mg.at[:, :, :, pl.ds(MW, 128)]))
         )
     ]
-    for copy in loads:
-        copy.start()
+    loads[0].start()
     quarter, at = me.dp // 8, me.dp % 8
     gate_to = (8 * quarter + me.sq, at)
     gate_self = me.sq == at
@@ -1197,6 +1202,8 @@
     inner = Scatter(me, part, *one)
     loads[0].wait()
     inner.start()
+    for copy in loads[1:]:
+        copy.start()
     loads[1].wait()
     feed_up.start()
     feed_low.start()
@@ -1205,24 +1212,32 @@
         copy.wait()
 
     def tile(i, carry):
-        here = pl.ds(pl.multiple_of(i * 256, 256), 256)
+        tx, ty = (me.x + 2 + i) % 4, ((me.y + 2) // 2 + i // 4) % 2
+        here = pl.ds(pl.multiple_of((tx * 2 + ty) * 256, 256), 256)
         left = tn(normed[:, here], both[...]).astype(bf16)
         right = tn(adj_out[:, here], mixed[...]).astype(bf16)
         for h in range(2):
-            mg[i // 2, i % 2 * 2 + h, :, : 2 * WP] = left[h * T : (h + 1) * T]
-            mg[i // 2, i % 2 * 2 + h, :, 2 * WP : MW] = right[h * T : (h + 1) * T]
-
-        @pl.when(i == 4)
+            mg[tx, ty * 2 + h, :, : 2 * WP] = left[h * T : (h + 1) * T]
+            mg[tx, ty * 2 + h, :, 2 * WP : MW] = right[h * T : (h + 1) * T]
+
+        @pl.when(i == 3)
         def _():
+            mix_up.start_far()
             inner.relay()
             feed_up.relay()
             feed_low.relay()
 
+        @pl.when(i == 4)
+        def _():
+            mix_low.start_far()
+
         return carry
 
     lax.fori_loop(0, 8, tile, 0)
-    mix_up.start()
-    mix_low.start()
+    mix_up.start_near()
+    mix_low.start_near()
+    mix_up.relay()
+    mix_low.relay()
     inner.finish(adj)
 
     def pull(i, carry):
@@ -1231,7 +1246,7 @@
         in_grad[here] = adj_middle[here] + pulled
         return carry + jnp.sum(terms, axis=0, keepdims=True)
 
-    gain_one = lax.fori_loop(0, T // 16, pull, jnp.zeros((1, D), f32))
+    gain_one = lax.fori_loop(0, T // 16, pull, jnp.zeros((1, D), f32), unroll=2)
     gp[...] = jnp.zeros(gp.shape, f32)
     for k in range(DP):
         gp[k, 0:1] = gain_one[:, k * 128 : (k + 1) * 128]
@@ -1261,29 +1276,20 @@
             push(lastf.at[0, rows_of(to * 16, 16), pl.ds(p * FL, FL)], feed_out.at[:, feed_columns(p, me.sq)],
                  f3s.at[p, k], f3r.at[p, k], me.seq_peer(k))
 
-    mix_up.relay()
-    mix_low.relay()
-
-    for k in range(1, DP):
-        arrived(gp_in.at[k], gs.at[k], gr.at[k])
-
-    def sum_gains(k, total):
-        return total + gp_in[k]
-
-    gain_sum[...] = lax.fori_loop(1, DP, sum_gains, gp[me.dp])
-    for k in range(1, SEQ):
-        push(gain_sum, gain_in.at[k], qs.at[k], qr.at[k], me.seq_peer(k))
-
     mix_up.finish(lambda q: s1.at[0, :, pl.ds(q * 32, 32)])
     last_up.start()
     mix_low.finish(lambda q: s1.at[1, :, pl.ds(q * 32, 32)])
     last_low.start()
+    for k in range(1, DP):
+        arrived(gp_in.at[k], gs.at[k], gr.at[k])
+
+    def sum_gains(k, total):
+        return total + gp_in[k]
+
+    gain_sum[...] = lax.fori_loop(1, DP, sum_gains, gp[me.dp])
     for k in range(1, SEQ):
-        arrived(gain_in.at[k], qs.at[k], qr.at[k])
-    total = gain_sum[...]
-    for k in range(1, SEQ):
-        total = total + gain_in[k]
-    gain_out[...] = total
+        push(gain_sum, gain_in.at[k], qs.at[k], qr.at[k], me.seq_peer(k))
+
     last_up.relay()
     last_low.relay()
     last_up.finish(lambda q: last.at[:, pl.ds(q * 32, 32)])
@@ -1317,6 +1323,12 @@
     def _():
         chan_local.start()
 
+    for k in range(1, SEQ):
+        arrived(gain_in.at[k], qs.at[k], qr.at[k])
+    total = gain_sum[...]
+    for k in range(1, SEQ):
+        total = total + gain_in[k]
+    gain_out[...] = total
     for k in range(1, SEQ):
         source = (me.sq - k + SEQ) % SEQ
         for p in range(3):
@@ -1375,8 +1387,16 @@
     )(part, normed, both, adj_out, mixed, extra, s1, tok, adj_middle, gains, gain_two)
 
 
-def finish_kernel(mix, feed, gate, chan, gain, mix_out, feed_out, gate_out, chan_out, gain_out):
+def finish_kernel(in_grad, act, mix, feed, gate, chan, gain, in_out, act_out, mix_out, feed_out, gate_out, chan_out, gain_out):
     me = Place()
+
+    def keep(i, c):
+        here = pl.ds(pl.multiple_of(i * 16, 16), 16)
+        in_out[here] = in_grad[here]
+        act_out[here] = act[here]
+        return c
+
+    lax.fori_loop(0, T // 16, keep, 0)
     for p in range(3):
         for j in range(SEQ):
             value = mix[j, :, p * WP : (p + 1) * WP].astype(f32)
@@ -1397,20 +1417,20 @@
     gain_out[...] = pltpu.roll(gain[...], (128 - me.sq * 16) % 128, 1)[0:2, 0:16]
 
 
-def finish_call(mix, feed, gate, chan, gain):
+def finish_call(in_grad, act, mix, feed, gate, chan, gain):
     sds = jax.ShapeDtypeStruct
     vmem = pl.BlockSpec(memory_space=VMEM)
     return pl.pallas_call(
         finish_kernel,
         out_shape=(
-            sds((16, 3 * W), f32), sds((16, 3 * FF), f32),
+            sds((T, D), f32), sds((T, D), bf16), sds((16, 3 * W), f32), sds((16, 3 * FF), f32),
             sds((40, BW), f32), sds((8, 20), f32), sds((2, 16), f32),
         ),
-        in_specs=[vmem] * 5,
-        out_specs=[vmem] * 5,
+        in_specs=[vmem] * 7,
+        out_specs=[vmem] * 7,
         compiler_params=pltpu.CompilerParams(vmem_limit_bytes=62 << 20),
         name="finish",
-    )(mix, feed, gate, chan, gain)
+    )(in_grad, act, mix, feed, gate, chan, gain)
 
 
 def shards(tokens, segments, mixer_weights, norm_gains, gate_weights, channel_terms, feed_weights, cotangent):
@@ -1426,8 +1446,8 @@
     input_gradient, mix_out, feed_out, gate_out, chan_out, gain_out = close_call(
         in_part, normed, both, adj_all, mixed, extra.reshape(4, 4, 128, 128), s1, tokens, adj_middle, gains, gain_two
     )
-    mixer_gradient, feed_gradient, gate_gradient, channel_gradient, gain_gradient = finish_call(
-        mix_out, feed_out, gate_out, chan_out, gain_out
+    input_gradient, activations, mixer_gradient, feed_gradient, gate_gradient, channel_gradient, gain_gradient = (
+        finish_call(input_gradient, activations, mix_out, feed_out, gate_out, chan_out, gain_out)
     )
     return (
         activations, input_gradient, mixer_gradient, gain_gradient.T, gate_gradient, channel_gradient.T, feed_gradient

time: 273 us -> 268 us (0.982)
  local copies, waits for them, and re-layouts: 3.09 us -> 0 us
    unnamed x4 -> x0, local copies, waits for them, and re-layouts: 3.09 us -> none
where the time goes in v6:
time: 268 us
  Pallas kernels  267 us (100%)
    pallas_call x1, Pallas kernels, forward_call(): pl.pallas_call(forward_kernel, out_shape=(sds((G, D), bf16), sds((D, MW),...  130 us
    pallas_call x1, Pallas kernels, turn_call(): pl.pallas_call(turn_kernel, out_shape=(sds((G, D), bf16), sds((2, 4, HALF...  74.4 us
    pallas_call x1, Pallas kernels, close_call(): pl.pallas_call(close_kernel, out_shape=(sds((T, D), f32), sds((SEQ, 16, M...  59.3 us

profile of v6, /device:TPU:1, one launch (start us, length us, event | category | flops | bytes accessed | tf_op | source)
XLA Modules:
  0.0 267.6 jit_solution(677333799658934436)
XLA Ops:
  0.6 129.7 %forward.1 = (bf16[1024,2048]{1,0:T(8,128)(2,1)}, bf16[2048,1152]{1,0:T(8,128)(2,1)}, bf16[1024,2048]{1,0:T(8,128)(2,1)}, f32[1024,384]{1,0:T(8,128)}, f32[1024,...) custom-call(bf16[128,2048]{1,0:T(8,128)(2,1)} %tok.3, ...), custom_call_target="tpu_custom_call" | custom-call | flops 24159191040 | bytes 104857600 | tf_op jit(solution)/shard_map/forward/pallas_call | solution.py:902
  130.3 74.4 %turn.1 = (bf16[1024,2048]{1,0:T(8,128)(2,1)}, bf16[2,4,64,2304]{3,2,1,0:T(8,128)(2,1)}, bf16[1024,768]{1,0:T(8,128)(2,1)}, bf16[1024,2048]{1,0:T(8,128)(2,1)}, ...) custom-call(bf16[1024,2048]{1,0:T(8,128)(2,1)} %get-tuple-element.46.back_in, ...), custom_call_target="tpu_custom_call" | custom-call | flops 24159191040 | bytes 104857600 | tf_op jit(solution)/shard_map/turn/pallas_call | solution.py:1129
  204.7 59.3 %close.1 = (f32[128,2048]{1,0:T(8,128)}, bf16[8,16,1152]{2,1,0:T(8,128)(2,1)}, bf16[16,18432]{1,0:T(8,128)(2,1)}, bf16[96,128]{1,0:T(8,128)(2,1)}, bf16[32,128]{1,0:T(8,128)(2,1)}, /*index=5*/f32[8,128]{1,0:T(8,128)}) custom-call(bf16[1024,2048]{1,0:T(8,128)(2,1)} %get-tuple-element.62.part_in, bf16[1024,2048]{1,0:T(8,128)(2,1)} %get-tuple-element.63.normed_in, ...), custom_call_target="tpu_custom_call" | custom-call | flops 4026531840 | bytes 104857600 | tf_op jit(solution)/shard_map/close/pallas_call | solution.py:1364
  264.0 3.7 %finish.1 = (f32[128,2048]{1,0:T(8,128)}, bf16[128,2048]{1,0:T(8,128)(2,1)}, f32[16,7680]{1,0:T(8,128)}, f32[16,18432]{1,0:T(8,128)}, f32[40,160]{1,0:T(8,128)}, /*index=5*/f32[8,20]{1,0:T(8,128)}, f32[2,16]{1,0:T(2,128)}) custom-call(f32[128,2048]{1,0:T(8,128)} %get-tuple-element.71.in_grad, bf16[128,2048]{1,0:T(8,128)(2,1)} %get-tuple-element.72.act, ...), custom_call_target="tpu_custom_call" | custom-call | tf_op jit(solution)/shard_map/finish/pallas_call | solution.py:1423
